TPU v7x, 32 devices: a whole 2x2x4 slice. The times are simulated.
32 devices in a mesh: groups: 2 (over y), expert: 8 (over z, x), dp: 2 (over core).
Axes of the slice: x: 2, y: 2, z: 4, core: 2. Of those that a mesh axis runs over, the one named last changes fastest.
Arguments:
- out_grad: bfloat16 [4096, 3584], P(('groups', 'expert', 'dp')), parts along dimension 0, may hold values from -6 to 6
- hidden: bfloat16 [4096, 8, 1024], P(('groups', 'expert', 'dp')), parts along dimension 0, may hold values from -0.29882812 to 0.29882812
- routes: int32 [4096, 8], P(('groups', 'expert', 'dp')), parts along dimension 0, may hold values from 0 to 255, as said below
- gates: float32 [4096, 8], P(('groups', 'expert', 'dp')), parts along dimension 0, may hold values from 0.02 to 1
- w_down: bfloat16 [8, 1024, 3584], P('expert', 'dp'), may hold values from -0.1875 to 0.1875
Outputs:
- grad_down: bfloat16 [16, 1024, 3584], P(('groups', 'expert'), 'dp'), parts along dimension 0
- grad_hidden: bfloat16 [4096, 8, 1024], P(('groups', 'expert', 'dp')), parts along dimension 0
- grad_gates: float32 [4096, 8], P(('groups', 'expert', 'dp')), parts along dimension 0
There are 2 independent parts, one for each index of `groups`. A program takes and returns all parts, laid end to end along the dimension named above; an argument that names none is the same for every part. Nothing has to cross between parts.
Inputs may be any that keep to these rules, and one draw needn't show every extreme that they name: `routes`: each row names 8 different ids; ids below 8 are the window's experts. Among the 128 rows of one device (aligned blocks in order), each window expert is named by at most 12 rows, and in every block one same expert is named by exactly 12 rows.
All inputs are finite; a program needn't handle non-finite values.
Results may differ from a plain program's by a relative error of at most 0.005.
Values may be sent and summed in bfloat16 or wider, within the bound.
No kernel may reach another device: no remote copies, remote signals or barrier semaphores. Data moves between devices by JAX's collectives and lax.ppermute only.
A program may use at most 128 MiB of HBM per device.

v0:
```python
import jax
import jax.numpy as jnp
from jax import lax
from jax.sharding import PartitionSpec as P

MOST = 12


def route_slots(routes, peers, depth):
    flat_routes = routes.reshape(-1)
    inside = flat_routes < peers
    columns = jnp.arange(peers, dtype=jnp.int32)
    member = jnp.where(inside[:, None] & (flat_routes[:, None] == columns[None, :]), 1, 0).astype(
        jnp.int32
    )
    before = jnp.cumsum(member, axis=0) - member
    position = jnp.sum(before * member, axis=1)
    return jnp.where(inside, flat_routes * depth + position, peers * depth)


def local(out_grad, hidden, routes, gates, w_down):
    tokens_here, top_count = routes.shape
    units = hidden.shape[2]
    width = out_grad.shape[1]
    peers = lax.axis_size("expert")
    depth = MOST
    slots = peers * depth
    routed = tokens_here * top_count
    target = route_slots(routes, peers, depth)
    source = (
        jnp.full((slots + 1,), routed, jnp.int32)
        .at[target]
        .set(jnp.arange(routed, dtype=jnp.int32))[:slots]
    )
    flat_gates = gates.reshape(routed, 1)
    flat_hidden = hidden.reshape(routed, units)
    scaled = (flat_gates * flat_hidden.astype(jnp.float32)).astype(jnp.bfloat16)
    scaled_pad = jnp.concatenate([scaled, jnp.zeros((1, units), jnp.bfloat16)], 0)
    grad_pad = jnp.concatenate([out_grad, jnp.zeros((1, width), jnp.bfloat16)], 0)
    owner = jnp.where(source < routed, source // top_count, tokens_here)
    send_grad = grad_pad[owner].reshape(peers, depth, width)
    send_scaled = scaled_pad[source].reshape(peers, depth, units)
    recv_grad, recv_scaled = (
        lax.all_to_all(send_grad, "expert", split_axis=0, concat_axis=0, tiled=True),
        lax.all_to_all(send_scaled, "expert", split_axis=0, concat_axis=0, tiled=True),
    )
    recv_grad = recv_grad.reshape(slots, width)
    recv_scaled = recv_scaled.reshape(slots, units)
    unit_grad = lax.dot_general(
        recv_grad,
        lax.all_gather(w_down, "dp", axis=1, tiled=True)[0],
        (((1,), (1,)), ((), ())),
        preferred_element_type=jnp.float32,
    ).astype(jnp.bfloat16)
    weight_grad = lax.psum_scatter(
        lax.dot_general(
            recv_scaled, recv_grad, (((0,), (0,)), ((), ())), preferred_element_type=jnp.float32
        ),
        "dp",
        scatter_dimension=0,
        tiled=True,
    )
    back = lax.all_to_all(
        unit_grad.reshape(peers, depth, units), "expert", split_axis=0, concat_axis=0, tiled=True
    ).reshape(slots, units)
    back_pad = jnp.concatenate([back, jnp.zeros((1, units), jnp.bfloat16)], 0)
    route_grad = back_pad[target].astype(jnp.float32)
    grad_hidden = (
        (flat_gates * route_grad).astype(jnp.bfloat16).reshape(tokens_here, top_count, units)
    )
    grad_gates = jnp.sum(flat_hidden.astype(jnp.float32) * route_grad, axis=1).reshape(
        tokens_here, top_count
    )
    return (weight_grad.astype(jnp.bfloat16)[None], grad_hidden, grad_gates)


def solution(mesh):
    in_specs = (
        P(("groups", "expert", "dp"), None),
        P(("groups", "expert", "dp"), None, None),
        P(("groups", "expert", "dp"), None),
        P(("groups", "expert", "dp"), None),
        P("expert", "dp", None),
    )
    out_specs = (
        P(("groups", "expert"), "dp", None),
        P(("groups", "expert", "dp"), None, None),
        P(("groups", "expert", "dp"), None),
    )
    return jax.shard_map(local, mesh=mesh, in_specs=in_specs, out_specs=out_specs, check_vma=False)
```

profile of v0, /device:TPU:0, one launch (start us, length us, event | category | flops | bytes accessed | tf_op | source)
XLA Modules:
  0.0 113.2 jit_solution(8246313864086698935)
XLA Ops:
  7.2 0.0 copy-start.1
  7.2 0.0 copy-start.2
  7.2 0.0 copy-start
  7.2 0.0 all-gather.2.cloned.1.call-start
  7.2 0.7 all-gather.2.cloned.1.call-update
  7.9 0.0 copy-done.1
  7.9 0.1 copy.18
  8.0 0.1 reshape.115
  8.1 0.1 reshape.117
  8.3 2.3 %reduce-window.6 = s32[8,8,128]{2,1,0:T(8,128)S(1)} reduce-window(s32[8,8,128]{2,1,0:T(8,128)S(1)} %fusion.11, s32[]{:T(128)} %constant.20.clone.1), window={size=1x1x128 pad=0_0x0_0x127_0}, to_apply=%region_0.1 | reduce-window | flops 1040384 | bytes 65540 | tf_op jit(solution)/shard_map/reduce-window
  10.5 0.3 slice_reduce_fusion
  10.8 0.2 reduce-window.9
  11.0 0.1 copy.17
  11.1 0.1 mul.47
  11.2 0.1 copy.16
  11.3 0.1 lt.53
  11.4 0.0 copy-done.2
  11.4 0.1 copy.15
  11.5 0.1 mul.42
  11.6 0.0 copy-done
  11.6 0.4 fusion.3
  12.1 1.5 %concatenate.9 = bf16[1025,1024]{1,0:T(8,128)(2,1)} pad(bf16[1024,1024]{1,0:T(8,128)(2,1)S(1)} %fusion.3, bf16[]{:T(256)} %constant.15.clone.1), padding=0_1x0_0 | pad | bytes 4196354 | tf_op jit(solution)/shard_map/concatenate | solution.py:38
  13.6 0.1 add_bitcast_fusion
  13.7 4.3 %scatter_custom_fusion = s32[97]{0:T(128)S(1)} fusion(s32[1024]{0:T(1024)S(1)} %bitcast.36, s32[1024]{0:T(1024)S(1)} %iota.11, s32[]{:T(128)} %constant.16.clone.1), kind=kCustom, calls=%fused_computation.41 | custom fusion | bytes 392 | tf_op jit(solution)/shard_map/scatter | solution.py:33
  18.0 3.1 %gather_fusion = bf16[96,1024]{1,0:T(8,128)(2,1)S(1)} fusion(bf16[1025,1024]{1,0:T(8,128)(2,1)} %concatenate.9, s32[1024]{0:T(1024)S(1)} %get-tuple-element.11), kind=kCustom, calls=%fused_computation | custom fusion | bytes 393600 | tf_op jit(solution)/shard_map/gather | solution.py:42
  21.2 0.7 reshape.118
  21.9 7.3 %all-to-all-start = ((bf16[8,12,1024]{2,1,0:T(8,128)(2,1)}), bf16[8,12,1024]{2,1,0:T(8,128)(2,1)S(1)}, u32[]{:S(2)}, u32[]{:S(2)}) async-start(bf16[8,12,1024]{2,1,0:T(8,128)(2,1)} %reshape.118), calls=%async_computation | async-start | bytes 524288 | tf_op jit(solution)/shard_map/all_to_all | solution.py:45
  29.2 0.0 reduce-scatter.2.cloned.1.call-start
  29.2 1.2 %concatenate.10 = bf16[129,3584]{1,0:T(8,128)(2,1)S(1)} pad(bf16[128,3584]{1,0:T(8,128)(2,1)} %param.5, bf16[]{:T(256)} %constant.15.clone.1), padding=0_1x0_0 | pad | bytes 1842178 | tf_op jit(solution)/shard_map/concatenate | solution.py:39
  30.5 1.8 %gather_fusion.1 = bf16[96,3584]{1,0:T(8,128)(2,1)} fusion(bf16[129,3584]{1,0:T(8,128)(2,1)S(1)} %concatenate.10, s32[1024]{0:T(1024)S(1)} %get-tuple-element.10), kind=kCustom, calls=%fused_computation.1 | custom fusion | bytes 1376640 | tf_op jit(solution)/shard_map/gather | solution.py:41
  32.3 2.1 %reshape.119 = bf16[8,12,3584]{2,1,0:T(8,128)(2,1)} reshape(bf16[96,3584]{1,0:T(8,128)(2,1)} %gather_fusion.1) | data formatting | bytes 1376256 | tf_op jit(solution)/shard_map/reshape | solution.py:41
  34.4 3.7 %all-to-all-done = bf16[8,12,1024]{2,1,0:T(8,128)(2,1)S(1)} async-done(((bf16[8,12,1024]{2,1,0:T(8,128)(2,1)}), bf16[8,12,1024]{2,1,0:T(8,128)(2,1)S(1)}, u32[]{:S(2)}, u32[]{:S(2)}) %all-to-all-start) | async-done | bytes 196640 | tf_op jit(solution)/shard_map/all_to_all | solution.py:45
  38.1 26.6 %all_to_all.15 = bf16[8,12,3584]{2,1,0:T(8,128)(2,1)S(1)} all-to-all(bf16[8,12,3584]{2,1,0:T(8,128)(2,1)} %reshape.119), channel_id=1, replica_groups=mesh['groups'=2,'expert'=8,'dp'=2] {'expert'}, dimensions={0} | all-to-all | bytes 1376256 | tf_op jit(solution)/shard_map/all_to_all | solution.py:44
  64.6 7.3 %convolution_bitcast_fusion = f32[1024,3584]{1,0:T(8,128)} fusion(bf16[8,12,1024]{2,1,0:T(8,128)(2,1)S(1)} %all-to-all-done, bf16[8,12,3584]{2,1,0:T(8,128)(2,1)S(1)} %all_to_all.15), kind=kOutput, calls=%fused_computation.4 | convolution fusion | flops 704643072 | bytes 15564800 | tf_op jit(solution)/shard_map/dot_general | solution.py:56
  71.9 0.0 reduce-scatter.2.cloned.1.call-update
  72.0 1.0 reshape.120
  73.0 0.0 all-gather.2.cloned.1.call-done
  73.0 5.6 %fusion.6 = bf16[96,1024]{1,0:T(8,128)(2,1)S(1)} fusion(bf16[96,3584]{1,0:T(8,128)(2,1)} %reshape.120, bf16[1,1024,3584]{2,1,0:T(8,128)(2,1)} %all-gather.2.cloned.1.call-done), kind=kOutput, calls=%fused_computation.15 | convolution fusion | flops 704741376 | bytes 8224768 | tf_op jit(solution)/shard_map/dot_general | solution.py:49
  78.6 0.7 reshape.121
  79.4 3.4 %all-to-all-start.2 = ((bf16[8,12,1024]{2,1,0:T(8,128)(2,1)}), bf16[8,12,1024]{2,1,0:T(8,128)(2,1)S(1)}, u32[]{:S(2)}, u32[]{:S(2)}) async-start(bf16[8,12,1024]{2,1,0:T(8,128)(2,1)} %reshape.121), calls=%async_computation.3 | async-start | bytes 524288 | tf_op jit(solution)/shard_map/all_to_all | solution.py:63
  82.8 8.4 %all-to-all-done.2 = bf16[8,12,1024]{2,1,0:T(8,128)(2,1)S(1)} async-done(((bf16[8,12,1024]{2,1,0:T(8,128)(2,1)}), bf16[8,12,1024]{2,1,0:T(8,128)(2,1)S(1)}, u32[]{:S(2)}, u32[]{:S(2)}) %all-to-all-start.2) | async-done | bytes 196640 | tf_op jit(solution)/shard_map/all_to_all | solution.py:63
  91.3 5.3 %gather_fusion.2 = bf16[1024,1024]{1,0:T(8,128)(2,1)} fusion(bf16[97,1024]{1,0:T(8,128)(2,1)S(1)} %concatenate.11, s32[1024]{0:T(1024)S(1)} %broadcast_clamp_fusion), kind=kCustom, calls=%fused_computation.2 | custom fusion | bytes 4198400 | tf_op jit(solution)/shard_map/gather | solution.py:67
  96.6 3.8 %fusion.5 = (f32[128,8]{1,0:T(8,128)S(1)}, bf16[128,8,1024]{2,1,0:T(8,128)(2,1)}) fusion(bf16[128,8,1024]{2,1,0:T(8,128)(2,1)S(1)} %copy-done, bf16[1024,1024]{1,0:T(8,128)(2,1)} %gather_fusion.2, f32[128,8]{1,0:T(8,128)S(1)} %copy.15), kind=kLoop, calls=%fused_computation.13 | loop fusion | flops 6290432 | bytes 6299648 | tf_op jit(solution)/shard_map/reduce_sum | solution.py:71
  100.4 0.7 copy.21
  101.0 0.0 reduce-scatter.2.cloned.1.call-done
  101.0 5.3 %convert_bitcast_fusion.1 = bf16[1,512,3584]{2,1,0:T(8,128)(2,1)} fusion(f32[512,3584]{1,0:T(8,128)} %reduce-scatter.2.cloned.1.call-done), kind=kLoop, calls=%fused_computation.14 | loop fusion | flops 1835008 | bytes 11010048 | tf_op jit(solution)/shard_map/broadcast_in_dim | solution.py:74
  (13 shorter events, 0.2 us)
Async XLA Ops:
  7.2 0.8 copy-start.1
  7.2 4.3 %copy-start.2 = (f32[128,8]{0,1:T(8,128)S(1)}, f32[128,8]{0,1:T(8,128)}, u32[]{:S(2)}) copy-start(f32[128,8]{0,1:T(8,128)} %param.8) | copy-start | bytes 12292
  7.2 4.5 %copy-start = (bf16[128,8,1024]{2,1,0:T(8,128)(2,1)S(1)}, bf16[128,8,1024]{2,1,0:T(8,128)(2,1)}, u32[]{:S(2)}) copy-start(bf16[128,8,1024]{2,1,0:T(8,128)(2,1)} %param.6) | copy-start | bytes 6291460
  7.2 65.8 %all-gather.2.cloned.1.call-start = ((), (), s32[]{:S(2)}) async-start(), calls=%async_computation.5 | async-start | bytes 11010048 | tf_op jit(solution)/shard_map/all_gather | solution.py:51
  21.9 16.2 %all-to-all-start = ((bf16[8,12,1024]{2,1,0:T(8,128)(2,1)}), bf16[8,12,1024]{2,1,0:T(8,128)(2,1)S(1)}, u32[]{:S(2)}, u32[]{:S(2)}) async-start(bf16[8,12,1024]{2,1,0:T(8,128)(2,1)} %reshape.118), calls=%async_computation | async-start | bytes 524288 | tf_op jit(solution)/shard_map/all_to_all | solution.py:45
  29.2 71.9 %reduce-scatter.2.cloned.1.call-start = ((), (), s32[]{:S(2)}) async-start(), calls=%async_computation.4 | async-start | bytes 22020096 | tf_op jit(solution)/shard_map/reduce_scatter | solution.py:55
  79.4 11.8 %all-to-all-start.2 = ((bf16[8,12,1024]{2,1,0:T(8,128)(2,1)}), bf16[8,12,1024]{2,1,0:T(8,128)(2,1)S(1)}, u32[]{:S(2)}, u32[]{:S(2)}) async-start(bf16[8,12,1024]{2,1,0:T(8,128)(2,1)} %reshape.121), calls=%async_computation.3 | async-start | bytes 524288 | tf_op jit(solution)/shard_map/all_to_all | solution.py:63
Sparse Core Ops, SparseCore 0:
  9.6 21.0 all-gather.1
  72.1 22.6 reduce-scatter.1
where the time goes:
time: 114 us; the launch traced here: 113 us
  blocking collectives  26.6 us (23%)
  local copies, waits for them, and re-layouts  23.8 us (21%)
  between operations  14.2 us (12%)
  matrix products  13 us (11%)
  waiting for transfers between devices  12.8 us (11%)
  other arithmetic  12.1 us (11%)
  starting transfers between devices  10.8 us (9%)
    all_to_all x1, blocking collectives, local(): lax.all_to_all(send_grad, 'expert', split_axis=0, concat_axis=0, tiled=True)  26.6 us
    all_to_all x1, waiting for transfers between devices, local(): lax.all_to_all(unit_grad.reshape(peers, depth, units), 'expert', split_ax...  8.35 us
    dot_general x1, matrix products, local(): lax.dot_general(recv_scaled, recv_grad, (((0,), (0,)), ((), ())), preferr...  7.31 us
    all_to_all x1, starting transfers between devices, local(): lax.all_to_all(send_scaled, 'expert', split_axis=0, concat_axis=0, tiled=...  7.27 us
    dot_general x1, matrix products, local(): lax.dot_general(recv_grad, lax.all_gather(w_down, 'dp', axis=1, tiled=Tru...  5.64 us
    gather x1, local copies, waits for them, and re-layouts, local(): route_grad = back_pad[target].astype(jnp.float32)  5.34 us
    broadcast_in_dim x1, other arithmetic, local(): return (weight_grad.astype(jnp.bfloat16)[None], grad_hidden, grad_gates)  5.31 us
    scatter x1, local copies, waits for them, and re-layouts, local(): source = jnp.full((slots + 1,), routed, jnp.int32).at[target].set(jnp.ara...  4.3 us
  transfers between devices with their start and end apart: 4, of which 2 were waited for; matrix products, arithmetic and copies ran while one was open for 38% of the time, Pallas kernels for 0%

commit v1 on v0

v1 whole, which is shorter than its diff:
```python
import functools

import jax
import jax.numpy as jnp
from jax import lax
from jax.experimental import pallas as pl
from jax.experimental.pallas import tpu as pltpu
from jax.sharding import PartitionSpec as P

MOST = 12
ROWS = 16
COLS = 3
EXTRA = ROWS - MOST
BF = jnp.bfloat16
F32 = jnp.float32
MIB = 1 << 20


def params(mib=48, **kw):
    return pltpu.CompilerParams(vmem_limit_bytes=mib * MIB, **kw)


def vmem():
    return pl.BlockSpec(memory_space=pltpu.VMEM)


def partner(index, step, peers):
    if peers & (peers - 1) == 0:
        return index ^ step
    return lax.rem(index + step, peers) if isinstance(index, jax.Array) else (index + step) % peers


def routing(routes_t, peers):
    me = lax.axis_index("expert")
    tokens = routes_t.shape[1]
    hits = [routes_t == partner(me, step, peers) for step in range(peers)]
    member = jnp.concatenate(
        [jnp.max(hit.astype(F32), axis=0, keepdims=True) for hit in hits], axis=0
    )
    earlier = lax.broadcasted_iota(jnp.int32, (tokens, tokens), 0) < lax.broadcasted_iota(
        jnp.int32, (tokens, tokens), 1
    )
    before = jnp.dot(member.astype(BF), earlier.astype(F32).astype(BF), preferred_element_type=F32)
    return hits, jnp.where(member > 0, before, -1.0)


def picks(place, peers, block):
    tokens = place.shape[1]
    row = lax.broadcasted_iota(jnp.int32, (ROWS, tokens), 0)
    wanted = jnp.where(row < MOST, row, row - MOST + EXTRA * block).astype(F32)
    return jnp.concatenate(
        [(place[step : step + 1, :] == wanted).astype(F32) for step in range(peers)], axis=0
    )


def low_rows(rows, width):
    return lax.broadcasted_iota(jnp.int32, (rows, width), 0) % ROWS < MOST


def pack_grad(peers, routes_ref, grad_ref, *out_refs):
    _, place = routing(routes_ref[...], peers)
    quarter = grad_ref.shape[1] // 4
    tokens = grad_ref.shape[0]
    low = low_rows(peers * ROWS, tokens)
    last = grad_ref[:, COLS * quarter :]
    for block in range(COLS):
        pick = picks(place, peers, block)
        both = jnp.concatenate(
            [jnp.where(low, pick, 0.0).astype(BF), jnp.where(low, 0.0, pick).astype(BF)], axis=1
        )
        columns = slice(block * quarter, (block + 1) * quarter)
        source = jnp.concatenate([grad_ref[:, columns], last], axis=0)
        packed = jnp.dot(both, source, preferred_element_type=F32).astype(BF)
        for step in range(peers):
            out_refs[step][:, columns] = packed[step * ROWS : (step + 1) * ROWS, :]


def gate_of(hits, gates_t):
    return jnp.concatenate(
        [jnp.sum(jnp.where(hit, gates_t, 0.0), axis=0, keepdims=True) for hit in hits], axis=0
    )


def choice_of(hits):
    return jnp.concatenate(
        [
            jnp.sum(
                jnp.where(hit, lax.broadcasted_iota(jnp.int32, hit.shape, 0).astype(F32), 0.0),
                axis=0,
                keepdims=True,
            )
            for hit in hits
        ],
        axis=0,
    )


def spread(table, pick, peers):
    return jnp.concatenate(
        [
            jnp.sum(
                pick[step * ROWS : (step + 1) * ROWS, :] * table[step : step + 1, :],
                axis=1,
                keepdims=True,
            )
            for step in range(peers)
        ],
        axis=0,
    )


def route_picks(pick, choice, top_count):
    tokens = pick.shape[1]
    routed = tokens * top_count
    token = lax.broadcasted_iota(jnp.int32, (tokens, routed), 0)
    column = lax.broadcasted_iota(jnp.int32, (tokens, routed), 1)
    wide = (column // top_count == token).astype(F32).astype(BF)
    mine = jnp.dot(pick.astype(BF), wide, preferred_element_type=F32)
    which = (
        lax.broadcasted_iota(jnp.int32, (pick.shape[0], routed), 1) % top_count
    ).astype(F32)
    return jnp.where(which == choice, mine, 0.0)


def pack_hidden(peers, routes_ref, gates_ref, hidden_ref, raw_ref, *out_refs):
    hits, place = routing(routes_ref[...], peers)
    gate = gate_of(hits, gates_ref[...])
    choice = choice_of(hits)
    quarter = hidden_ref.shape[1] // 4
    low = low_rows(peers * ROWS, quarter)
    last = hidden_ref[:, COLS * quarter :]
    for block in range(COLS):
        pick = picks(place, peers, block)
        take = route_picks(pick, spread(choice, pick, peers), routes_ref.shape[0]).astype(BF)
        columns = slice(block * quarter, (block + 1) * quarter)
        first = jnp.dot(take, hidden_ref[:, columns], preferred_element_type=F32)
        rest = jnp.dot(take, last, preferred_element_type=F32)
        raw = jnp.where(low, first, rest)
        raw_ref[:, columns] = raw.astype(BF)
        scaled = (spread(gate, pick, peers) * raw).astype(BF)
        for step in range(peers):
            out_refs[step][:, columns] = scaled[step * ROWS : (step + 1) * ROWS, :]


def last_quarter(peers, block):
    rows = peers * ROWS
    to = lax.broadcasted_iota(jnp.int32, (rows, rows), 0)
    at = lax.broadcasted_iota(jnp.int32, (rows, rows), 1)
    inside = at % ROWS
    wanted = at - inside + inside - MOST + EXTRA * block
    return ((inside >= MOST) & (to == wanted)).astype(F32).astype(BF)


def stack(refs, columns):
    return jnp.concatenate([ref[:, columns] for ref in refs], axis=0)


def unpack_last(peers, parts):
    moves = jnp.concatenate([last_quarter(peers, block) for block in range(COLS)], axis=1)
    return jnp.dot(moves, jnp.concatenate(parts, axis=0), preferred_element_type=F32).astype(BF)


def unit_grads(peers, tiles, *refs):
    in_refs, own_ref, other_ref = refs[:peers], refs[peers], refs[peers + 1]
    all_ref, out_refs, quarters_ref = refs[peers + 2], refs[peers + 3 : -1], refs[-1]
    tile = pl.program_id(0)
    quarter = all_ref.shape[1] // 4

    @pl.when(tile == 0)
    def _():
        parts = []
        for block in range(COLS):
            columns = slice(block * quarter, (block + 1) * quarter)
            part = stack(in_refs, columns)
            all_ref[:, columns] = part
            parts.append(part)
        all_ref[:, COLS * quarter :] = unpack_last(peers, parts)

    where = lax.rem(tile + lax.axis_index("dp") * (tiles // 2), tiles)

    def one(weight):
        quarters_ref[where] = lax.dot_general(
            all_ref[...], weight, (((1,), (1,)), ((), ())), preferred_element_type=F32
        ).astype(BF)

    @pl.when(tile < tiles // 2)
    def _():
        one(own_ref[0])

    @pl.when(tile >= tiles // 2)
    def _():
        one(other_ref[0])

    @pl.when(tile == tiles - 1)
    def _():
        width = quarters_ref.shape[2]
        low = low_rows(peers * ROWS, width)
        last = quarters_ref[COLS]
        for block in range(COLS):
            moved = lax.dot_general(
                last_quarter(peers, block),
                last,
                (((0,), (0,)), ((), ())),
                preferred_element_type=F32,
            )
            packed = jnp.where(low, quarters_ref[block].astype(F32), moved).astype(BF)
            for step in range(peers):
                out_refs[step][:, block * width : (block + 1) * width] = packed[
                    step * ROWS : (step + 1) * ROWS, :
                ]


def split_hidden(peers, *refs):
    in_refs, keep_ref, give_ref = refs[:peers], refs[peers], refs[peers + 1]
    quarter = keep_ref.shape[1] // 2
    low = low_rows(peers * ROWS, quarter)
    parts = [stack(in_refs, slice(b * quarter, (b + 1) * quarter)) for b in range(COLS)]
    whole = [jnp.where(low, part.astype(F32), 0.0).astype(BF) for part in parts]
    whole.append(unpack_last(peers, parts))
    half = lax.axis_index("dp") == 0
    for place in range(2):
        columns = slice(place * quarter, (place + 1) * quarter)
        first, second = whole[place].astype(F32), whole[place + 2].astype(F32)
        keep_ref[:, columns] = jnp.where(half, first, second).astype(BF)
        give_ref[:, columns] = jnp.where(half, second, first).astype(BF)


def weight_grad(keep_ref, kept_ref, own_ref, other_ref, out_ref):
    left = jnp.concatenate([keep_ref[...], kept_ref[...]], axis=0)
    right = jnp.concatenate([own_ref[...], other_ref[...]], axis=0)
    out_ref[0] = lax.dot_general(
        left, right, (((0,), (0,)), ((), ())), preferred_element_type=F32
    ).astype(BF)


def finish(peers, routes_ref, gates_ref, raw_ref, *refs):
    in_refs, hidden_ref, gate_ref = refs[:peers], refs[peers], refs[peers + 1]
    hits, place = routing(routes_ref[...], peers)
    gate = gate_of(hits, gates_ref[...])
    choice = choice_of(hits)
    top_count = routes_ref.shape[0]
    quarter = hidden_ref.shape[1] // 4
    rows = peers * ROWS
    routed = hidden_ref.shape[0]
    low = low_rows(rows, routed)
    total = jnp.zeros(gate_ref.shape, F32)
    ways, sent = [], []
    for block in range(COLS):
        columns = slice(block * quarter, (block + 1) * quarter)
        back = stack(in_refs, columns).astype(F32)
        pick = picks(place, peers, block)
        chosen = spread(choice, pick, peers)
        take = route_picks(pick, chosen, top_count)
        down = (((0,), (0,)), ((), ()))
        scaled = (spread(gate, pick, peers) * back).astype(BF)
        hidden_ref[:, columns] = lax.dot_general(
            jnp.where(low, take, 0.0).astype(BF), scaled, down, preferred_element_type=F32
        ).astype(BF)
        ways.append(jnp.where(low, 0.0, take).astype(BF))
        sent.append(scaled)
        value = jnp.sum(raw_ref[:, columns].astype(F32) * back, axis=1, keepdims=True)
        lines = [
            jnp.sum(jnp.where(chosen == float(k), pick * value, 0.0), axis=0, keepdims=True)
            for k in range(top_count)
        ]
        total = total + jnp.concatenate(lines, axis=0)
    hidden_ref[:, COLS * quarter :] = lax.dot_general(
        jnp.concatenate(ways, axis=0),
        jnp.concatenate(sent, axis=0),
        (((0,), (0,)), ((), ())),
        preferred_element_type=F32,
    ).astype(BF)
    gate_ref[...] = total


def local(out_grad, hidden, routes, gates, w_down):
    tokens, top_count = routes.shape
    units = hidden.shape[2]
    width = out_grad.shape[1]
    half = w_down.shape[1]
    routed = tokens * top_count
    peers = lax.axis_size("expert")
    rows = peers * ROWS
    routes_t, gates_t = routes.T, gates.T
    shape = jax.ShapeDtypeStruct
    packed_grad = [shape((ROWS, COLS * width // 4), BF)] * peers
    packed_units = [shape((ROWS, COLS * units // 4), BF)] * peers

    def across(array, step, back=False):
        pairs = [(i, partner(i, step, peers)) for i in range(peers)]
        return lax.ppermute(array, "expert", [(b, a) for a, b in pairs] if back else pairs)

    def swap(array):
        return lax.ppermute(array, "dp", [(0, 1), (1, 0)])

    send_grad = pl.pallas_call(
        functools.partial(pack_grad, peers),
        out_shape=packed_grad,
        in_specs=[vmem()] * 2,
        out_specs=[vmem()] * peers,
        compiler_params=params(),
        name="pack_grad",
    )(routes_t, out_grad)
    recv_grad = [send_grad[0]] + [across(send_grad[s], s) for s in range(1, peers)]
    w_other = swap(w_down)
    raw, *send_units = pl.pallas_call(
        functools.partial(pack_hidden, peers),
        out_shape=[shape((rows, COLS * units // 4), BF)] + packed_units,
        in_specs=[vmem()] * 3,
        out_specs=[vmem()] * (peers + 1),
        compiler_params=params(),
        name="pack_hidden",
    )(routes_t, gates_t, hidden.reshape(routed, units))
    recv_units = [send_units[0]] + [across(send_units[s], s) for s in range(1, peers)]
    tiles = 4
    whole = lambda *dims: pl.BlockSpec(dims, lambda i: (0,) * len(dims))
    all_grad, *unit_out = pl.pallas_call(
        functools.partial(unit_grads, peers, tiles),
        grid=(tiles,),
        out_shape=[shape((rows, width), BF)] + packed_units,
        in_specs=[whole(ROWS, COLS * width // 4)] * peers
        + [
            pl.BlockSpec((1, units // tiles, width), lambda i: (0, jnp.minimum(i, tiles // 2 - 1), 0)),
            pl.BlockSpec((1, units // tiles, width), lambda i: (0, jnp.maximum(i - tiles // 2, 0), 0)),
        ],
        out_specs=[whole(rows, width)] + [whole(ROWS, COLS * units // 4)] * peers,
        scratch_shapes=[pltpu.VMEM((tiles, rows, units // tiles), BF)],
        compiler_params=params(),
        name="unit_grads",
    )(*recv_grad, w_down, w_other)
    back = [unit_out[0]] + [across(unit_out[s], s, True) for s in range(1, peers)]
    other_grad = swap(all_grad)
    keep, give = pl.pallas_call(
        functools.partial(split_hidden, peers),
        out_shape=[shape((rows, half), BF)] * 2,
        in_specs=[vmem()] * peers,
        out_specs=[vmem()] * 2,
        compiler_params=params(),
        name="split_hidden",
    )(*recv_units)
    kept = swap(give)
    strip = 896 if width % 896 == 0 else width
    grad_down = pl.pallas_call(
        weight_grad,
        grid=(width // strip,),
        out_shape=shape((1, half, width), BF),
        in_specs=[whole(rows, half)] * 2 + [pl.BlockSpec((rows, strip), lambda i: (0, i))] * 2,
        out_specs=pl.BlockSpec((1, half, strip), lambda i: (0, 0, i)),
        compiler_params=params(),
        name="weight_grad",
    )(keep, kept, all_grad, other_grad)
    grad_hidden, grad_gates_t = pl.pallas_call(
        functools.partial(finish, peers),
        out_shape=[shape((routed, units), BF), shape((top_count, tokens), F32)],
        in_specs=[vmem()] * (peers + 3),
        out_specs=[vmem()] * 2,
        compiler_params=params(),
        name="finish",
    )(routes_t, gates_t, raw, *back)
    return grad_down, grad_hidden.reshape(tokens, top_count, units), grad_gates_t.T


def solution(mesh):
    in_specs = (
        P(("groups", "expert", "dp"), None),
        P(("groups", "expert", "dp"), None, None),
        P(("groups", "expert", "dp"), None),
        P(("groups", "expert", "dp"), None),
        P("expert", "dp", None),
    )
    out_specs = (
        P(("groups", "expert"), "dp", None),
        P(("groups", "expert", "dp"), None, None),
        P(("groups", "expert", "dp"), None),
    )
    return jax.shard_map(local, mesh=mesh, in_specs=in_specs, out_specs=out_specs, check_vma=False)
```

time: 114 us -> 76.1 us (0.67)
  starting transfers between devices: 10.8 us -> 39.1 us
  blocking collectives: 26.6 us -> 0 us
  local copies, waits for them, and re-layouts: 23.8 us -> 5.74 us
  Pallas kernels: 0 us -> 14.1 us
  between operations: 14.2 us -> 0.74 us
  matrix products: 13 us -> 0 us
  other arithmetic: 12.1 us -> 0 us
  waiting for transfers between devices: 12.8 us -> 16.1 us
    ppermute x0 -> x24, starting transfers between devices: none -> 39.1 us  [the longest x21 38.5 us: across(): lax.ppermute(array, 'expert', [(b, a) for a, b in pairs] if back else pairs)]
    all_to_all x1 -> x0, blocking collectives: 26.6 us -> none  [local(): lax.all_to_all(send_grad, 'expert', split_axis=0, concat_axis=0, tiled=True)]
    ppermute x0 -> x24, waiting for transfers between devices: none -> 16.1 us  [the longest x21 16.1 us: across(): lax.ppermute(array, 'expert', [(b, a) for a, b in pairs] if back else pairs)]
    pallas_call x0 -> x6, Pallas kernels: none -> 14.1 us  [the longest x1 5.95 us: local(): pl.pallas_call(functools.partial(unit_grads, peers, tiles), grid=(tiles,)...]
    dot_general x2 -> x0, matrix products: 13 us -> none  [the longest x1 7.31 us: local(): lax.dot_general(recv_scaled, recv_grad, (((0,), (0,)), ((), ())), preferr...]
    all_to_all x2 -> x0, waiting for transfers between devices: 12.1 us -> none  [the longest x1 8.35 us: local(): lax.all_to_all(unit_grad.reshape(peers, depth, units), 'expert', split_ax...]
    all_to_all x2 -> x0, starting transfers between devices: 10.7 us -> none  [the longest x1 7.27 us: local(): lax.all_to_all(send_scaled, 'expert', split_axis=0, concat_axis=0, tiled=...]
    gather x3 -> x0, local copies, waits for them, and re-layouts: 10.3 us -> none  [the longest x1 5.34 us: local(): route_grad = back_pad[target].astype(jnp.float32)]
  transfers between devices with their start and end apart: 4 -> 24, of which waited for: 2 -> 9; matrix products, arithmetic and copies ran while one was open for 38% -> 0% of each run, Pallas kernels for 0% -> 6%
where the time goes in v1:
time: 76.1 us; the launch traced here: 75.8 us
  starting transfers between devices  39.1 us (51%)
  waiting for transfers between devices  16.1 us (21%)
  Pallas kernels  14.1 us (19%)
  local copies, waits for them, and re-layouts  5.74 us (8%)
    ppermute x21, starting transfers between devices, across(): lax.ppermute(array, 'expert', [(b, a) for a, b in pairs] if back else pairs)  38.5 us
    ppermute x21, waiting for transfers between devices, across(): lax.ppermute(array, 'expert', [(b, a) for a, b in pairs] if back else pairs)  16.1 us
    pallas_call x1, Pallas kernels, local(): pl.pallas_call(functools.partial(unit_grads, peers, tiles), grid=(tiles,)...  5.95 us
    unnamed x14, local copies, waits for them, and re-layouts  5.74 us
    pallas_call x1, Pallas kernels, local(): pl.pallas_call(weight_grad, grid=(width // strip,), out_shape=shape((1, h...  3.38 us
    pallas_call x1, Pallas kernels, local(): pl.pallas_call(functools.partial(finish, peers), out_shape=[shape((routed...  2.98 us
  transfers between devices with their start and end apart: 24, of which 9 were waited for; matrix products, arithmetic and copies ran while one was open for 0% of the time, Pallas kernels for 6%

profile of v1, /device:TPU:0, one launch (start us, length us, event | category | flops | bytes accessed | tf_op | source)
XLA Modules:
  0.0 75.8 jit_solution(6481228777345106365)
XLA Ops:
  0.6 0.5 collective-permute-start.15
  1.1 1.2 %copy-done.2 = bf16[128,3584]{1,0:T(8,128)(2,1)S(1)} copy-done((bf16[128,3584]{1,0:T(8,128)(2,1)S(1)}, bf16[128,3584]{1,0:T(8,128)(2,1)}, u32[]{:S(2)}) %copy-start.2) | copy-done | bytes 917528
  2.3 0.7 copy-done.3
  3.0 0.5 pack_grad.1
  3.5 2.6 %collective-permute-start.8 = (bf16[16,2688]{1,0:T(8,128)(2,1)S(1)}, bf16[16,2688]{1,0:T(8,128)(2,1)S(1)}, u32[]{:S(2)}, u32[]{:S(2)}) collective-permute-start(bf16[16,2688]{1,0:T(8,128)(2,1)S(1)} %get-tuple-element.44), channel_id=1, source_target_pairs={{0,2},{2,0},{4,6},{6,4},{8,10},{10,8},{12,14},{14,12},{1,3},{3,1},... | collective-permute-start | bytes 258056 | tf_op jit(solution)/shard_map/ppermute | solution.py:291
  6.1 1.6 %collective-permute-start.9 = (bf16[16,2688]{1,0:T(8,128)(2,1)S(1)}, bf16[16,2688]{1,0:T(8,128)(2,1)S(1)}, u32[]{:S(2)}, u32[]{:S(2)}) collective-permute-start(bf16[16,2688]{1,0:T(8,128)(2,1)S(1)} %get-tuple-element.45), channel_id=1, source_target_pairs={{0,4},{2,6},{4,0},{6,2},{8,12},{10,14},{12,8},{14,10},{1,5},{3,7},... | collective-permute-start | bytes 258056 | tf_op jit(solution)/shard_map/ppermute | solution.py:291
  7.7 0.0 collective-permute-start.10
  7.7 3.0 %collective-permute-start.11 = (bf16[16,2688]{1,0:T(8,128)(2,1)S(1)}, bf16[16,2688]{1,0:T(8,128)(2,1)S(1)}, u32[]{:S(2)}, u32[]{:S(2)}) collective-permute-start(bf16[16,2688]{1,0:T(8,128)(2,1)S(1)} %get-tuple-element.47), channel_id=1, source_target_pairs={{0,8},{2,10},{4,12},{6,14},{8,0},{10,2},{12,4},{14,6},{1,9},{3,11}... | collective-permute-start | bytes 258056 | tf_op jit(solution)/shard_map/ppermute | solution.py:291
  10.7 0.0 collective-permute-done.8.refs_1_
  10.7 2.4 %collective-permute-start.12 = (bf16[16,2688]{1,0:T(8,128)(2,1)S(1)}, bf16[16,2688]{1,0:T(8,128)(2,1)S(1)}, u32[]{:S(2)}, u32[]{:S(2)}) collective-permute-start(bf16[16,2688]{1,0:T(8,128)(2,1)S(1)} %get-tuple-element.48), channel_id=1, source_target_pairs={{0,10},{2,8},{4,14},{6,12},{8,2},{10,0},{12,6},{14,4},{1,11},{3,9}... | collective-permute-start | bytes 258056 | tf_op jit(solution)/shard_map/ppermute | solution.py:291
  13.0 0.1 collective-permute-done.9.refs_2_
  13.2 2.5 %collective-permute-start.13 = (bf16[16,2688]{1,0:T(8,128)(2,1)S(1)}, bf16[16,2688]{1,0:T(8,128)(2,1)S(1)}, u32[]{:S(2)}, u32[]{:S(2)}) collective-permute-start(bf16[16,2688]{1,0:T(8,128)(2,1)S(1)} %get-tuple-element.49), channel_id=1, source_target_pairs={{0,12},{2,14},{4,8},{6,10},{8,4},{10,6},{12,0},{14,2},{1,13},{3,15... | collective-permute-start | bytes 258056 | tf_op jit(solution)/shard_map/ppermute | solution.py:291
  15.7 0.0 collective-permute-done.10.refs_3_
  15.7 2.6 %collective-permute-start.14 = (bf16[16,2688]{1,0:T(8,128)(2,1)S(1)}, bf16[16,2688]{1,0:T(8,128)(2,1)S(1)}, u32[]{:S(2)}, u32[]{:S(2)}) collective-permute-start(bf16[16,2688]{1,0:T(8,128)(2,1)S(1)} %get-tuple-element.50), channel_id=1, source_target_pairs={{0,14},{2,12},{4,10},{6,8},{8,6},{10,4},{12,2},{14,0},{1,15},{3,13... | collective-permute-start | bytes 258056 | tf_op jit(solution)/shard_map/ppermute | solution.py:291
  18.3 0.0 collective-permute-done.11.refs_4_
  18.3 5.9 %collective-permute-done.12.refs_5_ = bf16[16,2688]{1,0:T(8,128)(2,1)S(1)} collective-permute-done((bf16[16,2688]{1,0:T(8,128)(2,1)S(1)}, bf16[16,2688]{1,0:T(8,128)(2,1)S(1)}, u32[]{:S(2)}, u32[]{:S(2)}) %collective-permute-start.12) | collective-permute-done | bytes 86048 | tf_op jit(solution)/shard_map/ppermute | solution.py:291
  24.2 0.0 collective-permute-done.13.refs_6_
  24.2 0.0 copy-start.6
  24.3 1.8 %copy-done.6 = bf16[1,512,3584]{2,1,0:T(8,128)(2,1)} copy-done((bf16[1,512,3584]{2,1,0:T(8,128)(2,1)}, bf16[1,512,3584]{2,1,0:T(8,128)(2,1)S(1)}, u32[]{:S(2)}) %copy-start.6) | copy-done | bytes 3670040
  26.1 2.0 %copy-done = bf16[1,512,3584]{2,1,0:T(8,128)(2,1)S(1)} copy-done((bf16[1,512,3584]{2,1,0:T(8,128)(2,1)S(1)}, bf16[1,512,3584]{2,1,0:T(8,128)(2,1)}, u32[]{:S(2)}) %copy-start) | copy-done | bytes 3670040
  28.1 6.0 %unit_grads.1 = (bf16[128,3584]{1,0:T(8,128)(2,1)S(1)}, bf16[16,768]{1,0:T(8,128)(2,1)S(1)}, bf16[16,768]{1,0:T(8,128)(2,1)S(1)}, bf16[16,768]{1,0:T(8,128)(2,1)...) custom-call(bf16[16,2688]{1,0:T(8,128)(2,1)S(1)} %get-tuple-element., ...), custom_call_target="tpu_custom_call" | custom-call | tf_op jit(solution)/shard_map/unit_grads/pallas_call | solution.py:317
  34.1 0.1 collective-permute-start.16
  34.2 1.1 %pack_hidden.1 = (bf16[128,768]{1,0:T(8,128)(2,1)S(1)}, bf16[16,768]{1,0:T(8,128)(2,1)S(1)}, bf16[16,768]{1,0:T(8,128)(2,1)S(1)}, bf16[16,768]{1,0:T(8,128)(2,1)...) custom-call(s32[8,128]{1,0:T(8,128)S(1)} %bitcast.7, ...), custom_call_target="tpu_custom_call" | custom-call | tf_op jit(solution)/shard_map/pack_hidden/pallas_call | solution.py:306
  35.3 1.3 %collective-permute-start = (bf16[16,768]{1,0:T(8,128)(2,1)S(1)}, bf16[16,768]{1,0:T(8,128)(2,1)S(1)}, u32[]{:S(2)}, u32[]{:S(2)}) collective-permute-start(bf16[16,768]{1,0:T(8,128)(2,1)S(1)} %get-tuple-element.34), channel_id=1, source_target_pairs={{0,2},{2,0},{4,6},{6,4},{8,10},{10,8},{12,14},{14,12},{1,3},{3,1},... | collective-permute-start | bytes 73736 | tf_op jit(solution)/shard_map/ppermute | solution.py:291
  36.6 3.7 %collective-permute-start.1 = (bf16[16,768]{1,0:T(8,128)(2,1)S(1)}, bf16[16,768]{1,0:T(8,128)(2,1)S(1)}, u32[]{:S(2)}, u32[]{:S(2)}) collective-permute-start(bf16[16,768]{1,0:T(8,128)(2,1)S(1)} %get-tuple-element.35), channel_id=1, source_target_pairs={{0,4},{2,6},{4,0},{6,2},{8,12},{10,14},{12,8},{14,10},{1,5},{3,7},... | collective-permute-start | bytes 73736 | tf_op jit(solution)/shard_map/ppermute | solution.py:291
  40.3 0.2 collective-permute-start.2
  40.5 3.7 %collective-permute-start.3 = (bf16[16,768]{1,0:T(8,128)(2,1)S(1)}, bf16[16,768]{1,0:T(8,128)(2,1)S(1)}, u32[]{:S(2)}, u32[]{:S(2)}) collective-permute-start(bf16[16,768]{1,0:T(8,128)(2,1)S(1)} %get-tuple-element.37), channel_id=1, source_target_pairs={{0,8},{2,10},{4,12},{6,14},{8,0},{10,2},{12,4},{14,6},{1,9},{3,11}... | collective-permute-start | bytes 73736 | tf_op jit(solution)/shard_map/ppermute | solution.py:291
  44.2 0.3 collective-permute-start.4
  44.6 2.0 %collective-permute-start.5 = (bf16[16,768]{1,0:T(8,128)(2,1)S(1)}, bf16[16,768]{1,0:T(8,128)(2,1)S(1)}, u32[]{:S(2)}, u32[]{:S(2)}) collective-permute-start(bf16[16,768]{1,0:T(8,128)(2,1)S(1)} %get-tuple-element.39), channel_id=1, source_target_pairs={{0,12},{2,14},{4,8},{6,10},{8,4},{10,6},{12,0},{14,2},{1,13},{3,15... | collective-permute-start | bytes 73736 | tf_op jit(solution)/shard_map/ppermute | solution.py:291
  46.6 2.7 %collective-permute-start.6 = (bf16[16,768]{1,0:T(8,128)(2,1)S(1)}, bf16[16,768]{1,0:T(8,128)(2,1)S(1)}, u32[]{:S(2)}, u32[]{:S(2)}) collective-permute-start(bf16[16,768]{1,0:T(8,128)(2,1)S(1)} %get-tuple-element.40), channel_id=1, source_target_pairs={{0,14},{2,12},{4,10},{6,8},{8,6},{10,4},{12,2},{14,0},{1,15},{3,13... | collective-permute-start | bytes 73736 | tf_op jit(solution)/shard_map/ppermute | solution.py:291
  49.3 0.7 collective-permute-done.4.refs_5_
  50.0 0.2 collective-permute-done.5.refs_6_
  50.2 2.9 %collective-permute-done.6.refs_7_ = bf16[16,768]{1,0:T(8,128)(2,1)S(1)} collective-permute-done((bf16[16,768]{1,0:T(8,128)(2,1)S(1)}, bf16[16,768]{1,0:T(8,128)(2,1)S(1)}, u32[]{:S(2)}, u32[]{:S(2)}) %collective-permute-start.6) | collective-permute-done | bytes 24608 | tf_op jit(solution)/shard_map/ppermute | solution.py:291
  53.1 0.2 split_hidden.1
  53.3 0.1 collective-permute-start.7
  53.4 1.5 %collective-permute-start.17 = (bf16[16,768]{1,0:T(8,128)(2,1)S(1)}, bf16[16,768]{1,0:T(8,128)(2,1)S(1)}, u32[]{:S(2)}, u32[]{:S(2)}) collective-permute-start(bf16[16,768]{1,0:T(8,128)(2,1)S(1)} %get-tuple-element.54), channel_id=1, source_target_pairs={{2,0},{0,2},{6,4},{4,6},{10,8},{8,10},{14,12},{12,14},{3,1},{1,3},... | collective-permute-start | bytes 73736 | tf_op jit(solution)/shard_map/ppermute | solution.py:291
  54.9 0.0 collective-permute-start.18
  54.9 2.0 %collective-permute-start.19 = (bf16[16,768]{1,0:T(8,128)(2,1)S(1)}, bf16[16,768]{1,0:T(8,128)(2,1)S(1)}, u32[]{:S(2)}, u32[]{:S(2)}) collective-permute-start(bf16[16,768]{1,0:T(8,128)(2,1)S(1)} %get-tuple-element.56), channel_id=1, source_target_pairs={{6,0},{4,2},{2,4},{0,6},{14,8},{12,10},{10,12},{8,14},{7,1},{5,3},... | collective-permute-start | bytes 73736 | tf_op jit(solution)/shard_map/ppermute | solution.py:291
  57.0 0.3 collective-permute-done.17.refs_1_
  57.3 0.0 collective-permute-start.20
  57.3 1.5 %collective-permute-done.18.refs_2_ = bf16[16,768]{1,0:T(8,128)(2,1)S(1)} collective-permute-done((bf16[16,768]{1,0:T(8,128)(2,1)S(1)}, bf16[16,768]{1,0:T(8,128)(2,1)S(1)}, u32[]{:S(2)}, u32[]{:S(2)}) %collective-permute-start.18) | collective-permute-done | bytes 24608 | tf_op jit(solution)/shard_map/ppermute | solution.py:291
  58.8 2.4 %collective-permute-start.21 = (bf16[16,768]{1,0:T(8,128)(2,1)S(1)}, bf16[16,768]{1,0:T(8,128)(2,1)S(1)}, u32[]{:S(2)}, u32[]{:S(2)}) collective-permute-start(bf16[16,768]{1,0:T(8,128)(2,1)S(1)} %get-tuple-element.58), channel_id=1, source_target_pairs={{10,0},{8,2},{14,4},{12,6},{2,8},{0,10},{6,12},{4,14},{11,1},{9,3}... | collective-permute-start | bytes 73736 | tf_op jit(solution)/shard_map/ppermute | solution.py:291
  61.1 1.8 %collective-permute-start.22 = (bf16[16,768]{1,0:T(8,128)(2,1)S(1)}, bf16[16,768]{1,0:T(8,128)(2,1)S(1)}, u32[]{:S(2)}, u32[]{:S(2)}) collective-permute-start(bf16[16,768]{1,0:T(8,128)(2,1)S(1)} %get-tuple-element.59), channel_id=1, source_target_pairs={{12,0},{14,2},{8,4},{10,6},{4,8},{6,10},{0,12},{2,14},{13,1},{15,3... | collective-permute-start | bytes 73736 | tf_op jit(solution)/shard_map/ppermute | solution.py:291
  62.9 2.1 %collective-permute-start.23 = (bf16[16,768]{1,0:T(8,128)(2,1)S(1)}, bf16[16,768]{1,0:T(8,128)(2,1)S(1)}, u32[]{:S(2)}, u32[]{:S(2)}) collective-permute-start(bf16[16,768]{1,0:T(8,128)(2,1)S(1)} %get-tuple-element.60), channel_id=1, source_target_pairs={{14,0},{12,2},{10,4},{8,6},{6,8},{4,10},{2,12},{0,14},{15,1},{13,3... | collective-permute-start | bytes 73736 | tf_op jit(solution)/shard_map/ppermute | solution.py:291
  65.1 1.7 %collective-permute-done.22.refs_6_ = bf16[16,768]{1,0:T(8,128)(2,1)S(1)} collective-permute-done((bf16[16,768]{1,0:T(8,128)(2,1)S(1)}, bf16[16,768]{1,0:T(8,128)(2,1)S(1)}, u32[]{:S(2)}, u32[]{:S(2)}) %collective-permute-start.22) | collective-permute-done | bytes 24608 | tf_op jit(solution)/shard_map/ppermute | solution.py:291
  66.8 2.7 %collective-permute-done.23.refs_7_ = bf16[16,768]{1,0:T(8,128)(2,1)S(1)} collective-permute-done((bf16[16,768]{1,0:T(8,128)(2,1)S(1)}, bf16[16,768]{1,0:T(8,128)(2,1)S(1)}, u32[]{:S(2)}, u32[]{:S(2)}) %collective-permute-start.23) | collective-permute-done | bytes 24608 | tf_op jit(solution)/shard_map/ppermute | solution.py:291
  69.5 3.0 %finish.1 = (bf16[1024,1024]{1,0:T(8,128)(2,1)}, f32[8,128]{1,0:T(8,128)}) custom-call(s32[8,128]{1,0:T(8,128)S(1)} %bitcast.8, f32[8,128]{1,0:T(8,128)S(1)} %bitcast.10, bf16[128,768]{1,0:T(8,128)(2,1)S(1)} %get-tuple-element.52.raw_ref, bf16[16,768]{1,0:T(8,128)(2,1)S(1)} %get-tuple-element.53.refs_0_, ...), custom_call_target="tpu_custom_call" | custom-call | tf_op jit(solution)/shard_map/finish/pallas_call | solution.py:352
  72.5 3.4 %weight_grad.1 = bf16[1,512,3584]{2,1,0:T(8,128)(2,1)} custom-call(bf16[128,512]{1,0:T(8,128)(2,1)S(1)} %get-tuple-element.41.keep_ref, bf16[128,512]{1,0:T(8,128)(2,1)S(1)} %collective-permute-done.7.kept_ref, bf16[128,3584]{1,0:T(8,128)(2,1)S(1)} %get-tuple-element.51.own_ref, bf16[128,3584]{1,0:T(8,128)(2,1)S(1)} %collective-permute-done.16.other_ref), custom_call_target="tpu_custom_call" | custom-call | tf_op jit(solution)/shard_map/weight_grad/pallas_call | solution.py:343
  (20 shorter events, 0.0 us)
Async XLA Ops:
  0.6 23.6 %collective-permute-start.15 = (bf16[1,512,3584]{2,1,0:T(8,128)(2,1)}, bf16[1,512,3584]{2,1,0:T(8,128)(2,1)S(1)}, u32[]{:S(2)}, u32[]{:S(2)}) collective-permute-start(bf16[1,512,3584]{2,1,0:T(8,128)(2,1)} %refs_8_.1), channel_id=1, source_target_pairs={{0,1},{1,0},{2,3},{3,2},{4,5},{5,4},{6,7},{7,6},{8,9},{9,8},{10,11... | collective-permute-start | bytes 11010056 | tf_op jit(solution)/shard_map/ppermute | solution.py:294
  1.1 1.2 %copy-start.2 = (bf16[128,3584]{1,0:T(8,128)(2,1)S(1)}, bf16[128,3584]{1,0:T(8,128)(2,1)}, u32[]{:S(2)}) copy-start(bf16[128,3584]{1,0:T(8,128)(2,1)} %grad_ref.1) | copy-start | bytes 2752516
  2.3 0.7 copy-start.3
  3.5 7.2 %collective-permute-start.8 = (bf16[16,2688]{1,0:T(8,128)(2,1)S(1)}, bf16[16,2688]{1,0:T(8,128)(2,1)S(1)}, u32[]{:S(2)}, u32[]{:S(2)}) collective-permute-start(bf16[16,2688]{1,0:T(8,128)(2,1)S(1)} %get-tuple-element.44), channel_id=1, source_target_pairs={{0,2},{2,0},{4,6},{6,4},{8,10},{10,8},{12,14},{14,12},{1,3},{3,1},... | collective-permute-start | bytes 258056 | tf_op jit(solution)/shard_map/ppermute | solution.py:291
  6.1 7.1 %collective-permute-start.9 = (bf16[16,2688]{1,0:T(8,128)(2,1)S(1)}, bf16[16,2688]{1,0:T(8,128)(2,1)S(1)}, u32[]{:S(2)}, u32[]{:S(2)}) collective-permute-start(bf16[16,2688]{1,0:T(8,128)(2,1)S(1)} %get-tuple-element.45), channel_id=1, source_target_pairs={{0,4},{2,6},{4,0},{6,2},{8,12},{10,14},{12,8},{14,10},{1,5},{3,7},... | collective-permute-start | bytes 258056 | tf_op jit(solution)/shard_map/ppermute | solution.py:291
  7.7 8.0 %collective-permute-start.10 = (bf16[16,2688]{1,0:T(8,128)(2,1)S(1)}, bf16[16,2688]{1,0:T(8,128)(2,1)S(1)}, u32[]{:S(2)}, u32[]{:S(2)}) collective-permute-start(bf16[16,2688]{1,0:T(8,128)(2,1)S(1)} %get-tuple-element.46), channel_id=1, source_target_pairs={{0,6},{2,4},{4,2},{6,0},{8,14},{10,12},{12,10},{14,8},{1,7},{3,5},... | collective-permute-start | bytes 258056 | tf_op jit(solution)/shard_map/ppermute | solution.py:291
  7.7 10.6 %collective-permute-start.11 = (bf16[16,2688]{1,0:T(8,128)(2,1)S(1)}, bf16[16,2688]{1,0:T(8,128)(2,1)S(1)}, u32[]{:S(2)}, u32[]{:S(2)}) collective-permute-start(bf16[16,2688]{1,0:T(8,128)(2,1)S(1)} %get-tuple-element.47), channel_id=1, source_target_pairs={{0,8},{2,10},{4,12},{6,14},{8,0},{10,2},{12,4},{14,6},{1,9},{3,11}... | collective-permute-start | bytes 258056 | tf_op jit(solution)/shard_map/ppermute | solution.py:291
  10.7 13.6 %collective-permute-start.12 = (bf16[16,2688]{1,0:T(8,128)(2,1)S(1)}, bf16[16,2688]{1,0:T(8,128)(2,1)S(1)}, u32[]{:S(2)}, u32[]{:S(2)}) collective-permute-start(bf16[16,2688]{1,0:T(8,128)(2,1)S(1)} %get-tuple-element.48), channel_id=1, source_target_pairs={{0,10},{2,8},{4,14},{6,12},{8,2},{10,0},{12,6},{14,4},{1,11},{3,9}... | collective-permute-start | bytes 258056 | tf_op jit(solution)/shard_map/ppermute | solution.py:291
  13.2 11.1 %collective-permute-start.13 = (bf16[16,2688]{1,0:T(8,128)(2,1)S(1)}, bf16[16,2688]{1,0:T(8,128)(2,1)S(1)}, u32[]{:S(2)}, u32[]{:S(2)}) collective-permute-start(bf16[16,2688]{1,0:T(8,128)(2,1)S(1)} %get-tuple-element.49), channel_id=1, source_target_pairs={{0,12},{2,14},{4,8},{6,10},{8,4},{10,6},{12,0},{14,2},{1,13},{3,15... | collective-permute-start | bytes 258056 | tf_op jit(solution)/shard_map/ppermute | solution.py:291
  15.7 8.6 %collective-permute-start.14 = (bf16[16,2688]{1,0:T(8,128)(2,1)S(1)}, bf16[16,2688]{1,0:T(8,128)(2,1)S(1)}, u32[]{:S(2)}, u32[]{:S(2)}) collective-permute-start(bf16[16,2688]{1,0:T(8,128)(2,1)S(1)} %get-tuple-element.50), channel_id=1, source_target_pairs={{0,14},{2,12},{4,10},{6,8},{8,6},{10,4},{12,2},{14,0},{1,15},{3,13... | collective-permute-start | bytes 258056 | tf_op jit(solution)/shard_map/ppermute | solution.py:291
  24.2 1.8 %copy-start.6 = (bf16[1,512,3584]{2,1,0:T(8,128)(2,1)}, bf16[1,512,3584]{2,1,0:T(8,128)(2,1)S(1)}, u32[]{:S(2)}) copy-start(bf16[1,512,3584]{2,1,0:T(8,128)(2,1)S(1)} %collective-permute-done.15.refs_9_) | copy-start | bytes 11010052
  26.1 2.0 %copy-start = (bf16[1,512,3584]{2,1,0:T(8,128)(2,1)S(1)}, bf16[1,512,3584]{2,1,0:T(8,128)(2,1)}, u32[]{:S(2)}) copy-start(bf16[1,512,3584]{2,1,0:T(8,128)(2,1)} %refs_8_.1) | copy-start | bytes 11010052
  28.1 6.0 %copy-start.1 = (bf16[128,8,1024]{2,1,0:T(8,128)(2,1)S(1)}, bf16[128,8,1024]{2,1,0:T(8,128)(2,1)}, u32[]{:S(2)}) copy-start(bf16[128,8,1024]{2,1,0:T(8,128)(2,1)} %param.6) | copy-start | bytes 6291460
  28.1 6.1 %copy-start.4 = (s32[128,8]{0,1:T(8,128)S(1)}, s32[128,8]{0,1:T(8,128)}, u32[]{:S(2)}) copy-start(s32[128,8]{0,1:T(8,128)} %param.7) | copy-start | bytes 12292
  28.1 6.1 %copy-start.5 = (f32[128,8]{0,1:T(8,128)S(1)}, f32[128,8]{0,1:T(8,128)}, u32[]{:S(2)}) copy-start(f32[128,8]{0,1:T(8,128)} %param.8) | copy-start | bytes 12292
  34.1 38.4 %collective-permute-start.16 = (bf16[128,3584]{1,0:T(8,128)(2,1)S(1)}, bf16[128,3584]{1,0:T(8,128)(2,1)S(1)}, u32[]{:S(2)}, u32[]{:S(2)}) collective-permute-start(bf16[128,3584]{1,0:T(8,128)(2,1)S(1)} %get-tuple-element.51.own_ref), channel_id=1, source_target_pairs={{0,1},{1,0},{2,3},{3,2},{4,5},{5,4},{6,7},{7,6},{8,9},{9,8},{10,11... | collective-permute-start | bytes 2752520 | tf_op jit(solution)/shard_map/ppermute | solution.py:294
  35.3 8.9 %collective-permute-start = (bf16[16,768]{1,0:T(8,128)(2,1)S(1)}, bf16[16,768]{1,0:T(8,128)(2,1)S(1)}, u32[]{:S(2)}, u32[]{:S(2)}) collective-permute-start(bf16[16,768]{1,0:T(8,128)(2,1)S(1)} %get-tuple-element.34), channel_id=1, source_target_pairs={{0,2},{2,0},{4,6},{6,4},{8,10},{10,8},{12,14},{14,12},{1,3},{3,1},... | collective-permute-start | bytes 73736 | tf_op jit(solution)/shard_map/ppermute | solution.py:291
  36.6 8.0 %collective-permute-start.1 = (bf16[16,768]{1,0:T(8,128)(2,1)S(1)}, bf16[16,768]{1,0:T(8,128)(2,1)S(1)}, u32[]{:S(2)}, u32[]{:S(2)}) collective-permute-start(bf16[16,768]{1,0:T(8,128)(2,1)S(1)} %get-tuple-element.35), channel_id=1, source_target_pairs={{0,4},{2,6},{4,0},{6,2},{8,12},{10,14},{12,8},{14,10},{1,5},{3,7},... | collective-permute-start | bytes 73736 | tf_op jit(solution)/shard_map/ppermute | solution.py:291
  40.3 6.3 %collective-permute-start.2 = (bf16[16,768]{1,0:T(8,128)(2,1)S(1)}, bf16[16,768]{1,0:T(8,128)(2,1)S(1)}, u32[]{:S(2)}, u32[]{:S(2)}) collective-permute-start(bf16[16,768]{1,0:T(8,128)(2,1)S(1)} %get-tuple-element.36), channel_id=1, source_target_pairs={{0,6},{2,4},{4,2},{6,0},{8,14},{10,12},{12,10},{14,8},{1,7},{3,5},... | collective-permute-start | bytes 73736 | tf_op jit(solution)/shard_map/ppermute | solution.py:291
  40.5 8.8 %collective-permute-start.3 = (bf16[16,768]{1,0:T(8,128)(2,1)S(1)}, bf16[16,768]{1,0:T(8,128)(2,1)S(1)}, u32[]{:S(2)}, u32[]{:S(2)}) collective-permute-start(bf16[16,768]{1,0:T(8,128)(2,1)S(1)} %get-tuple-element.37), channel_id=1, source_target_pairs={{0,8},{2,10},{4,12},{6,14},{8,0},{10,2},{12,4},{14,6},{1,9},{3,11}... | collective-permute-start | bytes 73736 | tf_op jit(solution)/shard_map/ppermute | solution.py:291
  44.2 5.7 %collective-permute-start.4 = (bf16[16,768]{1,0:T(8,128)(2,1)S(1)}, bf16[16,768]{1,0:T(8,128)(2,1)S(1)}, u32[]{:S(2)}, u32[]{:S(2)}) collective-permute-start(bf16[16,768]{1,0:T(8,128)(2,1)S(1)} %get-tuple-element.38), channel_id=1, source_target_pairs={{0,10},{2,8},{4,14},{6,12},{8,2},{10,0},{12,6},{14,4},{1,11},{3,9}... | collective-permute-start | bytes 73736 | tf_op jit(solution)/shard_map/ppermute | solution.py:291
  44.6 5.6 %collective-permute-start.5 = (bf16[16,768]{1,0:T(8,128)(2,1)S(1)}, bf16[16,768]{1,0:T(8,128)(2,1)S(1)}, u32[]{:S(2)}, u32[]{:S(2)}) collective-permute-start(bf16[16,768]{1,0:T(8,128)(2,1)S(1)} %get-tuple-element.39), channel_id=1, source_target_pairs={{0,12},{2,14},{4,8},{6,10},{8,4},{10,6},{12,0},{14,2},{1,13},{3,15... | collective-permute-start | bytes 73736 | tf_op jit(solution)/shard_map/ppermute | solution.py:291
  46.6 6.5 %collective-permute-start.6 = (bf16[16,768]{1,0:T(8,128)(2,1)S(1)}, bf16[16,768]{1,0:T(8,128)(2,1)S(1)}, u32[]{:S(2)}, u32[]{:S(2)}) collective-permute-start(bf16[16,768]{1,0:T(8,128)(2,1)S(1)} %get-tuple-element.40), channel_id=1, source_target_pairs={{0,14},{2,12},{4,10},{6,8},{8,6},{10,4},{12,2},{14,0},{1,15},{3,13... | collective-permute-start | bytes 73736 | tf_op jit(solution)/shard_map/ppermute | solution.py:291
  53.3 19.1 %collective-permute-start.7 = (bf16[128,512]{1,0:T(8,128)(2,1)S(1)}, bf16[128,512]{1,0:T(8,128)(2,1)S(1)}, u32[]{:S(2)}, u32[]{:S(2)}) collective-permute-start(bf16[128,512]{1,0:T(8,128)(2,1)S(1)} %get-tuple-element.42), channel_id=1, source_target_pairs={{0,1},{1,0},{2,3},{3,2},{4,5},{5,4},{6,7},{7,6},{8,9},{9,8},{10,11... | collective-permute-start | bytes 393224 | tf_op jit(solution)/shard_map/ppermute | solution.py:294
  53.4 3.9 %collective-permute-start.17 = (bf16[16,768]{1,0:T(8,128)(2,1)S(1)}, bf16[16,768]{1,0:T(8,128)(2,1)S(1)}, u32[]{:S(2)}, u32[]{:S(2)}) collective-permute-start(bf16[16,768]{1,0:T(8,128)(2,1)S(1)} %get-tuple-element.54), channel_id=1, source_target_pairs={{2,0},{0,2},{6,4},{4,6},{10,8},{8,10},{14,12},{12,14},{3,1},{1,3},... | collective-permute-start | bytes 73736 | tf_op jit(solution)/shard_map/ppermute | solution.py:291
  54.9 3.8 %collective-permute-start.18 = (bf16[16,768]{1,0:T(8,128)(2,1)S(1)}, bf16[16,768]{1,0:T(8,128)(2,1)S(1)}, u32[]{:S(2)}, u32[]{:S(2)}) collective-permute-start(bf16[16,768]{1,0:T(8,128)(2,1)S(1)} %get-tuple-element.55), channel_id=1, source_target_pairs={{4,0},{6,2},{0,4},{2,6},{12,8},{14,10},{8,12},{10,14},{5,1},{7,3},... | collective-permute-start | bytes 73736 | tf_op jit(solution)/shard_map/ppermute | solution.py:291
  54.9 6.2 %collective-permute-start.19 = (bf16[16,768]{1,0:T(8,128)(2,1)S(1)}, bf16[16,768]{1,0:T(8,128)(2,1)S(1)}, u32[]{:S(2)}, u32[]{:S(2)}) collective-permute-start(bf16[16,768]{1,0:T(8,128)(2,1)S(1)} %get-tuple-element.56), channel_id=1, source_target_pairs={{6,0},{4,2},{2,4},{0,6},{14,8},{12,10},{10,12},{8,14},{7,1},{5,3},... | collective-permute-start | bytes 73736 | tf_op jit(solution)/shard_map/ppermute | solution.py:291
  57.3 5.6 %collective-permute-start.20 = (bf16[16,768]{1,0:T(8,128)(2,1)S(1)}, bf16[16,768]{1,0:T(8,128)(2,1)S(1)}, u32[]{:S(2)}, u32[]{:S(2)}) collective-permute-start(bf16[16,768]{1,0:T(8,128)(2,1)S(1)} %get-tuple-element.57), channel_id=1, source_target_pairs={{8,0},{10,2},{12,4},{14,6},{0,8},{2,10},{4,12},{6,14},{9,1},{11,3}... | collective-permute-start | bytes 73736 | tf_op jit(solution)/shard_map/ppermute | solution.py:291
  58.8 6.3 %collective-permute-start.21 = (bf16[16,768]{1,0:T(8,128)(2,1)S(1)}, bf16[16,768]{1,0:T(8,128)(2,1)S(1)}, u32[]{:S(2)}, u32[]{:S(2)}) collective-permute-start(bf16[16,768]{1,0:T(8,128)(2,1)S(1)} %get-tuple-element.58), channel_id=1, source_target_pairs={{10,0},{8,2},{14,4},{12,6},{2,8},{0,10},{6,12},{4,14},{11,1},{9,3}... | collective-permute-start | bytes 73736 | tf_op jit(solution)/shard_map/ppermute | solution.py:291
  61.1 5.6 %collective-permute-start.22 = (bf16[16,768]{1,0:T(8,128)(2,1)S(1)}, bf16[16,768]{1,0:T(8,128)(2,1)S(1)}, u32[]{:S(2)}, u32[]{:S(2)}) collective-permute-start(bf16[16,768]{1,0:T(8,128)(2,1)S(1)} %get-tuple-element.59), channel_id=1, source_target_pairs={{12,0},{14,2},{8,4},{10,6},{4,8},{6,10},{0,12},{2,14},{13,1},{15,3... | collective-permute-start | bytes 73736 | tf_op jit(solution)/shard_map/ppermute | solution.py:291
  62.9 6.5 %collective-permute-start.23 = (bf16[16,768]{1,0:T(8,128)(2,1)S(1)}, bf16[16,768]{1,0:T(8,128)(2,1)S(1)}, u32[]{:S(2)}, u32[]{:S(2)}) collective-permute-start(bf16[16,768]{1,0:T(8,128)(2,1)S(1)} %get-tuple-element.60), channel_id=1, source_target_pairs={{14,0},{12,2},{10,4},{8,6},{6,8},{4,10},{2,12},{0,14},{15,1},{13,3... | collective-permute-start | bytes 73736 | tf_op jit(solution)/shard_map/ppermute | solution.py:291

commit v2 on v1

v2 whole, which is shorter than its diff:
```python
import functools

import jax
import jax.numpy as jnp
from jax import lax
from jax.experimental import pallas as pl
from jax.experimental.pallas import tpu as pltpu
from jax.sharding import PartitionSpec as P

MOST = 12
ROWS = 16
COLS = 3
EXTRA = ROWS - MOST
BF = jnp.bfloat16
F32 = jnp.float32
MIB = 1 << 20
DOWN = (((0,), (0,)), ((), ()))


FREE = pl.CostEstimate(flops=0, bytes_accessed=0, transcendentals=0)


def params(mib=20, **kw):
    return pltpu.CompilerParams(vmem_limit_bytes=mib * MIB, **kw)


def vmem():
    return pl.BlockSpec(memory_space=pltpu.VMEM)


def anywhere():
    return pl.BlockSpec(memory_space=pl.ANY)


def partner(index, step, peers):
    if peers & (peers - 1) == 0:
        return index ^ step
    return lax.rem(index + step, peers) if isinstance(index, jax.Array) else (index + step) % peers


def routing(routes_t, peers):
    me = lax.axis_index("expert")
    tokens = routes_t.shape[1]
    hits = [routes_t == partner(me, step, peers) for step in range(peers)]
    member = jnp.concatenate(
        [jnp.max(hit.astype(F32), axis=0, keepdims=True) for hit in hits], axis=0
    )
    earlier = lax.broadcasted_iota(jnp.int32, (tokens, tokens), 0) < lax.broadcasted_iota(
        jnp.int32, (tokens, tokens), 1
    )
    before = jnp.dot(member.astype(BF), earlier.astype(F32).astype(BF), preferred_element_type=F32)
    return hits, jnp.where(member > 0, before, -1.0)


def picks(place, peers, block):
    tokens = place.shape[1]
    row = lax.broadcasted_iota(jnp.int32, (ROWS, tokens), 0)
    wanted = jnp.where(row < MOST, row, row - MOST + EXTRA * block).astype(F32)
    return jnp.concatenate(
        [(place[step : step + 1, :] == wanted).astype(F32) for step in range(peers)], axis=0
    )


def low_rows(rows, width):
    return lax.broadcasted_iota(jnp.int32, (rows, width), 0) % ROWS < MOST


def gate_of(hits, gates_t):
    return jnp.concatenate(
        [jnp.sum(jnp.where(hit, gates_t, 0.0), axis=0, keepdims=True) for hit in hits], axis=0
    )


def choice_of(hits):
    return jnp.concatenate(
        [
            jnp.sum(
                jnp.where(hit, lax.broadcasted_iota(jnp.int32, hit.shape, 0).astype(F32), 0.0),
                axis=0,
                keepdims=True,
            )
            for hit in hits
        ],
        axis=0,
    )


def spread(table, pick, peers):
    return jnp.concatenate(
        [
            jnp.sum(
                pick[step * ROWS : (step + 1) * ROWS, :] * table[step : step + 1, :],
                axis=1,
                keepdims=True,
            )
            for step in range(peers)
        ],
        axis=0,
    )


def route_picks(pick, choice, top_count):
    tokens = pick.shape[1]
    routed = tokens * top_count
    token = lax.broadcasted_iota(jnp.int32, (tokens, routed), 0)
    column = lax.broadcasted_iota(jnp.int32, (tokens, routed), 1)
    wide = (column // top_count == token).astype(F32).astype(BF)
    mine = jnp.dot(pick.astype(BF), wide, preferred_element_type=F32)
    which = (lax.broadcasted_iota(jnp.int32, (pick.shape[0], routed), 1) % top_count).astype(F32)
    return jnp.where(which == choice, mine, 0.0)


def pack(peers, *refs):
    sources, raw_ref, out_refs = refs[:4], refs[4], refs[5 : 5 + peers]
    held, sems = refs[5 + peers : -1], refs[-1]
    copies = [
        pltpu.make_async_copy(source, target, sems.at[index])
        for index, (source, target) in enumerate(zip(sources, held))
    ]
    for copy in copies:
        copy.start()
    for copy in copies:
        copy.wait()
    routes_ref, gates_ref, grad_ref, hidden_ref = held
    hits, place = routing(routes_ref[...], peers)
    gate = gate_of(hits, gates_ref[...])
    choice = choice_of(hits)
    tokens = grad_ref.shape[0]
    wide, quarter = grad_ref.shape[1] // 4, hidden_ref.shape[1] // 4
    low = low_rows(peers * ROWS, tokens)
    low_units = low_rows(peers * ROWS, quarter)
    last = grad_ref[:, COLS * wide :]
    last_units = hidden_ref[:, COLS * quarter :]
    for block in range(COLS):
        pick = picks(place, peers, block)
        both = jnp.concatenate(
            [jnp.where(low, pick, 0.0).astype(BF), jnp.where(low, 0.0, pick).astype(BF)], axis=1
        )
        columns = slice(block * wide, (block + 1) * wide)
        source = jnp.concatenate([grad_ref[:, columns], last], axis=0)
        packed = jnp.dot(both, source, preferred_element_type=F32).astype(BF)
        for step in range(peers):
            out_refs[step][:, columns] = packed[step * ROWS : (step + 1) * ROWS, :]
        take = route_picks(pick, spread(choice, pick, peers), routes_ref.shape[0]).astype(BF)
        columns = slice(block * quarter, (block + 1) * quarter)
        first = jnp.dot(take, hidden_ref[:, columns], preferred_element_type=F32)
        rest = jnp.dot(take, last_units, preferred_element_type=F32)
        raw = jnp.where(low_units, first, rest)
        raw_ref[:, columns] = raw.astype(BF)
        scaled = (spread(gate, pick, peers) * raw).astype(BF)
        columns = slice(COLS * wide + block * quarter, COLS * wide + (block + 1) * quarter)
        for step in range(peers):
            out_refs[step][:, columns] = scaled[step * ROWS : (step + 1) * ROWS, :]


def maps(peers, routes_ref, gates_ref, low_ref, high_ref, pick_ref, side_ref):
    hits, place = routing(routes_ref[...], peers)
    gate = gate_of(hits, gates_ref[...])
    choice = choice_of(hits)
    rows = peers * ROWS
    routed = low_ref.shape[0]
    low = low_rows(rows, routed)
    side_ref[...] = jnp.zeros_like(side_ref)
    for block in range(COLS):
        pick = picks(place, peers, block)
        chosen = spread(choice, pick, peers)
        take = route_picks(pick, chosen, routes_ref.shape[0])
        if block == 0:
            low_ref[...] = jnp.where(low, take, 0.0).T.astype(BF)
        high_ref[:, block * rows : (block + 1) * rows] = jnp.where(low, 0.0, take).T.astype(BF)
        pick_ref[block] = pick
        side_ref[:, block : block + 1] = spread(gate, pick, peers)
        side_ref[:, COLS + block : COLS + block + 1] = chosen


def last_quarter(peers, block):
    rows = peers * ROWS
    to = lax.broadcasted_iota(jnp.int32, (rows, rows), 0)
    at = lax.broadcasted_iota(jnp.int32, (rows, rows), 1)
    inside = at % ROWS
    wanted = at - MOST + EXTRA * block
    return ((inside >= MOST) & (to == wanted)).astype(F32).astype(BF)


def stack(refs, columns):
    return jnp.concatenate([ref[:, columns] for ref in refs], axis=0)


def unpack_last(peers, parts):
    moves = jnp.concatenate([last_quarter(peers, block) for block in range(COLS)], axis=1)
    return jnp.dot(moves, jnp.concatenate(parts, axis=0), preferred_element_type=F32).astype(BF)


def unit_grads(count, extra, *refs):
    in_refs, own_ref, other_ref = refs[:count], refs[count], refs[count + 1]
    refs = refs[: count + 2] + refs[count + 2 + extra :]
    swap_ref, keep_ref = refs[count + 2], refs[count + 3]
    out_refs = refs[count + 4 : 2 * count + 4]
    half_units, width = own_ref.shape[1], own_ref.shape[2]
    quarter, wide = half_units // 2, width // 4
    rows = count * ROWS
    first_core = lax.axis_index("dp") == 0
    parts = []
    for block in range(COLS):
        part = stack(in_refs, slice(block * wide, (block + 1) * wide))
        swap_ref[:, block * wide : (block + 1) * wide] = part
        parts.append(part)
    swap_ref[:, COLS * wide : 4 * wide] = unpack_last(count, parts)
    left = swap_ref[:, : 4 * wide]
    across = (((1,), (1,)), ((), ()))
    halves = [
        lax.dot_general(left, ref[0], across, preferred_element_type=F32)
        for ref in (own_ref, other_ref)
    ]
    low_half = jnp.where(first_core, halves[0], halves[1])
    high_half = jnp.where(first_core, halves[1], halves[0])
    units = [low_half[:, :quarter], low_half[:, quarter:], high_half[:, :quarter]]
    last = high_half[:, quarter:].astype(BF)
    low = low_rows(rows, quarter)
    for block in range(COLS):
        moved = lax.dot_general(
            last_quarter(count, block), last, DOWN, preferred_element_type=F32
        )
        packed = jnp.where(low, units[block], moved).astype(BF)
        for step in range(count):
            out_refs[step][:, block * quarter : (block + 1) * quarter] = packed[
                step * ROWS : (step + 1) * ROWS, :
            ]
    start = COLS * wide
    parts = [
        stack(in_refs, slice(start + b * quarter, start + (b + 1) * quarter)) for b in range(COLS)
    ]
    scaled = [jnp.where(low, part.astype(F32), 0.0) for part in parts]
    scaled.append(unpack_last(count, parts).astype(F32))
    for place in range(2):
        one, two = scaled[place], scaled[place + 2]
        keep_ref[:, place * quarter : (place + 1) * quarter] = jnp.where(
            first_core, one, two
        ).astype(BF)
        swap_ref[:, width + place * quarter : width + (place + 1) * quarter] = jnp.where(
            first_core, two, one
        ).astype(BF)


def weight_grad(groups, strip, *refs):
    keep_refs, own_refs, other_refs = (refs[i * groups : (i + 1) * groups] for i in range(3))
    out_ref, done_ref, held, sems = refs[3 * groups :]
    done_ref[...] = jnp.zeros_like(done_ref)
    width = out_ref.shape[2]
    half = out_ref.shape[1]
    left = jnp.concatenate(
        [ref[...] for ref in keep_refs] + [ref[:, width : width + half] for ref in other_refs], axis=0
    )
    copies = []
    for index in range(width // strip):
        columns = slice(index * strip, (index + 1) * strip)
        right = jnp.concatenate([ref[:, columns] for ref in (*own_refs, *other_refs)], axis=0)
        slot = index % 2
        if index >= 2:
            copies[index - 2].wait()
        held[slot] = lax.dot_general(left, right, DOWN, preferred_element_type=F32).astype(BF)
        copy = pltpu.make_async_copy(held.at[slot], out_ref.at[0, :, columns], sems.at[slot])
        copy.start()
        copies.append(copy)
    for copy in copies[-2:]:
        copy.wait()


def finish(peers, pieces, low_ref, high_ref, pick_ref, side_ref, raw_ref, *refs):
    in_refs, (hidden_ref, gate_ref, held, sems) = refs[:peers], refs[peers + 1 :]
    top_count = gate_ref.shape[0]
    routed, units = hidden_ref.shape
    quarter = units // 4
    total = jnp.zeros(gate_ref.shape, F32)
    sent = []
    for block in range(COLS):
        columns = slice(block * quarter, (block + 1) * quarter)
        back = stack(in_refs, columns).astype(F32)
        sent.append((side_ref[:, block : block + 1] * back).astype(BF))
        value = jnp.sum(raw_ref[:, columns].astype(F32) * back, axis=1, keepdims=True)
        chosen = side_ref[:, COLS + block : COLS + block + 1]
        weighted = pick_ref[block] * value
        lines = [
            jnp.sum(jnp.where(chosen == float(k), weighted, 0.0), axis=0, keepdims=True)
            for k in range(top_count)
        ]
        total = total + jnp.concatenate(lines, axis=0)
    stacked = jnp.concatenate(sent, axis=0)
    size = routed // pieces
    copies = []
    for piece in range(pieces):
        at = slice(piece * size, (piece + 1) * size)
        for block in range(COLS):
            held[at, block * quarter : (block + 1) * quarter] = jnp.dot(
                low_ref[at, :], sent[block], preferred_element_type=F32
            ).astype(BF)
        held[at, COLS * quarter :] = jnp.dot(
            high_ref[at, :], stacked, preferred_element_type=F32
        ).astype(BF)
        copy = pltpu.make_async_copy(held.at[at], hidden_ref.at[at], sems.at[piece])
        copy.start()
        copies.append(copy)
    gate_ref[...] = total
    for copy in copies:
        copy.wait()


def local(out_grad, hidden, routes, gates, w_down):
    tokens, top_count = routes.shape
    units = hidden.shape[2]
    width = out_grad.shape[1]
    half = w_down.shape[1]
    routed = tokens * top_count
    peers = lax.axis_size("expert")
    rows = peers * ROWS
    routes_t, gates_t = routes.T, gates.T
    shape = jax.ShapeDtypeStruct
    near = list(range(peers // 2))
    far = list(range(peers // 2, peers))
    batches = [near, far]
    order = far[:1] + near[1:] + far[1:]

    def across(array, step, back=False):
        pairs = [(i, partner(i, step, peers)) for i in range(peers)]
        return lax.ppermute(array, "expert", [(b, a) for a, b in pairs] if back else pairs)

    def swap(array):
        return lax.ppermute(array, "dp", [(0, 1), (1, 0)])

    w_other = swap(w_down)
    raw, *sent = pl.pallas_call(
        functools.partial(pack, peers),
        out_shape=[shape((rows, COLS * units // 4), BF)]
        + [shape((ROWS, COLS * (units + width) // 4), BF)] * peers,
        in_specs=[pl.BlockSpec(memory_space=pltpu.HBM)] * 4,
        out_specs=[vmem()] * (peers + 1),
        scratch_shapes=[
            pltpu.VMEM((top_count, tokens), jnp.int32),
            pltpu.VMEM((top_count, tokens), F32),
            pltpu.VMEM((tokens, width), BF),
            pltpu.VMEM((routed, units), BF),
            pltpu.SemaphoreType.DMA((4,)),
        ],
        compiler_params=params(58),
        name="pack",
        cost_estimate=FREE,
    )(routes_t, gates_t, out_grad, hidden.reshape(routed, units))
    received = {0: sent[0]}
    for step in order:
        received[step] = across(sent[step], step)
    low_map, high_map, pick_map, side = pl.pallas_call(
        functools.partial(maps, peers),
        out_shape=[
            shape((routed, rows), BF),
            shape((routed, COLS * rows), BF),
            shape((COLS, rows, tokens), F32),
            shape((rows, 128), F32),
        ],
        in_specs=[vmem()] * 2,
        out_specs=[vmem()] * 4,
        compiler_params=params(),
        name="maps",
        cost_estimate=FREE,
    )(routes_t, gates_t)
    keeps, owns, others, back = [], [], [], {}
    for batch in batches:
        count = len(batch)
        after = [pick_map] + [back[step] for step in back if step]
        own, keep, *out = pl.pallas_call(
            functools.partial(unit_grads, count, len(after)),
            out_shape=[
                shape((count * ROWS, width + half), BF),
                shape((count * ROWS, half), BF),
            ]
            + [shape((ROWS, COLS * units // 4), BF)] * count,
            in_specs=[vmem()] * (count + 2) + [anywhere()] * len(after),
            out_specs=[vmem()] * (count + 2),
            compiler_params=params(),
            name="unit_grads",
            cost_estimate=FREE,
        )(*[received[step] for step in batch], w_down, w_other, *after)
        for step, array in zip(batch, out):
            back[step] = array if step == 0 else across(array, step, True)
        keeps.append(keep)
        owns.append(own)
        others.append(swap(own))
    strip = 512 if width % 512 == 0 else width
    grad_down, done = pl.pallas_call(
        functools.partial(weight_grad, len(batches), strip),
        out_shape=[shape((1, half, width), BF), shape((8, 128), F32)],
        in_specs=[vmem()] * (3 * len(batches)),
        out_specs=[anywhere(), vmem()],
        scratch_shapes=[pltpu.VMEM((2, half, strip), BF), pltpu.SemaphoreType.DMA((2,))],
        compiler_params=params(),
        name="weight_grad",
    )(*keeps, *owns, *others)
    pieces = 4
    grad_hidden, grad_gates_t = pl.pallas_call(
        functools.partial(finish, peers, pieces),
        out_shape=[shape((routed, units), BF), shape((top_count, tokens), F32)],
        in_specs=[vmem()] * (peers + 5) + [anywhere()],
        out_specs=[anywhere(), vmem()],
        scratch_shapes=[pltpu.VMEM((routed, units), BF), pltpu.SemaphoreType.DMA((pieces,))],
        compiler_params=params(),
        name="finish",
    )(low_map, high_map, pick_map, side, raw, *[back[step] for step in range(peers)], done)
    return grad_down, grad_hidden.reshape(tokens, top_count, units), grad_gates_t.T


def solution(mesh):
    in_specs = (
        P(("groups", "expert", "dp"), None),
        P(("groups", "expert", "dp"), None, None),
        P(("groups", "expert", "dp"), None),
        P(("groups", "expert", "dp"), None),
        P("expert", "dp", None),
    )
    out_specs = (
        P(("groups", "expert"), "dp", None),
        P(("groups", "expert", "dp"), None, None),
        P(("groups", "expert", "dp"), None),
    )
    return jax.shard_map(local, mesh=mesh, in_specs=in_specs, out_specs=out_specs, check_vma=False)
```

time: 76.1 us -> 53.7 us (0.71)
  waiting for transfers between devices: 16.1 us -> 2.86 us
  starting transfers between devices: 39.1 us -> 28 us
  Pallas kernels: 14.1 us -> 17.4 us
  local copies, waits for them, and re-layouts: 5.74 us -> 4.31 us
    ppermute x21 -> x14, waiting for transfers between devices: 16.1 us -> 2.85 us  [across(): lax.ppermute(array, 'expert', [(b, a) for a, b in pairs] if back else pairs)]
    ppermute x21 -> x14, starting transfers between devices: 38.5 us -> 27.4 us  [across(): lax.ppermute(array, 'expert', [(b, a) for a, b in pairs] if back else pairs)]
    pallas_call x6, Pallas kernels: 14.1 us -> 17.4 us  [the longest x2 5.23 us: local(): pl.pallas_call(functools.partial(unit_grads, count, len(after)), out_shap...]
    unnamed x14 -> x12, local copies, waits for them, and re-layouts: 5.74 us -> 4.31 us
  transfers between devices with their start and end apart: 24 -> 17, of which waited for: 9 -> 4; matrix products, arithmetic and copies ran while one was open for 0% -> 0% of each run, Pallas kernels for 6% -> 28%
where the time goes in v2:
time: 53.7 us; the launch traced here: 53.4 us
  starting transfers between devices  28 us (52%)
  Pallas kernels  17.4 us (32%)
  local copies, waits for them, and re-layouts  4.31 us (8%)
  waiting for transfers between devices  2.86 us (5%)
  between operations  0.78 us (1%)
    ppermute x14, starting transfers between devices, across(): lax.ppermute(array, 'expert', [(b, a) for a, b in pairs] if back else pairs)  27.4 us
    pallas_call x2, Pallas kernels, local(): pl.pallas_call(functools.partial(unit_grads, count, len(after)), out_shap...  5.23 us
    pallas_call x1, Pallas kernels, local(): pl.pallas_call(functools.partial(weight_grad, len(batches), strip), out_s...  4.4 us
    unnamed x12, local copies, waits for them, and re-layouts  4.31 us
    pallas_call x1, Pallas kernels, local(): pl.pallas_call(functools.partial(pack, peers), out_shape=[shape((rows, CO...  4.27 us
    ppermute x14, waiting for transfers between devices, across(): lax.ppermute(array, 'expert', [(b, a) for a, b in pairs] if back else pairs)  2.85 us
    pallas_call x1, Pallas kernels, local(): pl.pallas_call(functools.partial(finish, peers, pieces), out_shape=[shape...  2.61 us
  transfers between devices with their start and end apart: 17, of which 4 were waited for; matrix products, arithmetic and copies ran while one was open for 0% of the time, Pallas kernels for 28%

profile of v2, /device:TPU:0, one launch (start us, length us, event | category | flops | bytes accessed | tf_op | source)
XLA Modules:
  0.0 53.4 jit_solution(13419125349004023662)
XLA Ops:
  0.6 0.5 collective-permute-start.3
  1.1 4.3 %pack.1 = (bf16[128,768]{1,0:T(8,128)(2,1)}, bf16[16,3456]{1,0:T(8,128)(2,1)}, bf16[16,3456]{1,0:T(8,128)(2,1)}, bf16[16,3456]{1,0:T(8,128)(2,1)}, bf16[16,3456]...) custom-call(s32[8,128]{1,0:T(8,128)} %bitcast.5, ...), custom_call_target="tpu_custom_call" | custom-call | tf_op jit(solution)/shard_map/pack/pallas_call | solution.py:331
  5.4 2.6 %collective-permute-start = (bf16[16,3456]{1,0:T(8,128)(2,1)}, bf16[16,3456]{1,0:T(8,128)(2,1)S(1)}, u32[]{:S(2)}, u32[]{:S(2)}) collective-permute-start(bf16[16,3456]{1,0:T(8,128)(2,1)} %get-tuple-element.33), channel_id=1, source_target_pairs={{0,2},{2,0},{4,6},{6,4},{8,10},{10,8},{12,14},{14,12},{1,3},{3,1},... | collective-permute-start | bytes 331784 | tf_op jit(solution)/shard_map/ppermute | solution.py:325
  8.0 1.6 %collective-permute-start.1 = (bf16[16,3456]{1,0:T(8,128)(2,1)}, bf16[16,3456]{1,0:T(8,128)(2,1)S(1)}, u32[]{:S(2)}, u32[]{:S(2)}) collective-permute-start(bf16[16,3456]{1,0:T(8,128)(2,1)} %get-tuple-element.34), channel_id=1, source_target_pairs={{0,4},{2,6},{4,0},{6,2},{8,12},{10,14},{12,8},{14,10},{1,5},{3,7},... | collective-permute-start | bytes 331784 | tf_op jit(solution)/shard_map/ppermute | solution.py:325
  9.6 0.0 collective-permute-start.2
  9.6 3.0 %collective-permute-start.4 = (bf16[16,3456]{1,0:T(8,128)(2,1)}, bf16[16,3456]{1,0:T(8,128)(2,1)S(1)}, u32[]{:S(2)}, u32[]{:S(2)}) collective-permute-start(bf16[16,3456]{1,0:T(8,128)(2,1)} %get-tuple-element.38), channel_id=1, source_target_pairs={{0,8},{2,10},{4,12},{6,14},{8,0},{10,2},{12,4},{14,6},{1,9},{3,11}... | collective-permute-start | bytes 331784 | tf_op jit(solution)/shard_map/ppermute | solution.py:325
  12.6 0.0 collective-permute-done.refs_1_
  12.6 3.1 %collective-permute-start.5 = (bf16[16,3456]{1,0:T(8,128)(2,1)}, bf16[16,3456]{1,0:T(8,128)(2,1)S(1)}, u32[]{:S(2)}, u32[]{:S(2)}) collective-permute-start(bf16[16,3456]{1,0:T(8,128)(2,1)} %get-tuple-element.39), channel_id=1, source_target_pairs={{0,10},{2,8},{4,14},{6,12},{8,2},{10,0},{12,6},{14,4},{1,11},{3,9}... | collective-permute-start | bytes 331784 | tf_op jit(solution)/shard_map/ppermute | solution.py:325
  15.7 0.8 %collective-permute-done.1.refs_2_ = bf16[16,3456]{1,0:T(8,128)(2,1)S(1)} collective-permute-done((bf16[16,3456]{1,0:T(8,128)(2,1)}, bf16[16,3456]{1,0:T(8,128)(2,1)S(1)}, u32[]{:S(2)}, u32[]{:S(2)}) %collective-permute-start.1) | collective-permute-done | bytes 110624 | tf_op jit(solution)/shard_map/ppermute | solution.py:325
  16.5 3.2 %collective-permute-start.6 = (bf16[16,3456]{1,0:T(8,128)(2,1)}, bf16[16,3456]{1,0:T(8,128)(2,1)S(1)}, u32[]{:S(2)}, u32[]{:S(2)}) collective-permute-start(bf16[16,3456]{1,0:T(8,128)(2,1)} %get-tuple-element.40), channel_id=1, source_target_pairs={{0,12},{2,14},{4,8},{6,10},{8,4},{10,6},{12,0},{14,2},{1,13},{3,15... | collective-permute-start | bytes 331784 | tf_op jit(solution)/shard_map/ppermute | solution.py:325
  19.7 0.0 collective-permute-done.2.refs_3_
  19.7 2.7 %collective-permute-start.7 = (bf16[16,3456]{1,0:T(8,128)(2,1)}, bf16[16,3456]{1,0:T(8,128)(2,1)S(1)}, u32[]{:S(2)}, u32[]{:S(2)}) collective-permute-start(bf16[16,3456]{1,0:T(8,128)(2,1)} %get-tuple-element.41), channel_id=1, source_target_pairs={{0,14},{2,12},{4,10},{6,8},{8,6},{10,4},{12,2},{14,0},{1,15},{3,13... | collective-permute-start | bytes 331784 | tf_op jit(solution)/shard_map/ppermute | solution.py:325
  22.4 0.0 copy-start.4
  22.4 0.7 %copy-done.4 = s32[128,8]{0,1:T(8,128)S(1)} copy-done((s32[128,8]{0,1:T(8,128)S(1)}, s32[128,8]{0,1:T(8,128)}, u32[]{:S(2)}) %copy-start.4) | copy-done | bytes 4120
  23.1 0.7 %copy-done.5 = f32[128,8]{0,1:T(8,128)S(1)} copy-done((f32[128,8]{0,1:T(8,128)S(1)}, f32[128,8]{0,1:T(8,128)}, u32[]{:S(2)}) %copy-start.5) | copy-done | bytes 4120
  23.8 0.9 %maps.1 = (bf16[1024,128]{1,0:T(8,128)(2,1)S(1)}, bf16[1024,384]{1,0:T(8,128)(2,1)S(1)}, f32[3,128,128]{2,1,0:T(8,128)S(1)}, f32[128,128]{1,0:T(8,128)S(1)}) custom-call(s32[8,128]{1,0:T(8,128)S(1)} %bitcast.6, f32[8,128]{1,0:T(8,128)S(1)} %bitcast.8), custom_call_target="tpu_custom_call" | custom-call | tf_op jit(solution)/shard_map/maps/pallas_call | solution.py:351
  24.7 0.0 collective-permute-done.3.refs_5_
  24.7 0.0 copy-start
  24.7 2.0 %copy-done = bf16[1,512,3584]{2,1,0:T(8,128)(2,1)S(1)} copy-done((bf16[1,512,3584]{2,1,0:T(8,128)(2,1)S(1)}, bf16[1,512,3584]{2,1,0:T(8,128)(2,1)}, u32[]{:S(2)}) %copy-start) | copy-done | bytes 3670040
  26.8 0.9 %copy-done.3 = bf16[16,3456]{1,0:T(8,128)(2,1)S(1)} copy-done((bf16[16,3456]{1,0:T(8,128)(2,1)S(1)}, bf16[16,3456]{1,0:T(8,128)(2,1)}, u32[]{:S(2)}) %copy-start.3) | copy-done | bytes 110616
  27.7 2.6 %unit_grads.2 = (bf16[64,4096]{1,0:T(8,128)(2,1)S(1)}, bf16[64,512]{1,0:T(8,128)(2,1)S(1)}, bf16[16,768]{1,0:T(8,128)(2,1)S(1)}, bf16[16,768]{1,0:T(8,128)(2,1)S...) custom-call(bf16[16,3456]{1,0:T(8,128)(2,1)S(1)} %copy-done.3, ...), custom_call_target="tpu_custom_call" | custom-call | tf_op jit(solution)/shard_map/unit_grads/pallas_call | solution.py:369
  30.3 0.1 collective-permute-start.8
  30.4 0.0 collective-permute-done.4.refs_0_
  30.4 0.1 collective-permute-start.9
  30.5 0.0 collective-permute-done.5.refs_1_
  30.5 3.4 %collective-permute-start.10 = (bf16[16,768]{1,0:T(8,128)(2,1)S(1)}, bf16[16,768]{1,0:T(8,128)(2,1)S(1)}, u32[]{:S(2)}, u32[]{:S(2)}) collective-permute-start(bf16[16,768]{1,0:T(8,128)(2,1)S(1)} %get-tuple-element.44), channel_id=1, source_target_pairs={{6,0},{4,2},{2,4},{0,6},{14,8},{12,10},{10,12},{8,14},{7,1},{5,3},... | collective-permute-start | bytes 73736 | tf_op jit(solution)/shard_map/ppermute | solution.py:325
  33.9 0.0 collective-permute-done.6.refs_2_
  33.9 0.0 collective-permute-start.11
  33.9 0.0 collective-permute-done.7.refs_3_
  33.9 0.3 collective-permute-done.8.refs_7_.refs_1_
  34.2 0.1 collective-permute-done.9.refs_8_.refs_2_
  34.3 1.6 %collective-permute-done.10.refs_9_.refs_3_ = bf16[16,768]{1,0:T(8,128)(2,1)S(1)} collective-permute-done((bf16[16,768]{1,0:T(8,128)(2,1)S(1)}, bf16[16,768]{1,0:T(8,128)(2,1)S(1)}, u32[]{:S(2)}, u32[]{:S(2)}) %collective-permute-start.10) | collective-permute-done | bytes 24608 | tf_op jit(solution)/shard_map/ppermute | solution.py:325
  35.9 0.0 copy-done.1
  35.9 2.6 %unit_grads.3 = (bf16[64,4096]{1,0:T(8,128)(2,1)S(1)}, bf16[64,512]{1,0:T(8,128)(2,1)S(1)}, bf16[16,768]{1,0:T(8,128)(2,1)S(1)}, bf16[16,768]{1,0:T(8,128)(2,1)S...) custom-call(bf16[16,3456]{1,0:T(8,128)(2,1)S(1)} %collective-permute-done.4.refs_0_, ...), custom_call_target="tpu_custom_call" | custom-call | tf_op jit(solution)/shard_map/unit_grads/pallas_call | solution.py:369
  38.5 0.1 collective-permute-start.12
  38.6 2.4 %collective-permute-start.13 = (bf16[16,768]{1,0:T(8,128)(2,1)S(1)}, bf16[16,768]{1,0:T(8,128)(2,1)S(1)}, u32[]{:S(2)}, u32[]{:S(2)}) collective-permute-start(bf16[16,768]{1,0:T(8,128)(2,1)S(1)} %get-tuple-element.54), channel_id=1, source_target_pairs={{8,0},{10,2},{12,4},{14,6},{0,8},{2,10},{4,12},{6,14},{9,1},{11,3}... | collective-permute-start | bytes 73736 | tf_op jit(solution)/shard_map/ppermute | solution.py:325
  41.0 1.3 %collective-permute-start.14 = (bf16[16,768]{1,0:T(8,128)(2,1)S(1)}, bf16[16,768]{1,0:T(8,128)(2,1)S(1)}, u32[]{:S(2)}, u32[]{:S(2)}) collective-permute-start(bf16[16,768]{1,0:T(8,128)(2,1)S(1)} %get-tuple-element.55), channel_id=1, source_target_pairs={{10,0},{8,2},{14,4},{12,6},{2,8},{0,10},{6,12},{4,14},{11,1},{9,3}... | collective-permute-start | bytes 73736 | tf_op jit(solution)/shard_map/ppermute | solution.py:325
  42.3 1.7 %collective-permute-start.15 = (bf16[16,768]{1,0:T(8,128)(2,1)S(1)}, bf16[16,768]{1,0:T(8,128)(2,1)S(1)}, u32[]{:S(2)}, u32[]{:S(2)}) collective-permute-start(bf16[16,768]{1,0:T(8,128)(2,1)S(1)} %get-tuple-element.56), channel_id=1, source_target_pairs={{12,0},{14,2},{8,4},{10,6},{4,8},{6,10},{0,12},{2,14},{13,1},{15,3... | collective-permute-start | bytes 73736 | tf_op jit(solution)/shard_map/ppermute | solution.py:325
  44.0 0.0 collective-permute-done.11.refs_4_
  44.0 2.3 %collective-permute-start.16 = (bf16[16,768]{1,0:T(8,128)(2,1)S(1)}, bf16[16,768]{1,0:T(8,128)(2,1)S(1)}, u32[]{:S(2)}, u32[]{:S(2)}) collective-permute-start(bf16[16,768]{1,0:T(8,128)(2,1)S(1)} %get-tuple-element.57), channel_id=1, source_target_pairs={{14,0},{12,2},{10,4},{8,6},{6,8},{4,10},{2,12},{0,14},{15,1},{13,3... | collective-permute-start | bytes 73736 | tf_op jit(solution)/shard_map/ppermute | solution.py:325
  46.3 0.0 collective-permute-done.12.refs_5_
  46.3 4.4 %weight_grad.1 = (bf16[1,512,3584]{2,1,0:T(8,128)(2,1)}, f32[8,128]{1,0:T(8,128)S(1)}) custom-call(bf16[64,512]{1,0:T(8,128)(2,1)S(1)} %get-tuple-element.37.refs_0_, bf16[64,512]{1,0:T(8,128)(2,1)S(1)} %get-tuple-element.45.refs_1_, bf16[64,4096]{1,0:T(8,128)(2,1)S(1)} %get-tuple-element.46.refs_2_, bf16[64,4096]{1,0:T(8,128)(2,1)S(1)} %get-tuple-element.47.refs_3_, ...), custom_call_target="tpu_custom_call" | custom-call | tf_op jit(solution)/shard_map/weight_grad/pallas_call | solution.py:388
  50.8 0.0 collective-permute-done.13.refs_4_
  50.8 0.0 collective-permute-done.14.refs_5_
  50.8 0.0 collective-permute-done.15.refs_6_
  50.8 0.0 collective-permute-done.16.refs_7_
  50.8 0.0 copy-done.2
  50.8 2.6 %finish.1 = (bf16[1024,1024]{1,0:T(8,128)(2,1)}, f32[8,128]{1,0:T(8,128)}) custom-call(bf16[1024,128]{1,0:T(8,128)(2,1)S(1)} %get-tuple-element.49.low_ref, bf16[1024,384]{1,0:T(8,128)(2,1)S(1)} %get-tuple-element.50.high_ref, f32[3,128,128]{2,1,0:T(8,128)S(1)} %get-tuple-element.36.refs_6_.pick_ref, f32[128,128]{1,0:T(8,128)S(1)} %get-tuple-element.51.side_ref, ...), custom_call_target="tpu_custom_call" | custom-call | tf_op jit(solution)/shard_map/finish/pallas_call | solution.py:398
  (4 shorter events, 0.0 us)
Async XLA Ops:
  0.6 24.1 %collective-permute-start.3 = (bf16[1,512,3584]{2,1,0:T(8,128)(2,1)}, bf16[1,512,3584]{2,1,0:T(8,128)(2,1)S(1)}, u32[]{:S(2)}, u32[]{:S(2)}) collective-permute-start(bf16[1,512,3584]{2,1,0:T(8,128)(2,1)} %refs_4_.3), channel_id=1, source_target_pairs={{0,1},{1,0},{2,3},{3,2},{4,5},{5,4},{6,7},{7,6},{8,9},{9,8},{10,11... | collective-permute-start | bytes 11010056 | tf_op jit(solution)/shard_map/ppermute | solution.py:328
  5.4 7.2 %collective-permute-start = (bf16[16,3456]{1,0:T(8,128)(2,1)}, bf16[16,3456]{1,0:T(8,128)(2,1)S(1)}, u32[]{:S(2)}, u32[]{:S(2)}) collective-permute-start(bf16[16,3456]{1,0:T(8,128)(2,1)} %get-tuple-element.33), channel_id=1, source_target_pairs={{0,2},{2,0},{4,6},{6,4},{8,10},{10,8},{12,14},{14,12},{1,3},{3,1},... | collective-permute-start | bytes 331784 | tf_op jit(solution)/shard_map/ppermute | solution.py:325
  8.0 8.5 %collective-permute-start.1 = (bf16[16,3456]{1,0:T(8,128)(2,1)}, bf16[16,3456]{1,0:T(8,128)(2,1)S(1)}, u32[]{:S(2)}, u32[]{:S(2)}) collective-permute-start(bf16[16,3456]{1,0:T(8,128)(2,1)} %get-tuple-element.34), channel_id=1, source_target_pairs={{0,4},{2,6},{4,0},{6,2},{8,12},{10,14},{12,8},{14,10},{1,5},{3,7},... | collective-permute-start | bytes 331784 | tf_op jit(solution)/shard_map/ppermute | solution.py:325
  9.6 10.1 %collective-permute-start.2 = (bf16[16,3456]{1,0:T(8,128)(2,1)}, bf16[16,3456]{1,0:T(8,128)(2,1)S(1)}, u32[]{:S(2)}, u32[]{:S(2)}) collective-permute-start(bf16[16,3456]{1,0:T(8,128)(2,1)} %get-tuple-element.35), channel_id=1, source_target_pairs={{0,6},{2,4},{4,2},{6,0},{8,14},{10,12},{12,10},{14,8},{1,7},{3,5},... | collective-permute-start | bytes 331784 | tf_op jit(solution)/shard_map/ppermute | solution.py:325
  9.6 20.8 %collective-permute-start.4 = (bf16[16,3456]{1,0:T(8,128)(2,1)}, bf16[16,3456]{1,0:T(8,128)(2,1)S(1)}, u32[]{:S(2)}, u32[]{:S(2)}) collective-permute-start(bf16[16,3456]{1,0:T(8,128)(2,1)} %get-tuple-element.38), channel_id=1, source_target_pairs={{0,8},{2,10},{4,12},{6,14},{8,0},{10,2},{12,4},{14,6},{1,9},{3,11}... | collective-permute-start | bytes 331784 | tf_op jit(solution)/shard_map/ppermute | solution.py:325
  12.6 17.9 %collective-permute-start.5 = (bf16[16,3456]{1,0:T(8,128)(2,1)}, bf16[16,3456]{1,0:T(8,128)(2,1)S(1)}, u32[]{:S(2)}, u32[]{:S(2)}) collective-permute-start(bf16[16,3456]{1,0:T(8,128)(2,1)} %get-tuple-element.39), channel_id=1, source_target_pairs={{0,10},{2,8},{4,14},{6,12},{8,2},{10,0},{12,6},{14,4},{1,11},{3,9}... | collective-permute-start | bytes 331784 | tf_op jit(solution)/shard_map/ppermute | solution.py:325
  16.5 17.4 %collective-permute-start.6 = (bf16[16,3456]{1,0:T(8,128)(2,1)}, bf16[16,3456]{1,0:T(8,128)(2,1)S(1)}, u32[]{:S(2)}, u32[]{:S(2)}) collective-permute-start(bf16[16,3456]{1,0:T(8,128)(2,1)} %get-tuple-element.40), channel_id=1, source_target_pairs={{0,12},{2,14},{4,8},{6,10},{8,4},{10,6},{12,0},{14,2},{1,13},{3,15... | collective-permute-start | bytes 331784 | tf_op jit(solution)/shard_map/ppermute | solution.py:325
  19.7 14.2 %collective-permute-start.7 = (bf16[16,3456]{1,0:T(8,128)(2,1)}, bf16[16,3456]{1,0:T(8,128)(2,1)S(1)}, u32[]{:S(2)}, u32[]{:S(2)}) collective-permute-start(bf16[16,3456]{1,0:T(8,128)(2,1)} %get-tuple-element.41), channel_id=1, source_target_pairs={{0,14},{2,12},{4,10},{6,8},{8,6},{10,4},{12,2},{14,0},{1,15},{3,13... | collective-permute-start | bytes 331784 | tf_op jit(solution)/shard_map/ppermute | solution.py:325
  22.4 0.7 %copy-start.4 = (s32[128,8]{0,1:T(8,128)S(1)}, s32[128,8]{0,1:T(8,128)}, u32[]{:S(2)}) copy-start(s32[128,8]{0,1:T(8,128)} %param.7) | copy-start | bytes 12292
  23.1 0.7 %copy-start.5 = (f32[128,8]{0,1:T(8,128)S(1)}, f32[128,8]{0,1:T(8,128)}, u32[]{:S(2)}) copy-start(f32[128,8]{0,1:T(8,128)} %param.8) | copy-start | bytes 12292
  24.7 2.0 %copy-start = (bf16[1,512,3584]{2,1,0:T(8,128)(2,1)S(1)}, bf16[1,512,3584]{2,1,0:T(8,128)(2,1)}, u32[]{:S(2)}) copy-start(bf16[1,512,3584]{2,1,0:T(8,128)(2,1)} %refs_4_.3) | copy-start | bytes 11010052
  26.8 0.9 %copy-start.3 = (bf16[16,3456]{1,0:T(8,128)(2,1)S(1)}, bf16[16,3456]{1,0:T(8,128)(2,1)}, u32[]{:S(2)}) copy-start(bf16[16,3456]{1,0:T(8,128)(2,1)} %get-tuple-element.32.refs_0_) | copy-start | bytes 331780
  27.7 8.2 %copy-start.1 = (bf16[1,512,3584]{2,1,0:T(8,128)(2,1)S(1)}, bf16[1,512,3584]{2,1,0:T(8,128)(2,1)}, u32[]{:S(2)}) copy-start(bf16[1,512,3584]{2,1,0:T(8,128)(2,1)} %refs_4_.3) | copy-start | bytes 11010052
  30.3 3.9 %collective-permute-start.8 = (bf16[16,768]{1,0:T(8,128)(2,1)S(1)}, bf16[16,768]{1,0:T(8,128)(2,1)S(1)}, u32[]{:S(2)}, u32[]{:S(2)}) collective-permute-start(bf16[16,768]{1,0:T(8,128)(2,1)S(1)} %get-tuple-element.42), channel_id=1, source_target_pairs={{2,0},{0,2},{6,4},{4,6},{10,8},{8,10},{14,12},{12,14},{3,1},{1,3},... | collective-permute-start | bytes 73736 | tf_op jit(solution)/shard_map/ppermute | solution.py:325
  30.4 3.9 %collective-permute-start.9 = (bf16[16,768]{1,0:T(8,128)(2,1)S(1)}, bf16[16,768]{1,0:T(8,128)(2,1)S(1)}, u32[]{:S(2)}, u32[]{:S(2)}) collective-permute-start(bf16[16,768]{1,0:T(8,128)(2,1)S(1)} %get-tuple-element.43), channel_id=1, source_target_pairs={{4,0},{6,2},{0,4},{2,6},{12,8},{14,10},{8,12},{10,14},{5,1},{7,3},... | collective-permute-start | bytes 73736 | tf_op jit(solution)/shard_map/ppermute | solution.py:325
  30.5 5.4 %collective-permute-start.10 = (bf16[16,768]{1,0:T(8,128)(2,1)S(1)}, bf16[16,768]{1,0:T(8,128)(2,1)S(1)}, u32[]{:S(2)}, u32[]{:S(2)}) collective-permute-start(bf16[16,768]{1,0:T(8,128)(2,1)S(1)} %get-tuple-element.44), channel_id=1, source_target_pairs={{6,0},{4,2},{2,4},{0,6},{14,8},{12,10},{10,12},{8,14},{7,1},{5,3},... | collective-permute-start | bytes 73736 | tf_op jit(solution)/shard_map/ppermute | solution.py:325
  33.9 16.9 %copy-start.2 = (bf16[128,768]{1,0:T(8,128)(2,1)S(1)}, bf16[128,768]{1,0:T(8,128)(2,1)}, u32[]{:S(2)}) copy-start(bf16[128,768]{1,0:T(8,128)(2,1)} %get-tuple-element.52.raw_ref) | copy-start | bytes 589828
  33.9 10.2 %collective-permute-start.11 = (bf16[64,4096]{1,0:T(8,128)(2,1)S(1)}, bf16[64,4096]{1,0:T(8,128)(2,1)S(1)}, u32[]{:S(2)}, u32[]{:S(2)}) collective-permute-start(bf16[64,4096]{1,0:T(8,128)(2,1)S(1)} %get-tuple-element.46.refs_2_), channel_id=1, source_target_pairs={{0,1},{1,0},{2,3},{3,2},{4,5},{5,4},{6,7},{7,6},{8,9},{9,8},{10,11... | collective-permute-start | bytes 1572872 | tf_op jit(solution)/shard_map/ppermute | solution.py:328
  38.5 7.8 %collective-permute-start.12 = (bf16[64,4096]{1,0:T(8,128)(2,1)S(1)}, bf16[64,4096]{1,0:T(8,128)(2,1)S(1)}, u32[]{:S(2)}, u32[]{:S(2)}) collective-permute-start(bf16[64,4096]{1,0:T(8,128)(2,1)S(1)} %get-tuple-element.47.refs_3_), channel_id=1, source_target_pairs={{0,1},{1,0},{2,3},{3,2},{4,5},{5,4},{6,7},{7,6},{8,9},{9,8},{10,11... | collective-permute-start | bytes 1572872 | tf_op jit(solution)/shard_map/ppermute | solution.py:328
  38.6 12.1 %collective-permute-start.13 = (bf16[16,768]{1,0:T(8,128)(2,1)S(1)}, bf16[16,768]{1,0:T(8,128)(2,1)S(1)}, u32[]{:S(2)}, u32[]{:S(2)}) collective-permute-start(bf16[16,768]{1,0:T(8,128)(2,1)S(1)} %get-tuple-element.54), channel_id=1, source_target_pairs={{8,0},{10,2},{12,4},{14,6},{0,8},{2,10},{4,12},{6,14},{9,1},{11,3}... | collective-permute-start | bytes 73736 | tf_op jit(solution)/shard_map/ppermute | solution.py:325
  41.0 9.8 %collective-permute-start.14 = (bf16[16,768]{1,0:T(8,128)(2,1)S(1)}, bf16[16,768]{1,0:T(8,128)(2,1)S(1)}, u32[]{:S(2)}, u32[]{:S(2)}) collective-permute-start(bf16[16,768]{1,0:T(8,128)(2,1)S(1)} %get-tuple-element.55), channel_id=1, source_target_pairs={{10,0},{8,2},{14,4},{12,6},{2,8},{0,10},{6,12},{4,14},{11,1},{9,3}... | collective-permute-start | bytes 73736 | tf_op jit(solution)/shard_map/ppermute | solution.py:325
  42.3 8.5 %collective-permute-start.15 = (bf16[16,768]{1,0:T(8,128)(2,1)S(1)}, bf16[16,768]{1,0:T(8,128)(2,1)S(1)}, u32[]{:S(2)}, u32[]{:S(2)}) collective-permute-start(bf16[16,768]{1,0:T(8,128)(2,1)S(1)} %get-tuple-element.56), channel_id=1, source_target_pairs={{12,0},{14,2},{8,4},{10,6},{4,8},{6,10},{0,12},{2,14},{13,1},{15,3... | collective-permute-start | bytes 73736 | tf_op jit(solution)/shard_map/ppermute | solution.py:325
  44.0 6.7 %collective-permute-start.16 = (bf16[16,768]{1,0:T(8,128)(2,1)S(1)}, bf16[16,768]{1,0:T(8,128)(2,1)S(1)}, u32[]{:S(2)}, u32[]{:S(2)}) collective-permute-start(bf16[16,768]{1,0:T(8,128)(2,1)S(1)} %get-tuple-element.57), channel_id=1, source_target_pairs={{14,0},{12,2},{10,4},{8,6},{6,8},{4,10},{2,12},{0,14},{15,1},{13,3... | collective-permute-start | bytes 73736 | tf_op jit(solution)/shard_map/ppermute | solution.py:325

commit v3 on v2

v3 whole, which is shorter than its diff:
```python
import functools

import jax
import jax.numpy as jnp
from jax import lax
from jax.experimental import pallas as pl
from jax.experimental.pallas import tpu as pltpu
from jax.sharding import PartitionSpec as P

MOST = 12
ROWS = 16
COLS = 3
EXTRA = ROWS - MOST
BF = jnp.bfloat16
F32 = jnp.float32
MIB = 1 << 20
DOWN = (((0,), (0,)), ((), ()))


FREE = pl.CostEstimate(flops=0, bytes_accessed=0, transcendentals=0)


def params(mib=20, **kw):
    return pltpu.CompilerParams(vmem_limit_bytes=mib * MIB, **kw)


def vmem():
    return pl.BlockSpec(memory_space=pltpu.VMEM)


def anywhere():
    return pl.BlockSpec(memory_space=pl.ANY)


def partner(index, step, peers):
    if peers & (peers - 1) == 0:
        return index ^ step
    return lax.rem(index + step, peers) if isinstance(index, jax.Array) else (index + step) % peers


def routing(routes_t, peers, steps):
    me = lax.axis_index("expert")
    tokens = routes_t.shape[1]
    hits = [routes_t == partner(me, step, peers) for step in steps]
    member = jnp.concatenate(
        [jnp.max(hit.astype(F32), axis=0, keepdims=True) for hit in hits], axis=0
    )
    earlier = lax.broadcasted_iota(jnp.int32, (tokens, tokens), 0) < lax.broadcasted_iota(
        jnp.int32, (tokens, tokens), 1
    )
    before = jnp.dot(member.astype(BF), earlier.astype(F32).astype(BF), preferred_element_type=F32)
    return hits, jnp.where(member > 0, before, -1.0)


def picks(place, block):
    tokens = place.shape[1]
    row = lax.broadcasted_iota(jnp.int32, (ROWS, tokens), 0)
    wanted = jnp.where(row < MOST, row, row - MOST + EXTRA * block).astype(F32)
    return jnp.concatenate(
        [(place[step : step + 1, :] == wanted).astype(F32) for step in range(place.shape[0])], axis=0
    )


def low_rows(rows, width):
    return lax.broadcasted_iota(jnp.int32, (rows, width), 0) % ROWS < MOST


def gate_of(hits, gates_t):
    return jnp.concatenate(
        [jnp.sum(jnp.where(hit, gates_t, 0.0), axis=0, keepdims=True) for hit in hits], axis=0
    )


def choice_of(hits):
    return jnp.concatenate(
        [
            jnp.sum(
                jnp.where(hit, lax.broadcasted_iota(jnp.int32, hit.shape, 0).astype(F32), 0.0),
                axis=0,
                keepdims=True,
            )
            for hit in hits
        ],
        axis=0,
    )


def spread(table, pick):
    return jnp.concatenate(
        [
            jnp.sum(
                pick[step * ROWS : (step + 1) * ROWS, :] * table[step : step + 1, :],
                axis=1,
                keepdims=True,
            )
            for step in range(table.shape[0])
        ],
        axis=0,
    )


def route_picks(pick, choice, top_count):
    tokens = pick.shape[1]
    routed = tokens * top_count
    token = lax.broadcasted_iota(jnp.int32, (tokens, routed), 0)
    column = lax.broadcasted_iota(jnp.int32, (tokens, routed), 1)
    wide = (column // top_count == token).astype(F32).astype(BF)
    mine = jnp.dot(pick.astype(BF), wide, preferred_element_type=F32)
    which = (lax.broadcasted_iota(jnp.int32, (pick.shape[0], routed), 1) % top_count).astype(F32)
    return jnp.where(which == choice, mine, 0.0)


def pack(peers, steps, extra, *refs):
    sources, refs, count = refs[:4], refs[4 + extra :], len(steps)
    raw_ref, out_refs, held, sems = refs[0], refs[1 : 1 + count], refs[1 + count : -1], refs[-1]
    copies = [
        pltpu.make_async_copy(source, target, sems.at[index])
        for index, (source, target) in enumerate(zip(sources, held))
    ]
    for copy in copies:
        copy.start()
    for copy in copies[:3]:
        copy.wait()
    routes_ref, gates_ref, grad_ref, hidden_ref = held
    hits, place = routing(routes_ref[...], peers, steps)
    gate = gate_of(hits, gates_ref[...])
    choice = choice_of(hits)
    tokens = grad_ref.shape[0]
    wide, quarter = grad_ref.shape[1] // 4, hidden_ref.shape[1] // 4
    low = low_rows(count * ROWS, tokens)
    low_units = low_rows(count * ROWS, quarter)
    last = grad_ref[:, COLS * wide :]
    taken = []
    for block in range(COLS):
        pick = picks(place, block)
        both = jnp.concatenate(
            [jnp.where(low, pick, 0.0).astype(BF), jnp.where(low, 0.0, pick).astype(BF)], axis=1
        )
        columns = slice(block * wide, (block + 1) * wide)
        source = jnp.concatenate([grad_ref[:, columns], last], axis=0)
        packed = jnp.dot(both, source, preferred_element_type=F32).astype(BF)
        for step in range(count):
            out_refs[step][:, columns] = packed[step * ROWS : (step + 1) * ROWS, :]
        take = route_picks(pick, spread(choice, pick), routes_ref.shape[0]).astype(BF)
        taken.append((take, spread(gate, pick)))
    copies[3].wait()
    rows = count * ROWS
    first = jnp.dot(taken[0][0], hidden_ref[:, : COLS * quarter], preferred_element_type=F32)
    rest = jnp.dot(
        jnp.concatenate([take for take, _ in taken], axis=0),
        hidden_ref[:, COLS * quarter :],
        preferred_element_type=F32,
    )
    for block, (_, weight) in enumerate(taken):
        columns = slice(block * quarter, (block + 1) * quarter)
        raw = jnp.where(low_units, first[:, columns], rest[block * rows : (block + 1) * rows, :])
        raw_ref[:, columns] = raw.astype(BF)
        scaled = (weight * raw).astype(BF)
        columns = slice(COLS * wide + block * quarter, COLS * wide + (block + 1) * quarter)
        for step in range(count):
            out_refs[step][:, columns] = scaled[step * ROWS : (step + 1) * ROWS, :]


def maps(peers, routes_ref, gates_ref, weight_ref, low_ref, pick_ref, side_ref):
    hits, place = routing(routes_ref[...], peers, range(peers))
    gate, choice = gate_of(hits, gates_ref[...]), choice_of(hits)
    low = low_rows(peers * ROWS, low_ref.shape[0])
    side_ref[...] = jnp.zeros_like(side_ref)
    for block in range(COLS):
        pick = picks(place, block)
        chosen = spread(choice, pick)
        if block == 0:
            take = route_picks(pick, chosen, routes_ref.shape[0])
            low_ref[...] = jnp.where(low, take, 0.0).T.astype(BF)
        pick_ref[block] = pick
        side_ref[:, block : block + 1] = spread(gate, pick)
        side_ref[:, COLS + block : COLS + block + 1] = chosen


def last_quarter(peers, block):
    rows = peers * ROWS
    to = lax.broadcasted_iota(jnp.int32, (rows, rows), 0)
    at = lax.broadcasted_iota(jnp.int32, (rows, rows), 1)
    inside = at % ROWS
    wanted = at - MOST + EXTRA * block
    return ((inside >= MOST) & (to == wanted)).astype(F32).astype(BF)


def block_of(step, peers):
    return pl.ds(pl.multiple_of(partner(lax.axis_index("expert"), step, peers) * ROWS, ROWS), ROWS)


def stack(refs, columns):
    return jnp.concatenate([ref[:, columns] for ref in refs], axis=0)


def unpack_last(peers, parts):
    moves = jnp.concatenate([last_quarter(peers, block) for block in range(COLS)], axis=1)
    return jnp.dot(moves, jnp.concatenate(parts, axis=0), preferred_element_type=F32).astype(BF)


def unit_grads(steps, peers, *refs):
    count, base, extra = len(steps), 0, 1
    in_refs, own_ref, other_ref = refs[:count], refs[count], refs[count + 1]
    refs = refs[count + 2 + extra :]
    here = slice(base * ROWS, (base + count) * ROWS)
    swap_ref, keep_ref = refs[0].at[here], refs[1].at[here]
    out_refs = refs[2:]
    half_units, width = own_ref.shape[1], own_ref.shape[2]
    quarter, wide = half_units // 2, width // 4
    rows = count * ROWS
    first_core = lax.axis_index("dp") == 0
    parts = []
    for block in range(COLS):
        part = stack(in_refs, slice(block * wide, (block + 1) * wide))
        swap_ref[:, block * wide : (block + 1) * wide] = part
        parts.append(part)
    swap_ref[:, COLS * wide : 4 * wide] = unpack_last(count, parts)
    left = swap_ref[:, : 4 * wide]
    across = (((1,), (1,)), ((), ()))
    halves = [
        lax.dot_general(left, ref[0], across, preferred_element_type=F32)
        for ref in (own_ref, other_ref)
    ]
    low_half = jnp.where(first_core, halves[0], halves[1])
    high_half = jnp.where(first_core, halves[1], halves[0])
    units = [low_half[:, :quarter], low_half[:, quarter:], high_half[:, :quarter]]
    last = high_half[:, quarter:].astype(BF)
    low = low_rows(rows, quarter)
    for block in range(COLS):
        moved = lax.dot_general(
            last_quarter(count, block), last, DOWN, preferred_element_type=F32
        )
        packed = jnp.where(low, units[block], moved).astype(BF)
        for index, step in enumerate(steps):
            out_refs[0][block_of(step, peers), block * quarter : (block + 1) * quarter] = packed[
                index * ROWS : (index + 1) * ROWS, :
            ]
    start = COLS * wide
    parts = [
        stack(in_refs, slice(start + b * quarter, start + (b + 1) * quarter)) for b in range(COLS)
    ]
    scaled = [jnp.where(low, part.astype(F32), 0.0) for part in parts]
    scaled.append(unpack_last(count, parts).astype(F32))
    for place in range(2):
        one, two = scaled[place], scaled[place + 2]
        keep_ref[:, place * quarter : (place + 1) * quarter] = jnp.where(
            first_core, one, two
        ).astype(BF)
        swap_ref[:, width + place * quarter : width + (place + 1) * quarter] = jnp.where(
            first_core, two, one
        ).astype(BF)


def weight_grad(strip, keep_ref, own_ref, other_ref, out_ref, done_ref, held, sems):
    done_ref[...] = jnp.zeros_like(done_ref)
    width = out_ref.shape[2]
    half = out_ref.shape[1]
    left = jnp.concatenate([keep_ref[...], other_ref[:, width : width + half]], axis=0).T
    copies = []
    for index in range(width // strip):
        columns = slice(index * strip, (index + 1) * strip)
        right = jnp.concatenate([own_ref[:, columns], other_ref[:, columns]], axis=0)
        held[index] = jnp.dot(left, right, preferred_element_type=F32).astype(BF)
        copy = pltpu.make_async_copy(held.at[index], out_ref.at[0, :, columns], sems.at[index])
        copy.start()
        copies.append(copy)
    for copy in copies:
        copy.wait()


def finish(peers, packs, pieces, low_ref, pick_ref, side_ref, *refs):
    raw_refs, refs = refs[: len(packs)], refs[len(packs) :]
    found = {step: (ref, at) for ref, pack in zip(raw_refs, packs) for at, step in enumerate(pack)}
    back_ref, (hidden_ref, gate_ref, held, sems) = refs[0], refs[2:]
    top_count = gate_ref.shape[0]
    routed, units = hidden_ref.shape
    quarter = units // 4
    backs, sent = [], []
    for block in range(COLS):
        columns = slice(block * quarter, (block + 1) * quarter)
        back = jnp.concatenate(
            [back_ref[block_of(step, peers), columns] for step in range(peers)], axis=0
        ).astype(F32)
        backs.append(back)
        sent.append((side_ref[:, block : block + 1] * back).astype(BF))
    full = jnp.concatenate([*sent, unpack_last(peers, sent)], axis=1)
    size = routed // pieces
    copies = []
    for piece in range(pieces):
        at = slice(piece * size, (piece + 1) * size)
        held[at] = jnp.dot(low_ref[at, :], full, preferred_element_type=F32).astype(BF)
        copy = pltpu.make_async_copy(held.at[at], hidden_ref.at[at], sems.at[piece])
        copy.start()
        copies.append(copy)
    total = jnp.zeros(gate_ref.shape, F32)
    for block, back in enumerate(backs):
        columns = slice(block * quarter, (block + 1) * quarter)
        raws = jnp.concatenate(
            [
                found[step][0][found[step][1] * ROWS : (found[step][1] + 1) * ROWS, columns]
                for step in range(peers)
            ],
            axis=0,
        )
        value = jnp.sum(raws.astype(F32) * back, axis=1, keepdims=True)
        chosen = side_ref[:, COLS + block : COLS + block + 1]
        weighted = pick_ref[block] * value
        lines = [
            jnp.sum(jnp.where(chosen == float(k), weighted, 0.0), axis=0, keepdims=True)
            for k in range(top_count)
        ]
        total = total + jnp.concatenate(lines, axis=0)
    gate_ref[...] = total
    for copy in copies:
        copy.wait()


def local(out_grad, hidden, routes, gates, w_down):
    tokens, top_count = routes.shape
    units = hidden.shape[2]
    width = out_grad.shape[1]
    half = w_down.shape[1]
    routed = tokens * top_count
    peers = lax.axis_size("expert")
    rows = peers * ROWS
    routes_t, gates_t = routes.T, gates.T
    shape = jax.ShapeDtypeStruct
    half_way = peers // 2
    room = 20 if peers <= 8 else 60
    order = [half_way, *range(1, half_way), *range(half_way + 1, peers)]
    packs = [list(range(peers))]

    def across(array, step, back=False):
        pairs = [(i, partner(i, step, peers)) for i in range(peers)]
        return lax.ppermute(array, "expert", [(b, a) for a, b in pairs] if back else pairs)

    def swap(array):
        return lax.ppermute(array, "dp", [(0, 1), (1, 0)])

    w_other = swap(w_down)
    raws, received = [], {-1: w_other}
    for batch in packs:
        after = list(raws)
        count = len(batch)
        raw, *sent = pl.pallas_call(
            functools.partial(pack, peers, batch, len(raws)),
            out_shape=[shape((count * ROWS, COLS * units // 4), BF)]
            + [shape((ROWS, COLS * (units + width) // 4), BF)] * count,
            in_specs=[pl.BlockSpec(memory_space=pltpu.HBM)] * 4 + [anywhere()] * len(raws),
            out_specs=[vmem()] * (count + 1),
            scratch_shapes=[
                pltpu.VMEM((top_count, tokens), jnp.int32),
                pltpu.VMEM((top_count, tokens), F32),
                pltpu.VMEM((tokens, width), BF),
                pltpu.VMEM((routed, units), BF),
                pltpu.SemaphoreType.DMA((4,)),
            ],
            compiler_params=params(56 if peers <= 8 else 60),
            name="pack",
            cost_estimate=FREE,
        )(routes_t, gates_t, out_grad, hidden.reshape(routed, units), *after)
        raws.append(raw)
        received[0] = sent[0]
        chains = {step: -1 for step in range(half_way + 1, peers)}
        for step in order:
            array = sent[step]
            if step in chains:
                array = lax.optimization_barrier((array, received[chains[step]]))[0]
            received[step] = across(array, step)
    low_map, pick_map, side = pl.pallas_call(
        functools.partial(maps, peers),
        out_shape=[
            shape((routed, rows), BF),
            shape((COLS, rows, tokens), F32),
            shape((rows, 128), F32),
        ],
        in_specs=[vmem()] * 3,
        out_specs=[vmem()] * 3,
        compiler_params=params(room),
        name="maps",
        cost_estimate=FREE,
    )(routes_t, gates_t, w_down)
    steps = [*order, 0]
    own, keep, back = pl.pallas_call(
        functools.partial(unit_grads, steps, peers),
        out_shape=[
            shape((rows, width + half), BF),
            shape((rows, half), BF),
            shape((rows, COLS * units // 4), BF),
        ],
        in_specs=[vmem()] * (peers + 2) + [anywhere()],
        out_specs=[vmem()] * 3,
        compiler_params=params(room),
        name="unit_grads",
        cost_estimate=FREE,
    )(*[received[step] for step in steps], w_down, w_other, pick_map)
    other = swap(own)
    back = lax.all_to_all(back, "expert", split_axis=0, concat_axis=0, tiled=True)
    strip = 512 if width % 512 == 0 else width
    grad_down, done = pl.pallas_call(
        functools.partial(weight_grad, strip),
        out_shape=[shape((1, half, width), BF), shape((8, 128), F32)],
        in_specs=[vmem()] * 3,
        out_specs=[anywhere(), vmem()],
        scratch_shapes=[
            pltpu.VMEM((width // strip, half, strip), BF),
            pltpu.SemaphoreType.DMA((width // strip,)),
        ],
        compiler_params=params(room),
        name="weight_grad",
    )(keep, own, other)
    pieces = 4
    grad_hidden, grad_gates_t = pl.pallas_call(
        functools.partial(finish, peers, packs, pieces),
        out_shape=[shape((routed, units), BF), shape((top_count, tokens), F32)],
        in_specs=[vmem()] * (4 + len(packs)) + [anywhere()],
        out_specs=[anywhere(), vmem()],
        scratch_shapes=[pltpu.VMEM((routed, units), BF), pltpu.SemaphoreType.DMA((pieces,))],
        compiler_params=params(room),
        name="finish",
    )(low_map, pick_map, side, *raws, back, done)
    return grad_down, grad_hidden.reshape(tokens, top_count, units), grad_gates_t.T


def solution(mesh):
    in_specs = (
        P(("groups", "expert", "dp"), None),
        P(("groups", "expert", "dp"), None, None),
        P(("groups", "expert", "dp"), None),
        P(("groups", "expert", "dp"), None),
        P("expert", "dp", None),
    )
    out_specs = (
        P(("groups", "expert"), "dp", None),
        P(("groups", "expert", "dp"), None, None),
        P(("groups", "expert", "dp"), None),
    )
    return jax.shard_map(local, mesh=mesh, in_specs=in_specs, out_specs=out_specs, check_vma=False)
```

time: 53.7 us -> 49.7 us (0.926)
  waiting for transfers between devices: 2.86 us -> 10.6 us
  starting transfers between devices: 28 us -> 21.3 us
  Pallas kernels: 17.4 us -> 12.4 us
    ppermute x14 -> x7, starting transfers between devices: 27.4 us -> 13.2 us  [across(): lax.ppermute(array, 'expert', [(b, a) for a, b in pairs] if back else pairs)]
    all_to_all x0 -> x1, starting transfers between devices: none -> 7.57 us  [local(): lax.all_to_all(back, 'expert', split_axis=0, concat_axis=0, tiled=True)]
    all_to_all x0 -> x1, waiting for transfers between devices: none -> 6.32 us  [local(): lax.all_to_all(back, 'expert', split_axis=0, concat_axis=0, tiled=True)]
    pallas_call x5 -> x4, Pallas kernels: 16.5 us -> 11.8 us  [the longest x1 3.58 us: local(): pl.pallas_call(functools.partial(unit_grads, steps, peers), out_shape=[sh...]
    ppermute x14 -> x7, waiting for transfers between devices: 2.85 us -> 4.27 us  [across(): lax.ppermute(array, 'expert', [(b, a) for a, b in pairs] if back else pairs)]
  transfers between devices with their start and end apart: 17 -> 10, of which waited for: 4 -> 3; matrix products, arithmetic and copies ran while one was open for 0% -> 0% of each run, Pallas kernels for 28% -> 13%
where the time goes in v3:
time: 49.7 us; the launch traced here: 49.3 us
  starting transfers between devices  21.3 us (43%)
  Pallas kernels  12.4 us (25%)
  waiting for transfers between devices  10.6 us (21%)
  local copies, waits for them, and re-layouts  4.32 us (9%)
  between operations  0.69 us (1%)
    ppermute x7, starting transfers between devices, across(): lax.ppermute(array, 'expert', [(b, a) for a, b in pairs] if back else pairs)  13.2 us
    all_to_all x1, starting transfers between devices, local(): lax.all_to_all(back, 'expert', split_axis=0, concat_axis=0, tiled=True)  7.57 us
    all_to_all x1, waiting for transfers between devices, local(): lax.all_to_all(back, 'expert', split_axis=0, concat_axis=0, tiled=True)  6.32 us
    unnamed x12, local copies, waits for them, and re-layouts  4.32 us
    ppermute x7, waiting for transfers between devices, across(): lax.ppermute(array, 'expert', [(b, a) for a, b in pairs] if back else pairs)  4.27 us
    pallas_call x1, Pallas kernels, local(): pl.pallas_call(functools.partial(unit_grads, steps, peers), out_shape=[sh...  3.58 us
    pallas_call x1, Pallas kernels, local(): pl.pallas_call(functools.partial(pack, peers, batch, len(raws)), out_shap...  3.54 us
    pallas_call x1, Pallas kernels, local(): pl.pallas_call(functools.partial(finish, peers, packs, pieces), out_shape...  2.45 us
  transfers between devices with their start and end apart: 10, of which 3 were waited for; matrix products, arithmetic and copies ran while one was open for 0% of the time, Pallas kernels for 13%

profile of v3, /device:TPU:0, one launch (start us, length us, event | category | flops | bytes accessed | tf_op | source)
XLA Modules:
  0.0 49.3 jit_solution(12798520292941065647)
XLA Ops:
  0.6 0.5 %collective-permute-start.4 = (bf16[1,512,3584]{2,1,0:T(8,128)(2,1)}, bf16[1,512,3584]{2,1,0:T(8,128)(2,1)S(1)}, u32[]{:S(2)}, u32[]{:S(2)}) collective-permute-start(bf16[1,512,3584]{2,1,0:T(8,128)(2,1)} %refs_8_.1), channel_id=1, source_target_pairs={{0,1},{1,0},{2,3},{3,2},{4,5},{5,4},{6,7},{7,6},{8,9},{9,8},{10,11... | collective-permute-start | bytes 11010056 | tf_op jit(solution)/shard_map/ppermute | solution.py:339
  1.1 3.5 %pack.1 = (bf16[128,768]{1,0:T(8,128)(2,1)}, bf16[16,3456]{1,0:T(8,128)(2,1)}, bf16[16,3456]{1,0:T(8,128)(2,1)}, bf16[16,3456]{1,0:T(8,128)(2,1)}, bf16[16,3456]...) custom-call(s32[8,128]{1,0:T(8,128)} %bitcast.8, ...), custom_call_target="tpu_custom_call" | custom-call | tf_op jit(solution)/shard_map/pack/pallas_call | solution.py:346
  4.7 3.7 %collective-permute-start = (bf16[16,3456]{1,0:T(8,128)(2,1)}, bf16[16,3456]{1,0:T(8,128)(2,1)S(1)}, u32[]{:S(2)}, u32[]{:S(2)}) collective-permute-start(bf16[16,3456]{1,0:T(8,128)(2,1)} %get-tuple-element.25), channel_id=1, source_target_pairs={{0,8},{2,10},{4,12},{6,14},{8,0},{10,2},{12,4},{14,6},{1,9},{3,11}... | collective-permute-start | bytes 331784 | tf_op jit(solution)/shard_map/ppermute | solution.py:336
  8.4 1.5 %collective-permute-start.1 = (bf16[16,3456]{1,0:T(8,128)(2,1)}, bf16[16,3456]{1,0:T(8,128)(2,1)S(1)}, u32[]{:S(2)}, u32[]{:S(2)}) collective-permute-start(bf16[16,3456]{1,0:T(8,128)(2,1)} %get-tuple-element.26), channel_id=1, source_target_pairs={{0,2},{2,0},{4,6},{6,4},{8,10},{10,8},{12,14},{14,12},{1,3},{3,1},... | collective-permute-start | bytes 331784 | tf_op jit(solution)/shard_map/ppermute | solution.py:336
  9.9 1.6 %collective-permute-start.2 = (bf16[16,3456]{1,0:T(8,128)(2,1)}, bf16[16,3456]{1,0:T(8,128)(2,1)S(1)}, u32[]{:S(2)}, u32[]{:S(2)}) collective-permute-start(bf16[16,3456]{1,0:T(8,128)(2,1)} %get-tuple-element.27), channel_id=1, source_target_pairs={{0,4},{2,6},{4,0},{6,2},{8,12},{10,14},{12,8},{14,10},{1,5},{3,7},... | collective-permute-start | bytes 331784 | tf_op jit(solution)/shard_map/ppermute | solution.py:336
  11.4 0.4 collective-permute-start.3
  11.9 0.0 collective-permute-done.4.refs_9_
  11.9 1.3 %collective-permute-start.5 = (bf16[16,3456]{1,0:T(8,128)(2,1)}, bf16[16,3456]{1,0:T(8,128)(2,1)S(1)}, u32[]{:S(2)}, u32[]{:S(2)}) collective-permute-start(bf16[16,3456]{1,0:T(8,128)(2,1)} %get-tuple-element.30), channel_id=1, source_target_pairs={{0,10},{2,8},{4,14},{6,12},{8,2},{10,0},{12,6},{14,4},{1,11},{3,9}... | collective-permute-start | bytes 331784 | tf_op jit(solution)/shard_map/ppermute | solution.py:336
  13.1 1.6 %collective-permute-done.refs_0_ = bf16[16,3456]{1,0:T(8,128)(2,1)S(1)} collective-permute-done((bf16[16,3456]{1,0:T(8,128)(2,1)}, bf16[16,3456]{1,0:T(8,128)(2,1)S(1)}, u32[]{:S(2)}, u32[]{:S(2)}) %collective-permute-start) | collective-permute-done | bytes 110624 | tf_op jit(solution)/shard_map/ppermute | solution.py:336
  14.8 3.6 %collective-permute-start.6 = (bf16[16,3456]{1,0:T(8,128)(2,1)}, bf16[16,3456]{1,0:T(8,128)(2,1)S(1)}, u32[]{:S(2)}, u32[]{:S(2)}) collective-permute-start(bf16[16,3456]{1,0:T(8,128)(2,1)} %get-tuple-element.32), channel_id=1, source_target_pairs={{0,12},{2,14},{4,8},{6,10},{8,4},{10,6},{12,0},{14,2},{1,13},{3,15... | collective-permute-start | bytes 331784 | tf_op jit(solution)/shard_map/ppermute | solution.py:336
  18.3 0.0 collective-permute-done.1.refs_1_
  18.3 1.2 %collective-permute-start.7 = (bf16[16,3456]{1,0:T(8,128)(2,1)}, bf16[16,3456]{1,0:T(8,128)(2,1)S(1)}, u32[]{:S(2)}, u32[]{:S(2)}) collective-permute-start(bf16[16,3456]{1,0:T(8,128)(2,1)} %get-tuple-element.34), channel_id=1, source_target_pairs={{0,14},{2,12},{4,10},{6,8},{8,6},{10,4},{12,2},{14,0},{1,15},{3,13... | collective-permute-start | bytes 331784 | tf_op jit(solution)/shard_map/ppermute | solution.py:336
  19.6 0.0 copy-start
  19.6 2.0 %copy-done = bf16[1,512,3584]{2,1,0:T(8,128)(2,1)S(1)} copy-done((bf16[1,512,3584]{2,1,0:T(8,128)(2,1)S(1)}, bf16[1,512,3584]{2,1,0:T(8,128)(2,1)}, u32[]{:S(2)}) %copy-start) | copy-done | bytes 3670040
  21.6 0.0 copy-start.4
  21.6 0.7 %copy-done.4 = s32[128,8]{0,1:T(8,128)S(1)} copy-done((s32[128,8]{0,1:T(8,128)S(1)}, s32[128,8]{0,1:T(8,128)}, u32[]{:S(2)}) %copy-start.4) | copy-done | bytes 4120
  22.3 0.0 copy-start.5
  22.3 0.7 %copy-done.5 = f32[128,8]{0,1:T(8,128)S(1)} copy-done((f32[128,8]{0,1:T(8,128)S(1)}, f32[128,8]{0,1:T(8,128)}, u32[]{:S(2)}) %copy-start.5) | copy-done | bytes 4120
  23.0 0.0 copy-start.1
  23.0 0.6 %maps.1 = (bf16[1024,128]{1,0:T(8,128)(2,1)S(1)}, f32[3,128,128]{2,1,0:T(8,128)S(1)}, f32[128,128]{1,0:T(8,128)S(1)}) custom-call(s32[8,128]{1,0:T(8,128)S(1)} %bitcast.9, f32[8,128]{1,0:T(8,128)S(1)} %bitcast.11, bf16[1,512,3584]{2,1,0:T(8,128)(2,1)S(1)} %copy-done), custom_call_target="tpu_custom_call" | custom-call | tf_op jit(solution)/shard_map/maps/pallas_call | solution.py:371
  23.6 0.0 collective-permute-done.2.refs_2_
  23.6 0.0 collective-permute-done.3.refs_3_
  23.6 0.0 collective-permute-done.5.refs_4_
  23.6 0.0 collective-permute-done.6.refs_5_
  23.7 2.6 %collective-permute-done.7.refs_6_ = bf16[16,3456]{1,0:T(8,128)(2,1)S(1)} collective-permute-done((bf16[16,3456]{1,0:T(8,128)(2,1)}, bf16[16,3456]{1,0:T(8,128)(2,1)S(1)}, u32[]{:S(2)}, u32[]{:S(2)}) %collective-permute-start.7) | collective-permute-done | bytes 110624 | tf_op jit(solution)/shard_map/ppermute | solution.py:336
  26.3 0.0 copy-done.1
  26.3 0.0 copy-start.3
  26.3 0.9 %copy-done.3 = bf16[16,3456]{1,0:T(8,128)(2,1)S(1)} copy-done((bf16[16,3456]{1,0:T(8,128)(2,1)S(1)}, bf16[16,3456]{1,0:T(8,128)(2,1)}, u32[]{:S(2)}) %copy-start.3) | copy-done | bytes 110616
  27.2 0.0 copy-start.2
  27.2 3.6 %unit_grads.1 = (bf16[128,4096]{1,0:T(8,128)(2,1)S(1)}, bf16[128,512]{1,0:T(8,128)(2,1)S(1)}, bf16[128,768]{1,0:T(8,128)(2,1)}) custom-call(bf16[16,3456]{1,0:T(8,128)(2,1)S(1)} %collective-permute-done.refs_0_, bf16[16,3456]{1,0:T(8,128)(2,1)S(1)} %collective-permute-done.1.refs_1_, bf16[16,3456]{1,0:T(8,128)(2,1)S(1)} %collective-permute-done.2.refs_2_, ...), custom_call_target="tpu_custom_call" | custom-call | tf_op jit(solution)/shard_map/unit_grads/pallas_call | solution.py:385
  30.8 0.0 collective-permute-start.8
  30.8 7.6 %all-to-all-start = ((bf16[8,16,768]{2,1,0:T(8,128)(2,1)}), bf16[8,16,768]{2,1,0:T(8,128)(2,1)S(1)}, u32[]{:S(2)}, u32[]{:S(2)}) async-start(bf16[8,16,768]{2,1,0:T(8,128)(2,1)} %bitcast.3), calls=%async_computation | async-start | bytes 393216 | tf_op jit(solution)/shard_map/all_to_all | solution.py:399
  38.3 0.0 collective-permute-done.8.other_ref
  38.3 2.2 %weight_grad.1 = (bf16[1,512,3584]{2,1,0:T(8,128)(2,1)}, f32[8,128]{1,0:T(8,128)S(1)}) custom-call(bf16[128,512]{1,0:T(8,128)(2,1)S(1)} %get-tuple-element.37.keep_ref, bf16[128,4096]{1,0:T(8,128)(2,1)S(1)} %get-tuple-element.38.own_ref, bf16[128,4096]{1,0:T(8,128)(2,1)S(1)} %collective-permute-done.8.other_ref), custom_call_target="tpu_custom_call" | custom-call | tf_op jit(solution)/shard_map/weight_grad/pallas_call | solution.py:401
  40.6 6.3 %all-to-all-done = bf16[8,16,768]{2,1,0:T(8,128)(2,1)S(1)} async-done(((bf16[8,16,768]{2,1,0:T(8,128)(2,1)}), bf16[8,16,768]{2,1,0:T(8,128)(2,1)S(1)}, u32[]{:S(2)}, u32[]{:S(2)}) %all-to-all-start) | async-done | bytes 196640 | tf_op jit(solution)/shard_map/all_to_all | solution.py:399
  46.9 0.0 copy-done.2
  46.9 2.5 %finish.1 = (bf16[1024,1024]{1,0:T(8,128)(2,1)}, f32[8,128]{1,0:T(8,128)}) custom-call(bf16[1024,128]{1,0:T(8,128)(2,1)S(1)} %get-tuple-element.40.low_ref, f32[3,128,128]{2,1,0:T(8,128)S(1)} %get-tuple-element.36.refs_10_.pick_ref, f32[128,128]{1,0:T(8,128)S(1)} %get-tuple-element.41.side_ref, bf16[128,768]{1,0:T(8,128)(2,1)S(1)} %copy-done.2, ...), custom_call_target="tpu_custom_call" | custom-call | tf_op jit(solution)/shard_map/finish/pallas_call | solution.py:414
Async XLA Ops:
  0.6 11.2 %collective-permute-start.4 = (bf16[1,512,3584]{2,1,0:T(8,128)(2,1)}, bf16[1,512,3584]{2,1,0:T(8,128)(2,1)S(1)}, u32[]{:S(2)}, u32[]{:S(2)}) collective-permute-start(bf16[1,512,3584]{2,1,0:T(8,128)(2,1)} %refs_8_.1), channel_id=1, source_target_pairs={{0,1},{1,0},{2,3},{3,2},{4,5},{5,4},{6,7},{7,6},{8,9},{9,8},{10,11... | collective-permute-start | bytes 11010056 | tf_op jit(solution)/shard_map/ppermute | solution.py:339
  4.7 10.1 %collective-permute-start = (bf16[16,3456]{1,0:T(8,128)(2,1)}, bf16[16,3456]{1,0:T(8,128)(2,1)S(1)}, u32[]{:S(2)}, u32[]{:S(2)}) collective-permute-start(bf16[16,3456]{1,0:T(8,128)(2,1)} %get-tuple-element.25), channel_id=1, source_target_pairs={{0,8},{2,10},{4,12},{6,14},{8,0},{10,2},{12,4},{14,6},{1,9},{3,11}... | collective-permute-start | bytes 331784 | tf_op jit(solution)/shard_map/ppermute | solution.py:336
  8.4 10.0 %collective-permute-start.1 = (bf16[16,3456]{1,0:T(8,128)(2,1)}, bf16[16,3456]{1,0:T(8,128)(2,1)S(1)}, u32[]{:S(2)}, u32[]{:S(2)}) collective-permute-start(bf16[16,3456]{1,0:T(8,128)(2,1)} %get-tuple-element.26), channel_id=1, source_target_pairs={{0,2},{2,0},{4,6},{6,4},{8,10},{10,8},{12,14},{14,12},{1,3},{3,1},... | collective-permute-start | bytes 331784 | tf_op jit(solution)/shard_map/ppermute | solution.py:336
  9.9 13.8 %collective-permute-start.2 = (bf16[16,3456]{1,0:T(8,128)(2,1)}, bf16[16,3456]{1,0:T(8,128)(2,1)S(1)}, u32[]{:S(2)}, u32[]{:S(2)}) collective-permute-start(bf16[16,3456]{1,0:T(8,128)(2,1)} %get-tuple-element.27), channel_id=1, source_target_pairs={{0,4},{2,6},{4,0},{6,2},{8,12},{10,14},{12,8},{14,10},{1,5},{3,7},... | collective-permute-start | bytes 331784 | tf_op jit(solution)/shard_map/ppermute | solution.py:336
  11.4 12.2 %collective-permute-start.3 = (bf16[16,3456]{1,0:T(8,128)(2,1)}, bf16[16,3456]{1,0:T(8,128)(2,1)S(1)}, u32[]{:S(2)}, u32[]{:S(2)}) collective-permute-start(bf16[16,3456]{1,0:T(8,128)(2,1)} %get-tuple-element.28), channel_id=1, source_target_pairs={{0,6},{2,4},{4,2},{6,0},{8,14},{10,12},{12,10},{14,8},{1,7},{3,5},... | collective-permute-start | bytes 331784 | tf_op jit(solution)/shard_map/ppermute | solution.py:336
  11.9 11.8 %collective-permute-start.5 = (bf16[16,3456]{1,0:T(8,128)(2,1)}, bf16[16,3456]{1,0:T(8,128)(2,1)S(1)}, u32[]{:S(2)}, u32[]{:S(2)}) collective-permute-start(bf16[16,3456]{1,0:T(8,128)(2,1)} %get-tuple-element.30), channel_id=1, source_target_pairs={{0,10},{2,8},{4,14},{6,12},{8,2},{10,0},{12,6},{14,4},{1,11},{3,9}... | collective-permute-start | bytes 331784 | tf_op jit(solution)/shard_map/ppermute | solution.py:336
  14.8 8.9 %collective-permute-start.6 = (bf16[16,3456]{1,0:T(8,128)(2,1)}, bf16[16,3456]{1,0:T(8,128)(2,1)S(1)}, u32[]{:S(2)}, u32[]{:S(2)}) collective-permute-start(bf16[16,3456]{1,0:T(8,128)(2,1)} %get-tuple-element.32), channel_id=1, source_target_pairs={{0,12},{2,14},{4,8},{6,10},{8,4},{10,6},{12,0},{14,2},{1,13},{3,15... | collective-permute-start | bytes 331784 | tf_op jit(solution)/shard_map/ppermute | solution.py:336
  18.3 7.9 %collective-permute-start.7 = (bf16[16,3456]{1,0:T(8,128)(2,1)}, bf16[16,3456]{1,0:T(8,128)(2,1)S(1)}, u32[]{:S(2)}, u32[]{:S(2)}) collective-permute-start(bf16[16,3456]{1,0:T(8,128)(2,1)} %get-tuple-element.34), channel_id=1, source_target_pairs={{0,14},{2,12},{4,10},{6,8},{8,6},{10,4},{12,2},{14,0},{1,15},{3,13... | collective-permute-start | bytes 331784 | tf_op jit(solution)/shard_map/ppermute | solution.py:336
  19.6 2.0 %copy-start = (bf16[1,512,3584]{2,1,0:T(8,128)(2,1)S(1)}, bf16[1,512,3584]{2,1,0:T(8,128)(2,1)}, u32[]{:S(2)}) copy-start(bf16[1,512,3584]{2,1,0:T(8,128)(2,1)} %refs_8_.1) | copy-start | bytes 11010052
  21.6 0.7 %copy-start.4 = (s32[128,8]{0,1:T(8,128)S(1)}, s32[128,8]{0,1:T(8,128)}, u32[]{:S(2)}) copy-start(s32[128,8]{0,1:T(8,128)} %param.7) | copy-start | bytes 12292
  22.3 0.7 %copy-start.5 = (f32[128,8]{0,1:T(8,128)S(1)}, f32[128,8]{0,1:T(8,128)}, u32[]{:S(2)}) copy-start(f32[128,8]{0,1:T(8,128)} %param.8) | copy-start | bytes 12292
  23.0 3.3 %copy-start.1 = (bf16[1,512,3584]{2,1,0:T(8,128)(2,1)S(1)}, bf16[1,512,3584]{2,1,0:T(8,128)(2,1)}, u32[]{:S(2)}) copy-start(bf16[1,512,3584]{2,1,0:T(8,128)(2,1)} %refs_8_.1) | copy-start | bytes 11010052
  26.3 0.9 %copy-start.3 = (bf16[16,3456]{1,0:T(8,128)(2,1)S(1)}, bf16[16,3456]{1,0:T(8,128)(2,1)}, u32[]{:S(2)}) copy-start(bf16[16,3456]{1,0:T(8,128)(2,1)} %get-tuple-element.35.refs_7_) | copy-start | bytes 331780
  27.2 19.7 %copy-start.2 = (bf16[128,768]{1,0:T(8,128)(2,1)S(1)}, bf16[128,768]{1,0:T(8,128)(2,1)}, u32[]{:S(2)}) copy-start(bf16[128,768]{1,0:T(8,128)(2,1)} %get-tuple-element.42.refs_0_) | copy-start | bytes 589828
  30.8 7.6 %collective-permute-start.8 = (bf16[128,4096]{1,0:T(8,128)(2,1)S(1)}, bf16[128,4096]{1,0:T(8,128)(2,1)S(1)}, u32[]{:S(2)}, u32[]{:S(2)}) collective-permute-start(bf16[128,4096]{1,0:T(8,128)(2,1)S(1)} %get-tuple-element.38.own_ref), channel_id=1, source_target_pairs={{0,1},{1,0},{2,3},{3,2},{4,5},{5,4},{6,7},{7,6},{8,9},{9,8},{10,11... | collective-permute-start | bytes 3145736 | tf_op jit(solution)/shard_map/ppermute | solution.py:339
  30.8 16.1 %all-to-all-start = ((bf16[8,16,768]{2,1,0:T(8,128)(2,1)}), bf16[8,16,768]{2,1,0:T(8,128)(2,1)S(1)}, u32[]{:S(2)}, u32[]{:S(2)}) async-start(bf16[8,16,768]{2,1,0:T(8,128)(2,1)} %bitcast.3), calls=%async_computation | async-start | bytes 393216 | tf_op jit(solution)/shard_map/all_to_all | solution.py:399

commit v4 on v3

--- a/solution.py
+++ b/solution.py
@@ -161,7 +161,7 @@
             out_refs[step][:, columns] = scaled[step * ROWS : (step + 1) * ROWS, :]
 
 
-def maps(peers, routes_ref, gates_ref, weight_ref, low_ref, pick_ref, side_ref):
+def maps(peers, routes_ref, gates_ref, weight_ref, block_ref, low_ref, pick_ref, side_ref):
     hits, place = routing(routes_ref[...], peers, range(peers))
     gate, choice = gate_of(hits, gates_ref[...]), choice_of(hits)
     low = low_rows(peers * ROWS, low_ref.shape[0])
@@ -219,7 +219,7 @@
     left = swap_ref[:, : 4 * wide]
     across = (((1,), (1,)), ((), ()))
     halves = [
-        lax.dot_general(left, ref[0], across, preferred_element_type=F32)
+        lax.dot_general(ref[0], left, across, preferred_element_type=F32).T
         for ref in (own_ref, other_ref)
     ]
     low_half = jnp.where(first_core, halves[0], halves[1])
@@ -326,8 +326,8 @@
     rows = peers * ROWS
     routes_t, gates_t = routes.T, gates.T
     shape = jax.ShapeDtypeStruct
+    room = 20 if peers <= 8 else 60
     half_way = peers // 2
-    room = 20 if peers <= 8 else 60
     order = [half_way, *range(1, half_way), *range(half_way + 1, peers)]
     packs = [list(range(peers))]
 
@@ -375,12 +375,12 @@
             shape((COLS, rows, tokens), F32),
             shape((rows, 128), F32),
         ],
-        in_specs=[vmem()] * 3,
+        in_specs=[vmem()] * 4,
         out_specs=[vmem()] * 3,
         compiler_params=params(room),
         name="maps",
         cost_estimate=FREE,
-    )(routes_t, gates_t, w_down)
+    )(routes_t, gates_t, w_down, received[0])
     steps = [*order, 0]
     own, keep, back = pl.pallas_call(
         functools.partial(unit_grads, steps, peers),

time: 49.7 us -> 48.4 us (0.974)
  waiting for transfers between devices: 10.6 us -> 9.7 us
    ppermute x7, waiting for transfers between devices: 4.27 us -> 3.37 us  [across(): lax.ppermute(array, 'expert', [(b, a) for a, b in pairs] if back else pairs)]
where the time goes in v4:
time: 48.4 us; the launch traced here: 48 us
  starting transfers between devices  21.3 us (44%)
  Pallas kernels  12 us (25%)
  waiting for transfers between devices  9.7 us (20%)
  local copies, waits for them, and re-layouts  4.31 us (9%)
  between operations  0.69 us (1%)
    ppermute x7, starting transfers between devices, across(): lax.ppermute(array, 'expert', [(b, a) for a, b in pairs] if back else pairs)  13.2 us
    all_to_all x1, starting transfers between devices, local(): lax.all_to_all(back, 'expert', split_axis=0, concat_axis=0, tiled=True)  7.56 us
    all_to_all x1, waiting for transfers between devices, local(): lax.all_to_all(back, 'expert', split_axis=0, concat_axis=0, tiled=True)  6.32 us
    unnamed x12, local copies, waits for them, and re-layouts  4.31 us
    pallas_call x1, Pallas kernels, local(): pl.pallas_call(functools.partial(pack, peers, batch, len(raws)), out_shap...  3.54 us
    ppermute x7, waiting for transfers between devices, across(): lax.ppermute(array, 'expert', [(b, a) for a, b in pairs] if back else pairs)  3.37 us
    pallas_call x1, Pallas kernels, local(): pl.pallas_call(functools.partial(unit_grads, steps, peers), out_shape=[sh...  3.18 us
    pallas_call x1, Pallas kernels, local(): pl.pallas_call(functools.partial(finish, peers, packs, pieces), out_shape...  2.45 us
  transfers between devices with their start and end apart: 10, of which 3 were waited for; matrix products, arithmetic and copies ran while one was open for 0% of the time, Pallas kernels for 13%

profile of v4, /device:TPU:0, one launch (start us, length us, event | category | flops | bytes accessed | tf_op | source)
XLA Modules:
  0.0 48.0 jit_solution(18024891328941765601)
XLA Ops:
  0.6 0.5 %collective-permute-start.4 = (bf16[1,512,3584]{2,1,0:T(8,128)(2,1)}, bf16[1,512,3584]{2,1,0:T(8,128)(2,1)S(1)}, u32[]{:S(2)}, u32[]{:S(2)}) collective-permute-start(bf16[1,512,3584]{2,1,0:T(8,128)(2,1)} %refs_8_.1), channel_id=1, source_target_pairs={{0,1},{1,0},{2,3},{3,2},{4,5},{5,4},{6,7},{7,6},{8,9},{9,8},{10,11... | collective-permute-start | bytes 11010056 | tf_op jit(solution)/shard_map/ppermute | solution.py:339
  1.1 3.5 %pack.1 = (bf16[128,768]{1,0:T(8,128)(2,1)}, bf16[16,3456]{1,0:T(8,128)(2,1)}, bf16[16,3456]{1,0:T(8,128)(2,1)}, bf16[16,3456]{1,0:T(8,128)(2,1)}, bf16[16,3456]...) custom-call(s32[8,128]{1,0:T(8,128)} %bitcast.8, ...), custom_call_target="tpu_custom_call" | custom-call | tf_op jit(solution)/shard_map/pack/pallas_call | solution.py:346
  4.7 3.7 %collective-permute-start = (bf16[16,3456]{1,0:T(8,128)(2,1)}, bf16[16,3456]{1,0:T(8,128)(2,1)S(1)}, u32[]{:S(2)}, u32[]{:S(2)}) collective-permute-start(bf16[16,3456]{1,0:T(8,128)(2,1)} %get-tuple-element.25), channel_id=1, source_target_pairs={{0,8},{2,10},{4,12},{6,14},{8,0},{10,2},{12,4},{14,6},{1,9},{3,11}... | collective-permute-start | bytes 331784 | tf_op jit(solution)/shard_map/ppermute | solution.py:336
  8.4 1.5 %collective-permute-start.1 = (bf16[16,3456]{1,0:T(8,128)(2,1)}, bf16[16,3456]{1,0:T(8,128)(2,1)S(1)}, u32[]{:S(2)}, u32[]{:S(2)}) collective-permute-start(bf16[16,3456]{1,0:T(8,128)(2,1)} %get-tuple-element.26), channel_id=1, source_target_pairs={{0,2},{2,0},{4,6},{6,4},{8,10},{10,8},{12,14},{14,12},{1,3},{3,1},... | collective-permute-start | bytes 331784 | tf_op jit(solution)/shard_map/ppermute | solution.py:336
  9.9 1.6 %collective-permute-start.2 = (bf16[16,3456]{1,0:T(8,128)(2,1)}, bf16[16,3456]{1,0:T(8,128)(2,1)S(1)}, u32[]{:S(2)}, u32[]{:S(2)}) collective-permute-start(bf16[16,3456]{1,0:T(8,128)(2,1)} %get-tuple-element.27), channel_id=1, source_target_pairs={{0,4},{2,6},{4,0},{6,2},{8,12},{10,14},{12,8},{14,10},{1,5},{3,7},... | collective-permute-start | bytes 331784 | tf_op jit(solution)/shard_map/ppermute | solution.py:336
  11.4 0.4 collective-permute-start.3
  11.9 0.0 collective-permute-done.4.refs_9_
  11.9 1.3 %collective-permute-start.5 = (bf16[16,3456]{1,0:T(8,128)(2,1)}, bf16[16,3456]{1,0:T(8,128)(2,1)S(1)}, u32[]{:S(2)}, u32[]{:S(2)}) collective-permute-start(bf16[16,3456]{1,0:T(8,128)(2,1)} %get-tuple-element.30), channel_id=1, source_target_pairs={{0,10},{2,8},{4,14},{6,12},{8,2},{10,0},{12,6},{14,4},{1,11},{3,9}... | collective-permute-start | bytes 331784 | tf_op jit(solution)/shard_map/ppermute | solution.py:336
  13.1 1.6 %collective-permute-done.refs_0_ = bf16[16,3456]{1,0:T(8,128)(2,1)S(1)} collective-permute-done((bf16[16,3456]{1,0:T(8,128)(2,1)}, bf16[16,3456]{1,0:T(8,128)(2,1)S(1)}, u32[]{:S(2)}, u32[]{:S(2)}) %collective-permute-start) | collective-permute-done | bytes 110624 | tf_op jit(solution)/shard_map/ppermute | solution.py:336
  14.8 3.6 %collective-permute-start.6 = (bf16[16,3456]{1,0:T(8,128)(2,1)}, bf16[16,3456]{1,0:T(8,128)(2,1)S(1)}, u32[]{:S(2)}, u32[]{:S(2)}) collective-permute-start(bf16[16,3456]{1,0:T(8,128)(2,1)} %get-tuple-element.32), channel_id=1, source_target_pairs={{0,12},{2,14},{4,8},{6,10},{8,4},{10,6},{12,0},{14,2},{1,13},{3,15... | collective-permute-start | bytes 331784 | tf_op jit(solution)/shard_map/ppermute | solution.py:336
  18.3 0.0 collective-permute-done.1.refs_1_
  18.3 1.2 %collective-permute-start.7 = (bf16[16,3456]{1,0:T(8,128)(2,1)}, bf16[16,3456]{1,0:T(8,128)(2,1)S(1)}, u32[]{:S(2)}, u32[]{:S(2)}) collective-permute-start(bf16[16,3456]{1,0:T(8,128)(2,1)} %get-tuple-element.34), channel_id=1, source_target_pairs={{0,14},{2,12},{4,10},{6,8},{8,6},{10,4},{12,2},{14,0},{1,15},{3,13... | collective-permute-start | bytes 331784 | tf_op jit(solution)/shard_map/ppermute | solution.py:336
  19.6 0.0 copy-start
  19.6 2.0 %copy-done = bf16[1,512,3584]{2,1,0:T(8,128)(2,1)S(1)} copy-done((bf16[1,512,3584]{2,1,0:T(8,128)(2,1)S(1)}, bf16[1,512,3584]{2,1,0:T(8,128)(2,1)}, u32[]{:S(2)}) %copy-start) | copy-done | bytes 3670040
  21.6 0.0 copy-start.2
  21.6 0.9 %copy-done.2 = bf16[16,3456]{1,0:T(8,128)(2,1)S(1)} copy-done((bf16[16,3456]{1,0:T(8,128)(2,1)S(1)}, bf16[16,3456]{1,0:T(8,128)(2,1)}, u32[]{:S(2)}) %copy-start.2) | copy-done | bytes 110616
  22.5 0.0 copy-start.4
  22.5 0.7 %copy-done.4 = s32[128,8]{0,1:T(8,128)S(1)} copy-done((s32[128,8]{0,1:T(8,128)S(1)}, s32[128,8]{0,1:T(8,128)}, u32[]{:S(2)}) %copy-start.4) | copy-done | bytes 4120
  23.2 0.0 copy-start.5
  23.2 0.7 %copy-done.5 = f32[128,8]{0,1:T(8,128)S(1)} copy-done((f32[128,8]{0,1:T(8,128)S(1)}, f32[128,8]{0,1:T(8,128)}, u32[]{:S(2)}) %copy-start.5) | copy-done | bytes 4120
  23.9 0.0 copy-start.1
  23.9 0.6 %maps.1 = (bf16[1024,128]{1,0:T(8,128)(2,1)S(1)}, f32[3,128,128]{2,1,0:T(8,128)S(1)}, f32[128,128]{1,0:T(8,128)S(1)}) custom-call(s32[8,128]{1,0:T(8,128)S(1)} %bitcast.9, f32[8,128]{1,0:T(8,128)S(1)} %bitcast.11, bf16[1,512,3584]{2,1,0:T(8,128)(2,1)S(1)} %copy-done, bf16[16,3456]{1,0:T(8,128)(2,1)S(1)} %copy-done.2), custom_call_target="tpu_custom_call" | custom-call | tf_op jit(solution)/shard_map/maps/pallas_call | solution.py:371
  24.5 0.0 collective-permute-done.2.refs_2_
  24.5 0.0 collective-permute-done.3.refs_3_
  24.5 0.0 collective-permute-done.5.refs_4_
  24.5 0.0 collective-permute-done.6.refs_5_
  24.6 1.7 %collective-permute-done.7.refs_6_ = bf16[16,3456]{1,0:T(8,128)(2,1)S(1)} collective-permute-done((bf16[16,3456]{1,0:T(8,128)(2,1)}, bf16[16,3456]{1,0:T(8,128)(2,1)S(1)}, u32[]{:S(2)}, u32[]{:S(2)}) %collective-permute-start.7) | collective-permute-done | bytes 110624 | tf_op jit(solution)/shard_map/ppermute | solution.py:336
  26.3 0.0 copy-done.1
  26.3 0.0 copy-start.3
  26.3 3.2 %unit_grads.1 = (bf16[128,4096]{1,0:T(8,128)(2,1)S(1)}, bf16[128,512]{1,0:T(8,128)(2,1)S(1)}, bf16[128,768]{1,0:T(8,128)(2,1)}) custom-call(bf16[16,3456]{1,0:T(8,128)(2,1)S(1)} %collective-permute-done.refs_0_, bf16[16,3456]{1,0:T(8,128)(2,1)S(1)} %collective-permute-done.1.refs_1_, bf16[16,3456]{1,0:T(8,128)(2,1)S(1)} %collective-permute-done.2.refs_2_, ...), custom_call_target="tpu_custom_call" | custom-call | tf_op jit(solution)/shard_map/unit_grads/pallas_call | solution.py:385
  29.5 0.0 collective-permute-start.8
  29.5 7.6 %all-to-all-start = ((bf16[8,16,768]{2,1,0:T(8,128)(2,1)}), bf16[8,16,768]{2,1,0:T(8,128)(2,1)S(1)}, u32[]{:S(2)}, u32[]{:S(2)}) async-start(bf16[8,16,768]{2,1,0:T(8,128)(2,1)} %bitcast.3), calls=%async_computation | async-start | bytes 393216 | tf_op jit(solution)/shard_map/all_to_all | solution.py:399
  37.0 0.0 collective-permute-done.8.other_ref
  37.0 2.2 %weight_grad.1 = (bf16[1,512,3584]{2,1,0:T(8,128)(2,1)}, f32[8,128]{1,0:T(8,128)S(1)}) custom-call(bf16[128,512]{1,0:T(8,128)(2,1)S(1)} %get-tuple-element.37.keep_ref, bf16[128,4096]{1,0:T(8,128)(2,1)S(1)} %get-tuple-element.38.own_ref, bf16[128,4096]{1,0:T(8,128)(2,1)S(1)} %collective-permute-done.8.other_ref), custom_call_target="tpu_custom_call" | custom-call | tf_op jit(solution)/shard_map/weight_grad/pallas_call | solution.py:401
  39.3 6.3 %all-to-all-done = bf16[8,16,768]{2,1,0:T(8,128)(2,1)S(1)} async-done(((bf16[8,16,768]{2,1,0:T(8,128)(2,1)}), bf16[8,16,768]{2,1,0:T(8,128)(2,1)S(1)}, u32[]{:S(2)}, u32[]{:S(2)}) %all-to-all-start) | async-done | bytes 196640 | tf_op jit(solution)/shard_map/all_to_all | solution.py:399
  45.6 0.0 copy-done.3
  45.6 2.5 %finish.1 = (bf16[1024,1024]{1,0:T(8,128)(2,1)}, f32[8,128]{1,0:T(8,128)}) custom-call(bf16[1024,128]{1,0:T(8,128)(2,1)S(1)} %get-tuple-element.40.low_ref, f32[3,128,128]{2,1,0:T(8,128)S(1)} %get-tuple-element.36.refs_10_.pick_ref, f32[128,128]{1,0:T(8,128)S(1)} %get-tuple-element.41.side_ref, bf16[128,768]{1,0:T(8,128)(2,1)S(1)} %copy-done.3, ...), custom_call_target="tpu_custom_call" | custom-call | tf_op jit(solution)/shard_map/finish/pallas_call | solution.py:414
Async XLA Ops:
  0.6 11.2 %collective-permute-start.4 = (bf16[1,512,3584]{2,1,0:T(8,128)(2,1)}, bf16[1,512,3584]{2,1,0:T(8,128)(2,1)S(1)}, u32[]{:S(2)}, u32[]{:S(2)}) collective-permute-start(bf16[1,512,3584]{2,1,0:T(8,128)(2,1)} %refs_8_.1), channel_id=1, source_target_pairs={{0,1},{1,0},{2,3},{3,2},{4,5},{5,4},{6,7},{7,6},{8,9},{9,8},{10,11... | collective-permute-start | bytes 11010056 | tf_op jit(solution)/shard_map/ppermute | solution.py:339
  4.7 10.1 %collective-permute-start = (bf16[16,3456]{1,0:T(8,128)(2,1)}, bf16[16,3456]{1,0:T(8,128)(2,1)S(1)}, u32[]{:S(2)}, u32[]{:S(2)}) collective-permute-start(bf16[16,3456]{1,0:T(8,128)(2,1)} %get-tuple-element.25), channel_id=1, source_target_pairs={{0,8},{2,10},{4,12},{6,14},{8,0},{10,2},{12,4},{14,6},{1,9},{3,11}... | collective-permute-start | bytes 331784 | tf_op jit(solution)/shard_map/ppermute | solution.py:336
  8.4 10.0 %collective-permute-start.1 = (bf16[16,3456]{1,0:T(8,128)(2,1)}, bf16[16,3456]{1,0:T(8,128)(2,1)S(1)}, u32[]{:S(2)}, u32[]{:S(2)}) collective-permute-start(bf16[16,3456]{1,0:T(8,128)(2,1)} %get-tuple-element.26), channel_id=1, source_target_pairs={{0,2},{2,0},{4,6},{6,4},{8,10},{10,8},{12,14},{14,12},{1,3},{3,1},... | collective-permute-start | bytes 331784 | tf_op jit(solution)/shard_map/ppermute | solution.py:336
  9.9 14.7 %collective-permute-start.2 = (bf16[16,3456]{1,0:T(8,128)(2,1)}, bf16[16,3456]{1,0:T(8,128)(2,1)S(1)}, u32[]{:S(2)}, u32[]{:S(2)}) collective-permute-start(bf16[16,3456]{1,0:T(8,128)(2,1)} %get-tuple-element.27), channel_id=1, source_target_pairs={{0,4},{2,6},{4,0},{6,2},{8,12},{10,14},{12,8},{14,10},{1,5},{3,7},... | collective-permute-start | bytes 331784 | tf_op jit(solution)/shard_map/ppermute | solution.py:336
  11.4 13.1 %collective-permute-start.3 = (bf16[16,3456]{1,0:T(8,128)(2,1)}, bf16[16,3456]{1,0:T(8,128)(2,1)S(1)}, u32[]{:S(2)}, u32[]{:S(2)}) collective-permute-start(bf16[16,3456]{1,0:T(8,128)(2,1)} %get-tuple-element.28), channel_id=1, source_target_pairs={{0,6},{2,4},{4,2},{6,0},{8,14},{10,12},{12,10},{14,8},{1,7},{3,5},... | collective-permute-start | bytes 331784 | tf_op jit(solution)/shard_map/ppermute | solution.py:336
  11.9 12.7 %collective-permute-start.5 = (bf16[16,3456]{1,0:T(8,128)(2,1)}, bf16[16,3456]{1,0:T(8,128)(2,1)S(1)}, u32[]{:S(2)}, u32[]{:S(2)}) collective-permute-start(bf16[16,3456]{1,0:T(8,128)(2,1)} %get-tuple-element.30), channel_id=1, source_target_pairs={{0,10},{2,8},{4,14},{6,12},{8,2},{10,0},{12,6},{14,4},{1,11},{3,9}... | collective-permute-start | bytes 331784 | tf_op jit(solution)/shard_map/ppermute | solution.py:336
  14.8 9.8 %collective-permute-start.6 = (bf16[16,3456]{1,0:T(8,128)(2,1)}, bf16[16,3456]{1,0:T(8,128)(2,1)S(1)}, u32[]{:S(2)}, u32[]{:S(2)}) collective-permute-start(bf16[16,3456]{1,0:T(8,128)(2,1)} %get-tuple-element.32), channel_id=1, source_target_pairs={{0,12},{2,14},{4,8},{6,10},{8,4},{10,6},{12,0},{14,2},{1,13},{3,15... | collective-permute-start | bytes 331784 | tf_op jit(solution)/shard_map/ppermute | solution.py:336
  18.3 7.9 %collective-permute-start.7 = (bf16[16,3456]{1,0:T(8,128)(2,1)}, bf16[16,3456]{1,0:T(8,128)(2,1)S(1)}, u32[]{:S(2)}, u32[]{:S(2)}) collective-permute-start(bf16[16,3456]{1,0:T(8,128)(2,1)} %get-tuple-element.34), channel_id=1, source_target_pairs={{0,14},{2,12},{4,10},{6,8},{8,6},{10,4},{12,2},{14,0},{1,15},{3,13... | collective-permute-start | bytes 331784 | tf_op jit(solution)/shard_map/ppermute | solution.py:336
  19.6 2.0 %copy-start = (bf16[1,512,3584]{2,1,0:T(8,128)(2,1)S(1)}, bf16[1,512,3584]{2,1,0:T(8,128)(2,1)}, u32[]{:S(2)}) copy-start(bf16[1,512,3584]{2,1,0:T(8,128)(2,1)} %refs_8_.1) | copy-start | bytes 11010052
  21.6 0.9 %copy-start.2 = (bf16[16,3456]{1,0:T(8,128)(2,1)S(1)}, bf16[16,3456]{1,0:T(8,128)(2,1)}, u32[]{:S(2)}) copy-start(bf16[16,3456]{1,0:T(8,128)(2,1)} %get-tuple-element.35.block_ref.refs_7_) | copy-start | bytes 331780
  22.5 0.7 %copy-start.4 = (s32[128,8]{0,1:T(8,128)S(1)}, s32[128,8]{0,1:T(8,128)}, u32[]{:S(2)}) copy-start(s32[128,8]{0,1:T(8,128)} %param.7) | copy-start | bytes 12292
  23.2 0.7 %copy-start.5 = (f32[128,8]{0,1:T(8,128)S(1)}, f32[128,8]{0,1:T(8,128)}, u32[]{:S(2)}) copy-start(f32[128,8]{0,1:T(8,128)} %param.8) | copy-start | bytes 12292
  23.9 2.4 %copy-start.1 = (bf16[1,512,3584]{2,1,0:T(8,128)(2,1)S(1)}, bf16[1,512,3584]{2,1,0:T(8,128)(2,1)}, u32[]{:S(2)}) copy-start(bf16[1,512,3584]{2,1,0:T(8,128)(2,1)} %refs_8_.1) | copy-start | bytes 11010052
  26.3 19.3 %copy-start.3 = (bf16[128,768]{1,0:T(8,128)(2,1)S(1)}, bf16[128,768]{1,0:T(8,128)(2,1)}, u32[]{:S(2)}) copy-start(bf16[128,768]{1,0:T(8,128)(2,1)} %get-tuple-element.42.refs_0_) | copy-start | bytes 589828
  29.5 7.6 %collective-permute-start.8 = (bf16[128,4096]{1,0:T(8,128)(2,1)S(1)}, bf16[128,4096]{1,0:T(8,128)(2,1)S(1)}, u32[]{:S(2)}, u32[]{:S(2)}) collective-permute-start(bf16[128,4096]{1,0:T(8,128)(2,1)S(1)} %get-tuple-element.38.own_ref), channel_id=1, source_target_pairs={{0,1},{1,0},{2,3},{3,2},{4,5},{5,4},{6,7},{7,6},{8,9},{9,8},{10,11... | collective-permute-start | bytes 3145736 | tf_op jit(solution)/shard_map/ppermute | solution.py:339
  29.5 16.1 %all-to-all-start = ((bf16[8,16,768]{2,1,0:T(8,128)(2,1)}), bf16[8,16,768]{2,1,0:T(8,128)(2,1)S(1)}, u32[]{:S(2)}, u32[]{:S(2)}) async-start(bf16[8,16,768]{2,1,0:T(8,128)(2,1)} %bitcast.3), calls=%async_computation | async-start | bytes 393216 | tf_op jit(solution)/shard_map/all_to_all | solution.py:399

commit v5 on v4

--- a/solution.py
+++ b/solution.py
@@ -62,7 +62,8 @@
 
 
 def low_rows(rows, width):
-    return lax.broadcasted_iota(jnp.int32, (rows, width), 0) % ROWS < MOST
+    inside = lax.rem(lax.broadcasted_iota(jnp.int32, (rows, 1), 0), ROWS)
+    return jnp.broadcast_to(inside, (rows, width)) < MOST
 
 
 def gate_of(hits, gates_t):
@@ -102,11 +103,12 @@
 def route_picks(pick, choice, top_count):
     tokens = pick.shape[1]
     routed = tokens * top_count
+    column = lax.broadcasted_iota(jnp.int32, (1, routed), 1)
+    of_token = jnp.broadcast_to(lax.div(column, top_count), (tokens, routed))
     token = lax.broadcasted_iota(jnp.int32, (tokens, routed), 0)
-    column = lax.broadcasted_iota(jnp.int32, (tokens, routed), 1)
-    wide = (column // top_count == token).astype(F32).astype(BF)
+    wide = (of_token == token).astype(F32).astype(BF)
     mine = jnp.dot(pick.astype(BF), wide, preferred_element_type=F32)
-    which = (lax.broadcasted_iota(jnp.int32, (pick.shape[0], routed), 1) % top_count).astype(F32)
+    which = lax.rem(column, top_count).astype(F32)
     return jnp.where(which == choice, mine, 0.0)
 
 
@@ -180,10 +182,9 @@
 def last_quarter(peers, block):
     rows = peers * ROWS
     to = lax.broadcasted_iota(jnp.int32, (rows, rows), 0)
-    at = lax.broadcasted_iota(jnp.int32, (rows, rows), 1)
-    inside = at % ROWS
-    wanted = at - MOST + EXTRA * block
-    return ((inside >= MOST) & (to == wanted)).astype(F32).astype(BF)
+    at = lax.broadcasted_iota(jnp.int32, (1, rows), 1)
+    wanted = jnp.where(lax.rem(at, ROWS) >= MOST, at - MOST + EXTRA * block, -1)
+    return (to == jnp.broadcast_to(wanted, (rows, rows))).astype(F32).astype(BF)
 
 
 def block_of(step, peers):

time: 48.4 us -> 48.4 us (level)
  no operation moved by 1% of the time
where the time goes in v5:
time: 48.4 us; the launch traced here: 48 us
  starting transfers between devices  21.3 us (44%)
  Pallas kernels  12 us (25%)
  waiting for transfers between devices  9.69 us (20%)
  local copies, waits for them, and re-layouts  4.31 us (9%)
  between operations  0.69 us (1%)
    ppermute x7, starting transfers between devices, across(): lax.ppermute(array, 'expert', [(b, a) for a, b in pairs] if back else pairs)  13.2 us
    all_to_all x1, starting transfers between devices, local(): lax.all_to_all(back, 'expert', split_axis=0, concat_axis=0, tiled=True)  7.57 us
    all_to_all x1, waiting for transfers between devices, local(): lax.all_to_all(back, 'expert', split_axis=0, concat_axis=0, tiled=True)  6.32 us
    unnamed x12, local copies, waits for them, and re-layouts  4.31 us
    pallas_call x1, Pallas kernels, local(): pl.pallas_call(functools.partial(pack, peers, batch, len(raws)), out_shap...  3.55 us
    ppermute x7, waiting for transfers between devices, across(): lax.ppermute(array, 'expert', [(b, a) for a, b in pairs] if back else pairs)  3.36 us
    pallas_call x1, Pallas kernels, local(): pl.pallas_call(functools.partial(unit_grads, steps, peers), out_shape=[sh...  3.18 us
    pallas_call x1, Pallas kernels, local(): pl.pallas_call(functools.partial(finish, peers, packs, pieces), out_shape...  2.44 us
  transfers between devices with their start and end apart: 10, of which 3 were waited for; matrix products, arithmetic and copies ran while one was open for 0% of the time, Pallas kernels for 13%

profile of v5, /device:TPU:0, one launch (start us, length us, event | category | flops | bytes accessed | tf_op | source)
XLA Modules:
  0.0 48.0 jit_solution(1726161371334597083)
XLA Ops:
  0.6 0.5 %collective-permute-start.4 = (bf16[1,512,3584]{2,1,0:T(8,128)(2,1)}, bf16[1,512,3584]{2,1,0:T(8,128)(2,1)S(1)}, u32[]{:S(2)}, u32[]{:S(2)}) collective-permute-start(bf16[1,512,3584]{2,1,0:T(8,128)(2,1)} %refs_8_.1), channel_id=1, source_target_pairs={{0,1},{1,0},{2,3},{3,2},{4,5},{5,4},{6,7},{7,6},{8,9},{9,8},{10,11... | collective-permute-start | bytes 11010056 | tf_op jit(solution)/shard_map/ppermute | solution.py:340
  1.1 3.5 %pack.1 = (bf16[128,768]{1,0:T(8,128)(2,1)}, bf16[16,3456]{1,0:T(8,128)(2,1)}, bf16[16,3456]{1,0:T(8,128)(2,1)}, bf16[16,3456]{1,0:T(8,128)(2,1)}, bf16[16,3456]...) custom-call(s32[8,128]{1,0:T(8,128)} %bitcast.8, ...), custom_call_target="tpu_custom_call" | custom-call | tf_op jit(solution)/shard_map/pack/pallas_call | solution.py:347
  4.7 3.7 %collective-permute-start = (bf16[16,3456]{1,0:T(8,128)(2,1)}, bf16[16,3456]{1,0:T(8,128)(2,1)S(1)}, u32[]{:S(2)}, u32[]{:S(2)}) collective-permute-start(bf16[16,3456]{1,0:T(8,128)(2,1)} %get-tuple-element.25), channel_id=1, source_target_pairs={{0,8},{2,10},{4,12},{6,14},{8,0},{10,2},{12,4},{14,6},{1,9},{3,11}... | collective-permute-start | bytes 331784 | tf_op jit(solution)/shard_map/ppermute | solution.py:337
  8.4 1.5 %collective-permute-start.1 = (bf16[16,3456]{1,0:T(8,128)(2,1)}, bf16[16,3456]{1,0:T(8,128)(2,1)S(1)}, u32[]{:S(2)}, u32[]{:S(2)}) collective-permute-start(bf16[16,3456]{1,0:T(8,128)(2,1)} %get-tuple-element.26), channel_id=1, source_target_pairs={{0,2},{2,0},{4,6},{6,4},{8,10},{10,8},{12,14},{14,12},{1,3},{3,1},... | collective-permute-start | bytes 331784 | tf_op jit(solution)/shard_map/ppermute | solution.py:337
  9.9 1.6 %collective-permute-start.2 = (bf16[16,3456]{1,0:T(8,128)(2,1)}, bf16[16,3456]{1,0:T(8,128)(2,1)S(1)}, u32[]{:S(2)}, u32[]{:S(2)}) collective-permute-start(bf16[16,3456]{1,0:T(8,128)(2,1)} %get-tuple-element.27), channel_id=1, source_target_pairs={{0,4},{2,6},{4,0},{6,2},{8,12},{10,14},{12,8},{14,10},{1,5},{3,7},... | collective-permute-start | bytes 331784 | tf_op jit(solution)/shard_map/ppermute | solution.py:337
  11.5 0.4 collective-permute-start.3
  11.9 0.0 collective-permute-done.4.refs_9_
  11.9 1.3 %collective-permute-start.5 = (bf16[16,3456]{1,0:T(8,128)(2,1)}, bf16[16,3456]{1,0:T(8,128)(2,1)S(1)}, u32[]{:S(2)}, u32[]{:S(2)}) collective-permute-start(bf16[16,3456]{1,0:T(8,128)(2,1)} %get-tuple-element.30), channel_id=1, source_target_pairs={{0,10},{2,8},{4,14},{6,12},{8,2},{10,0},{12,6},{14,4},{1,11},{3,9}... | collective-permute-start | bytes 331784 | tf_op jit(solution)/shard_map/ppermute | solution.py:337
  13.1 1.6 %collective-permute-done.refs_0_ = bf16[16,3456]{1,0:T(8,128)(2,1)S(1)} collective-permute-done((bf16[16,3456]{1,0:T(8,128)(2,1)}, bf16[16,3456]{1,0:T(8,128)(2,1)S(1)}, u32[]{:S(2)}, u32[]{:S(2)}) %collective-permute-start) | collective-permute-done | bytes 110624 | tf_op jit(solution)/shard_map/ppermute | solution.py:337
  14.8 3.6 %collective-permute-start.6 = (bf16[16,3456]{1,0:T(8,128)(2,1)}, bf16[16,3456]{1,0:T(8,128)(2,1)S(1)}, u32[]{:S(2)}, u32[]{:S(2)}) collective-permute-start(bf16[16,3456]{1,0:T(8,128)(2,1)} %get-tuple-element.32), channel_id=1, source_target_pairs={{0,12},{2,14},{4,8},{6,10},{8,4},{10,6},{12,0},{14,2},{1,13},{3,15... | collective-permute-start | bytes 331784 | tf_op jit(solution)/shard_map/ppermute | solution.py:337
  18.3 0.0 collective-permute-done.1.refs_1_
  18.3 1.2 %collective-permute-start.7 = (bf16[16,3456]{1,0:T(8,128)(2,1)}, bf16[16,3456]{1,0:T(8,128)(2,1)S(1)}, u32[]{:S(2)}, u32[]{:S(2)}) collective-permute-start(bf16[16,3456]{1,0:T(8,128)(2,1)} %get-tuple-element.34), channel_id=1, source_target_pairs={{0,14},{2,12},{4,10},{6,8},{8,6},{10,4},{12,2},{14,0},{1,15},{3,13... | collective-permute-start | bytes 331784 | tf_op jit(solution)/shard_map/ppermute | solution.py:337
  19.6 0.0 copy-start
  19.6 2.0 %copy-done = bf16[1,512,3584]{2,1,0:T(8,128)(2,1)S(1)} copy-done((bf16[1,512,3584]{2,1,0:T(8,128)(2,1)S(1)}, bf16[1,512,3584]{2,1,0:T(8,128)(2,1)}, u32[]{:S(2)}) %copy-start) | copy-done | bytes 3670040
  21.6 0.0 copy-start.2
  21.6 0.9 %copy-done.2 = bf16[16,3456]{1,0:T(8,128)(2,1)S(1)} copy-done((bf16[16,3456]{1,0:T(8,128)(2,1)S(1)}, bf16[16,3456]{1,0:T(8,128)(2,1)}, u32[]{:S(2)}) %copy-start.2) | copy-done | bytes 110616
  22.5 0.0 copy-start.4
  22.5 0.7 %copy-done.4 = s32[128,8]{0,1:T(8,128)S(1)} copy-done((s32[128,8]{0,1:T(8,128)S(1)}, s32[128,8]{0,1:T(8,128)}, u32[]{:S(2)}) %copy-start.4) | copy-done | bytes 4120
  23.2 0.0 copy-start.5
  23.2 0.7 %copy-done.5 = f32[128,8]{0,1:T(8,128)S(1)} copy-done((f32[128,8]{0,1:T(8,128)S(1)}, f32[128,8]{0,1:T(8,128)}, u32[]{:S(2)}) %copy-start.5) | copy-done | bytes 4120
  23.9 0.0 copy-start.1
  23.9 0.6 %maps.1 = (bf16[1024,128]{1,0:T(8,128)(2,1)S(1)}, f32[3,128,128]{2,1,0:T(8,128)S(1)}, f32[128,128]{1,0:T(8,128)S(1)}) custom-call(s32[8,128]{1,0:T(8,128)S(1)} %bitcast.9, f32[8,128]{1,0:T(8,128)S(1)} %bitcast.11, bf16[1,512,3584]{2,1,0:T(8,128)(2,1)S(1)} %copy-done, bf16[16,3456]{1,0:T(8,128)(2,1)S(1)} %copy-done.2), custom_call_target="tpu_custom_call" | custom-call | tf_op jit(solution)/shard_map/maps/pallas_call | solution.py:372
  24.5 0.0 collective-permute-done.2.refs_2_
  24.5 0.0 collective-permute-done.3.refs_3_
  24.6 0.0 collective-permute-done.5.refs_4_
  24.6 0.0 collective-permute-done.6.refs_5_
  24.6 1.7 %collective-permute-done.7.refs_6_ = bf16[16,3456]{1,0:T(8,128)(2,1)S(1)} collective-permute-done((bf16[16,3456]{1,0:T(8,128)(2,1)}, bf16[16,3456]{1,0:T(8,128)(2,1)S(1)}, u32[]{:S(2)}, u32[]{:S(2)}) %collective-permute-start.7) | collective-permute-done | bytes 110624 | tf_op jit(solution)/shard_map/ppermute | solution.py:337
  26.3 0.0 copy-done.1
  26.3 0.0 copy-start.3
  26.3 3.2 %unit_grads.1 = (bf16[128,4096]{1,0:T(8,128)(2,1)S(1)}, bf16[128,512]{1,0:T(8,128)(2,1)S(1)}, bf16[128,768]{1,0:T(8,128)(2,1)}) custom-call(bf16[16,3456]{1,0:T(8,128)(2,1)S(1)} %collective-permute-done.refs_0_, bf16[16,3456]{1,0:T(8,128)(2,1)S(1)} %collective-permute-done.1.refs_1_, bf16[16,3456]{1,0:T(8,128)(2,1)S(1)} %collective-permute-done.2.refs_2_, ...), custom_call_target="tpu_custom_call" | custom-call | tf_op jit(solution)/shard_map/unit_grads/pallas_call | solution.py:386
  29.5 0.0 collective-permute-start.8
  29.5 7.6 %all-to-all-start = ((bf16[8,16,768]{2,1,0:T(8,128)(2,1)}), bf16[8,16,768]{2,1,0:T(8,128)(2,1)S(1)}, u32[]{:S(2)}, u32[]{:S(2)}) async-start(bf16[8,16,768]{2,1,0:T(8,128)(2,1)} %bitcast.3), calls=%async_computation | async-start | bytes 393216 | tf_op jit(solution)/shard_map/all_to_all | solution.py:400
  37.0 0.0 collective-permute-done.8.other_ref
  37.0 2.2 %weight_grad.1 = (bf16[1,512,3584]{2,1,0:T(8,128)(2,1)}, f32[8,128]{1,0:T(8,128)S(1)}) custom-call(bf16[128,512]{1,0:T(8,128)(2,1)S(1)} %get-tuple-element.37.keep_ref, bf16[128,4096]{1,0:T(8,128)(2,1)S(1)} %get-tuple-element.38.own_ref, bf16[128,4096]{1,0:T(8,128)(2,1)S(1)} %collective-permute-done.8.other_ref), custom_call_target="tpu_custom_call" | custom-call | tf_op jit(solution)/shard_map/weight_grad/pallas_call | solution.py:402
  39.3 6.3 %all-to-all-done = bf16[8,16,768]{2,1,0:T(8,128)(2,1)S(1)} async-done(((bf16[8,16,768]{2,1,0:T(8,128)(2,1)}), bf16[8,16,768]{2,1,0:T(8,128)(2,1)S(1)}, u32[]{:S(2)}, u32[]{:S(2)}) %all-to-all-start) | async-done | bytes 196640 | tf_op jit(solution)/shard_map/all_to_all | solution.py:400
  45.6 0.0 copy-done.3
  45.6 2.4 %finish.1 = (bf16[1024,1024]{1,0:T(8,128)(2,1)}, f32[8,128]{1,0:T(8,128)}) custom-call(bf16[1024,128]{1,0:T(8,128)(2,1)S(1)} %get-tuple-element.40.low_ref, f32[3,128,128]{2,1,0:T(8,128)S(1)} %get-tuple-element.36.refs_10_.pick_ref, f32[128,128]{1,0:T(8,128)S(1)} %get-tuple-element.41.side_ref, bf16[128,768]{1,0:T(8,128)(2,1)S(1)} %copy-done.3, ...), custom_call_target="tpu_custom_call" | custom-call | tf_op jit(solution)/shard_map/finish/pallas_call | solution.py:415
Async XLA Ops:
  0.6 11.2 %collective-permute-start.4 = (bf16[1,512,3584]{2,1,0:T(8,128)(2,1)}, bf16[1,512,3584]{2,1,0:T(8,128)(2,1)S(1)}, u32[]{:S(2)}, u32[]{:S(2)}) collective-permute-start(bf16[1,512,3584]{2,1,0:T(8,128)(2,1)} %refs_8_.1), channel_id=1, source_target_pairs={{0,1},{1,0},{2,3},{3,2},{4,5},{5,4},{6,7},{7,6},{8,9},{9,8},{10,11... | collective-permute-start | bytes 11010056 | tf_op jit(solution)/shard_map/ppermute | solution.py:340
  4.7 10.1 %collective-permute-start = (bf16[16,3456]{1,0:T(8,128)(2,1)}, bf16[16,3456]{1,0:T(8,128)(2,1)S(1)}, u32[]{:S(2)}, u32[]{:S(2)}) collective-permute-start(bf16[16,3456]{1,0:T(8,128)(2,1)} %get-tuple-element.25), channel_id=1, source_target_pairs={{0,8},{2,10},{4,12},{6,14},{8,0},{10,2},{12,4},{14,6},{1,9},{3,11}... | collective-permute-start | bytes 331784 | tf_op jit(solution)/shard_map/ppermute | solution.py:337
  8.4 10.0 %collective-permute-start.1 = (bf16[16,3456]{1,0:T(8,128)(2,1)}, bf16[16,3456]{1,0:T(8,128)(2,1)S(1)}, u32[]{:S(2)}, u32[]{:S(2)}) collective-permute-start(bf16[16,3456]{1,0:T(8,128)(2,1)} %get-tuple-element.26), channel_id=1, source_target_pairs={{0,2},{2,0},{4,6},{6,4},{8,10},{10,8},{12,14},{14,12},{1,3},{3,1},... | collective-permute-start | bytes 331784 | tf_op jit(solution)/shard_map/ppermute | solution.py:337
  9.9 14.7 %collective-permute-start.2 = (bf16[16,3456]{1,0:T(8,128)(2,1)}, bf16[16,3456]{1,0:T(8,128)(2,1)S(1)}, u32[]{:S(2)}, u32[]{:S(2)}) collective-permute-start(bf16[16,3456]{1,0:T(8,128)(2,1)} %get-tuple-element.27), channel_id=1, source_target_pairs={{0,4},{2,6},{4,0},{6,2},{8,12},{10,14},{12,8},{14,10},{1,5},{3,7},... | collective-permute-start | bytes 331784 | tf_op jit(solution)/shard_map/ppermute | solution.py:337
  11.5 13.1 %collective-permute-start.3 = (bf16[16,3456]{1,0:T(8,128)(2,1)}, bf16[16,3456]{1,0:T(8,128)(2,1)S(1)}, u32[]{:S(2)}, u32[]{:S(2)}) collective-permute-start(bf16[16,3456]{1,0:T(8,128)(2,1)} %get-tuple-element.28), channel_id=1, source_target_pairs={{0,6},{2,4},{4,2},{6,0},{8,14},{10,12},{12,10},{14,8},{1,7},{3,5},... | collective-permute-start | bytes 331784 | tf_op jit(solution)/shard_map/ppermute | solution.py:337
  11.9 12.7 %collective-permute-start.5 = (bf16[16,3456]{1,0:T(8,128)(2,1)}, bf16[16,3456]{1,0:T(8,128)(2,1)S(1)}, u32[]{:S(2)}, u32[]{:S(2)}) collective-permute-start(bf16[16,3456]{1,0:T(8,128)(2,1)} %get-tuple-element.30), channel_id=1, source_target_pairs={{0,10},{2,8},{4,14},{6,12},{8,2},{10,0},{12,6},{14,4},{1,11},{3,9}... | collective-permute-start | bytes 331784 | tf_op jit(solution)/shard_map/ppermute | solution.py:337
  14.8 9.8 %collective-permute-start.6 = (bf16[16,3456]{1,0:T(8,128)(2,1)}, bf16[16,3456]{1,0:T(8,128)(2,1)S(1)}, u32[]{:S(2)}, u32[]{:S(2)}) collective-permute-start(bf16[16,3456]{1,0:T(8,128)(2,1)} %get-tuple-element.32), channel_id=1, source_target_pairs={{0,12},{2,14},{4,8},{6,10},{8,4},{10,6},{12,0},{14,2},{1,13},{3,15... | collective-permute-start | bytes 331784 | tf_op jit(solution)/shard_map/ppermute | solution.py:337
  18.3 7.9 %collective-permute-start.7 = (bf16[16,3456]{1,0:T(8,128)(2,1)}, bf16[16,3456]{1,0:T(8,128)(2,1)S(1)}, u32[]{:S(2)}, u32[]{:S(2)}) collective-permute-start(bf16[16,3456]{1,0:T(8,128)(2,1)} %get-tuple-element.34), channel_id=1, source_target_pairs={{0,14},{2,12},{4,10},{6,8},{8,6},{10,4},{12,2},{14,0},{1,15},{3,13... | collective-permute-start | bytes 331784 | tf_op jit(solution)/shard_map/ppermute | solution.py:337
  19.6 2.0 %copy-start = (bf16[1,512,3584]{2,1,0:T(8,128)(2,1)S(1)}, bf16[1,512,3584]{2,1,0:T(8,128)(2,1)}, u32[]{:S(2)}) copy-start(bf16[1,512,3584]{2,1,0:T(8,128)(2,1)} %refs_8_.1) | copy-start | bytes 11010052
  21.6 0.9 %copy-start.2 = (bf16[16,3456]{1,0:T(8,128)(2,1)S(1)}, bf16[16,3456]{1,0:T(8,128)(2,1)}, u32[]{:S(2)}) copy-start(bf16[16,3456]{1,0:T(8,128)(2,1)} %get-tuple-element.35.block_ref.refs_7_) | copy-start | bytes 331780
  22.5 0.7 %copy-start.4 = (s32[128,8]{0,1:T(8,128)S(1)}, s32[128,8]{0,1:T(8,128)}, u32[]{:S(2)}) copy-start(s32[128,8]{0,1:T(8,128)} %param.7) | copy-start | bytes 12292
  23.2 0.7 %copy-start.5 = (f32[128,8]{0,1:T(8,128)S(1)}, f32[128,8]{0,1:T(8,128)}, u32[]{:S(2)}) copy-start(f32[128,8]{0,1:T(8,128)} %param.8) | copy-start | bytes 12292
  23.9 2.4 %copy-start.1 = (bf16[1,512,3584]{2,1,0:T(8,128)(2,1)S(1)}, bf16[1,512,3584]{2,1,0:T(8,128)(2,1)}, u32[]{:S(2)}) copy-start(bf16[1,512,3584]{2,1,0:T(8,128)(2,1)} %refs_8_.1) | copy-start | bytes 11010052
  26.3 19.3 %copy-start.3 = (bf16[128,768]{1,0:T(8,128)(2,1)S(1)}, bf16[128,768]{1,0:T(8,128)(2,1)}, u32[]{:S(2)}) copy-start(bf16[128,768]{1,0:T(8,128)(2,1)} %get-tuple-element.42.refs_0_) | copy-start | bytes 589828
  29.5 7.6 %collective-permute-start.8 = (bf16[128,4096]{1,0:T(8,128)(2,1)S(1)}, bf16[128,4096]{1,0:T(8,128)(2,1)S(1)}, u32[]{:S(2)}, u32[]{:S(2)}) collective-permute-start(bf16[128,4096]{1,0:T(8,128)(2,1)S(1)} %get-tuple-element.38.own_ref), channel_id=1, source_target_pairs={{0,1},{1,0},{2,3},{3,2},{4,5},{5,4},{6,7},{7,6},{8,9},{9,8},{10,11... | collective-permute-start | bytes 3145736 | tf_op jit(solution)/shard_map/ppermute | solution.py:340
  29.5 16.1 %all-to-all-start = ((bf16[8,16,768]{2,1,0:T(8,128)(2,1)}), bf16[8,16,768]{2,1,0:T(8,128)(2,1)S(1)}, u32[]{:S(2)}, u32[]{:S(2)}) async-start(bf16[8,16,768]{2,1,0:T(8,128)(2,1)} %bitcast.3), calls=%async_computation | async-start | bytes 393216 | tf_op jit(solution)/shard_map/all_to_all | solution.py:400

commit v6 on v5

--- a/solution.py
+++ b/solution.py
@@ -329,7 +329,7 @@
     shape = jax.ShapeDtypeStruct
     room = 20 if peers <= 8 else 60
     half_way = peers // 2
-    order = [half_way, *range(1, half_way), *range(half_way + 1, peers)]
+    order = [half_way, *range(half_way - 1, 0, -1), *range(half_way + 1, peers)]
     packs = [list(range(peers))]
 
     def across(array, step, back=False):

time: 48.4 us -> 48.4 us (level)
  local copies, waits for them, and re-layouts: 4.31 us -> 5.66 us
  waiting for transfers between devices: 9.69 us -> 8.7 us
    all_to_all x1, starting transfers between devices: 7.57 us -> 5.53 us  [local(): lax.all_to_all(back, 'expert', split_axis=0, concat_axis=0, tiled=True)]
    ppermute x7, starting transfers between devices: 13.2 us -> 14.9 us  [across(): lax.ppermute(array, 'expert', [(b, a) for a, b in pairs] if back else pairs)]
    unnamed x12, local copies, waits for them, and re-layouts: 4.31 us -> 5.66 us
    ppermute x7, waiting for transfers between devices: 3.36 us -> 2.36 us  [across(): lax.ppermute(array, 'expert', [(b, a) for a, b in pairs] if back else pairs)]
where the time goes in v6:
time: 48.4 us; the launch traced here: 48 us
  starting transfers between devices  21 us (43%)
  Pallas kernels  12 us (25%)
  waiting for transfers between devices  8.7 us (18%)
  local copies, waits for them, and re-layouts  5.66 us (12%)
  between operations  0.7 us (1%)
    ppermute x7, starting transfers between devices, across(): lax.ppermute(array, 'expert', [(b, a) for a, b in pairs] if back else pairs)  14.9 us
    all_to_all x1, waiting for transfers between devices, local(): lax.all_to_all(back, 'expert', split_axis=0, concat_axis=0, tiled=True)  6.33 us
    unnamed x12, local copies, waits for them, and re-layouts  5.66 us
    all_to_all x1, starting transfers between devices, local(): lax.all_to_all(back, 'expert', split_axis=0, concat_axis=0, tiled=True)  5.53 us
    pallas_call x1, Pallas kernels, local(): pl.pallas_call(functools.partial(pack, peers, batch, len(raws)), out_shap...  3.55 us
    pallas_call x1, Pallas kernels, local(): pl.pallas_call(functools.partial(unit_grads, steps, peers), out_shape=[sh...  3.17 us
    pallas_call x1, Pallas kernels, local(): pl.pallas_call(functools.partial(finish, peers, packs, pieces), out_shape...  2.44 us
    ppermute x7, waiting for transfers between devices, across(): lax.ppermute(array, 'expert', [(b, a) for a, b in pairs] if back else pairs)  2.36 us
  transfers between devices with their start and end apart: 10, of which 3 were waited for; matrix products, arithmetic and copies ran while one was open for 0% of the time, Pallas kernels for 13%

profile of v6, /device:TPU:0, one launch (start us, length us, event | category | flops | bytes accessed | tf_op | source)
XLA Modules:
  0.0 48.0 jit_solution(17389886246944478412)
XLA Ops:
  0.6 0.5 %collective-permute-start.4 = (bf16[1,512,3584]{2,1,0:T(8,128)(2,1)}, bf16[1,512,3584]{2,1,0:T(8,128)(2,1)S(1)}, u32[]{:S(2)}, u32[]{:S(2)}) collective-permute-start(bf16[1,512,3584]{2,1,0:T(8,128)(2,1)} %refs_8_.1), channel_id=1, source_target_pairs={{0,1},{1,0},{2,3},{3,2},{4,5},{5,4},{6,7},{7,6},{8,9},{9,8},{10,11... | collective-permute-start | bytes 11010056 | tf_op jit(solution)/shard_map/ppermute | solution.py:340
  1.1 3.5 %pack.1 = (bf16[128,768]{1,0:T(8,128)(2,1)}, bf16[16,3456]{1,0:T(8,128)(2,1)}, bf16[16,3456]{1,0:T(8,128)(2,1)}, bf16[16,3456]{1,0:T(8,128)(2,1)}, bf16[16,3456]...) custom-call(s32[8,128]{1,0:T(8,128)} %bitcast.8, ...), custom_call_target="tpu_custom_call" | custom-call | tf_op jit(solution)/shard_map/pack/pallas_call | solution.py:347
  4.7 3.7 %collective-permute-start = (bf16[16,3456]{1,0:T(8,128)(2,1)}, bf16[16,3456]{1,0:T(8,128)(2,1)S(1)}, u32[]{:S(2)}, u32[]{:S(2)}) collective-permute-start(bf16[16,3456]{1,0:T(8,128)(2,1)} %get-tuple-element.25), channel_id=1, source_target_pairs={{0,8},{2,10},{4,12},{6,14},{8,0},{10,2},{12,4},{14,6},{1,9},{3,11}... | collective-permute-start | bytes 331784 | tf_op jit(solution)/shard_map/ppermute | solution.py:337
  8.4 2.5 %collective-permute-start.1 = (bf16[16,3456]{1,0:T(8,128)(2,1)}, bf16[16,3456]{1,0:T(8,128)(2,1)S(1)}, u32[]{:S(2)}, u32[]{:S(2)}) collective-permute-start(bf16[16,3456]{1,0:T(8,128)(2,1)} %get-tuple-element.26), channel_id=1, source_target_pairs={{0,6},{2,4},{4,2},{6,0},{8,14},{10,12},{12,10},{14,8},{1,7},{3,5},... | collective-permute-start | bytes 331784 | tf_op jit(solution)/shard_map/ppermute | solution.py:337
  10.9 0.4 collective-permute-start.2
  11.3 0.5 %collective-permute-start.3 = (bf16[16,3456]{1,0:T(8,128)(2,1)}, bf16[16,3456]{1,0:T(8,128)(2,1)S(1)}, u32[]{:S(2)}, u32[]{:S(2)}) collective-permute-start(bf16[16,3456]{1,0:T(8,128)(2,1)} %get-tuple-element.28), channel_id=1, source_target_pairs={{0,2},{2,0},{4,6},{6,4},{8,10},{10,8},{12,14},{14,12},{1,3},{3,1},... | collective-permute-start | bytes 331784 | tf_op jit(solution)/shard_map/ppermute | solution.py:337
  11.9 0.0 collective-permute-done.4.refs_9_
  11.9 1.3 %collective-permute-start.5 = (bf16[16,3456]{1,0:T(8,128)(2,1)}, bf16[16,3456]{1,0:T(8,128)(2,1)S(1)}, u32[]{:S(2)}, u32[]{:S(2)}) collective-permute-start(bf16[16,3456]{1,0:T(8,128)(2,1)} %get-tuple-element.30), channel_id=1, source_target_pairs={{0,10},{2,8},{4,14},{6,12},{8,2},{10,0},{12,6},{14,4},{1,11},{3,9}... | collective-permute-start | bytes 331784 | tf_op jit(solution)/shard_map/ppermute | solution.py:337
  13.1 1.6 %collective-permute-done.refs_0_ = bf16[16,3456]{1,0:T(8,128)(2,1)S(1)} collective-permute-done((bf16[16,3456]{1,0:T(8,128)(2,1)}, bf16[16,3456]{1,0:T(8,128)(2,1)S(1)}, u32[]{:S(2)}, u32[]{:S(2)}) %collective-permute-start) | collective-permute-done | bytes 110624 | tf_op jit(solution)/shard_map/ppermute | solution.py:337
  14.8 3.6 %collective-permute-start.6 = (bf16[16,3456]{1,0:T(8,128)(2,1)}, bf16[16,3456]{1,0:T(8,128)(2,1)S(1)}, u32[]{:S(2)}, u32[]{:S(2)}) collective-permute-start(bf16[16,3456]{1,0:T(8,128)(2,1)} %get-tuple-element.32), channel_id=1, source_target_pairs={{0,12},{2,14},{4,8},{6,10},{8,4},{10,6},{12,0},{14,2},{1,13},{3,15... | collective-permute-start | bytes 331784 | tf_op jit(solution)/shard_map/ppermute | solution.py:337
  18.3 0.7 %collective-permute-done.1.refs_1_ = bf16[16,3456]{1,0:T(8,128)(2,1)S(1)} collective-permute-done((bf16[16,3456]{1,0:T(8,128)(2,1)}, bf16[16,3456]{1,0:T(8,128)(2,1)S(1)}, u32[]{:S(2)}, u32[]{:S(2)}) %collective-permute-start.1) | collective-permute-done | bytes 110624 | tf_op jit(solution)/shard_map/ppermute | solution.py:337
  19.1 2.9 %collective-permute-start.7 = (bf16[16,3456]{1,0:T(8,128)(2,1)}, bf16[16,3456]{1,0:T(8,128)(2,1)S(1)}, u32[]{:S(2)}, u32[]{:S(2)}) collective-permute-start(bf16[16,3456]{1,0:T(8,128)(2,1)} %get-tuple-element.34), channel_id=1, source_target_pairs={{0,14},{2,12},{4,10},{6,8},{8,6},{10,4},{12,2},{14,0},{1,15},{3,13... | collective-permute-start | bytes 331784 | tf_op jit(solution)/shard_map/ppermute | solution.py:337
  22.0 0.0 copy-start
  22.0 2.0 %copy-done = bf16[1,512,3584]{2,1,0:T(8,128)(2,1)S(1)} copy-done((bf16[1,512,3584]{2,1,0:T(8,128)(2,1)S(1)}, bf16[1,512,3584]{2,1,0:T(8,128)(2,1)}, u32[]{:S(2)}) %copy-start) | copy-done | bytes 3670040
  24.0 0.0 copy-start.2
  24.0 0.9 %copy-done.2 = bf16[16,3456]{1,0:T(8,128)(2,1)S(1)} copy-done((bf16[16,3456]{1,0:T(8,128)(2,1)S(1)}, bf16[16,3456]{1,0:T(8,128)(2,1)}, u32[]{:S(2)}) %copy-start.2) | copy-done | bytes 110616
  24.9 0.0 copy-start.4
  24.9 0.7 %copy-done.4 = s32[128,8]{0,1:T(8,128)S(1)} copy-done((s32[128,8]{0,1:T(8,128)S(1)}, s32[128,8]{0,1:T(8,128)}, u32[]{:S(2)}) %copy-start.4) | copy-done | bytes 4120
  25.6 0.0 copy-start.5
  25.6 0.7 %copy-done.5 = f32[128,8]{0,1:T(8,128)S(1)} copy-done((f32[128,8]{0,1:T(8,128)S(1)}, f32[128,8]{0,1:T(8,128)}, u32[]{:S(2)}) %copy-start.5) | copy-done | bytes 4120
  26.3 0.0 copy-start.1
  26.3 0.6 %maps.1 = (bf16[1024,128]{1,0:T(8,128)(2,1)S(1)}, f32[3,128,128]{2,1,0:T(8,128)S(1)}, f32[128,128]{1,0:T(8,128)S(1)}) custom-call(s32[8,128]{1,0:T(8,128)S(1)} %bitcast.9, f32[8,128]{1,0:T(8,128)S(1)} %bitcast.11, bf16[1,512,3584]{2,1,0:T(8,128)(2,1)S(1)} %copy-done, bf16[16,3456]{1,0:T(8,128)(2,1)S(1)} %copy-done.2), custom_call_target="tpu_custom_call" | custom-call | tf_op jit(solution)/shard_map/maps/pallas_call | solution.py:372
  26.9 0.0 collective-permute-done.2.refs_2_
  26.9 0.0 collective-permute-done.3.refs_3_
  26.9 0.0 collective-permute-done.5.refs_4_
  27.0 0.0 collective-permute-done.6.refs_5_
  27.0 0.0 collective-permute-done.7.refs_6_
  27.0 1.3 %copy-done.1 = bf16[1,512,3584]{2,1,0:T(8,128)(2,1)S(1)} copy-done((bf16[1,512,3584]{2,1,0:T(8,128)(2,1)S(1)}, bf16[1,512,3584]{2,1,0:T(8,128)(2,1)}, u32[]{:S(2)}) %copy-start.1) | copy-done | bytes 3670040
  28.3 0.0 copy-start.3
  28.3 3.2 %unit_grads.1 = (bf16[128,4096]{1,0:T(8,128)(2,1)S(1)}, bf16[128,512]{1,0:T(8,128)(2,1)S(1)}, bf16[128,768]{1,0:T(8,128)(2,1)}) custom-call(bf16[16,3456]{1,0:T(8,128)(2,1)S(1)} %collective-permute-done.refs_0_, bf16[16,3456]{1,0:T(8,128)(2,1)S(1)} %collective-permute-done.1.refs_1_, bf16[16,3456]{1,0:T(8,128)(2,1)S(1)} %collective-permute-done.2.refs_2_, ...), custom_call_target="tpu_custom_call" | custom-call | tf_op jit(solution)/shard_map/unit_grads/pallas_call | solution.py:386
  31.5 0.0 collective-permute-start.8
  31.5 5.5 %all-to-all-start = ((bf16[8,16,768]{2,1,0:T(8,128)(2,1)}), bf16[8,16,768]{2,1,0:T(8,128)(2,1)S(1)}, u32[]{:S(2)}, u32[]{:S(2)}) async-start(bf16[8,16,768]{2,1,0:T(8,128)(2,1)} %bitcast.3), calls=%async_computation | async-start | bytes 393216 | tf_op jit(solution)/shard_map/all_to_all | solution.py:400
  37.0 0.0 collective-permute-done.8.other_ref
  37.0 2.2 %weight_grad.1 = (bf16[1,512,3584]{2,1,0:T(8,128)(2,1)}, f32[8,128]{1,0:T(8,128)S(1)}) custom-call(bf16[128,512]{1,0:T(8,128)(2,1)S(1)} %get-tuple-element.37.keep_ref, bf16[128,4096]{1,0:T(8,128)(2,1)S(1)} %get-tuple-element.38.own_ref, bf16[128,4096]{1,0:T(8,128)(2,1)S(1)} %collective-permute-done.8.other_ref), custom_call_target="tpu_custom_call" | custom-call | tf_op jit(solution)/shard_map/weight_grad/pallas_call | solution.py:402
  39.3 6.3 %all-to-all-done = bf16[8,16,768]{2,1,0:T(8,128)(2,1)S(1)} async-done(((bf16[8,16,768]{2,1,0:T(8,128)(2,1)}), bf16[8,16,768]{2,1,0:T(8,128)(2,1)S(1)}, u32[]{:S(2)}, u32[]{:S(2)}) %all-to-all-start) | async-done | bytes 196640 | tf_op jit(solution)/shard_map/all_to_all | solution.py:400
  45.6 0.0 copy-done.3
  45.6 2.4 %finish.1 = (bf16[1024,1024]{1,0:T(8,128)(2,1)}, f32[8,128]{1,0:T(8,128)}) custom-call(bf16[1024,128]{1,0:T(8,128)(2,1)S(1)} %get-tuple-element.40.low_ref, f32[3,128,128]{2,1,0:T(8,128)S(1)} %get-tuple-element.36.refs_10_.pick_ref, f32[128,128]{1,0:T(8,128)S(1)} %get-tuple-element.41.side_ref, bf16[128,768]{1,0:T(8,128)(2,1)S(1)} %copy-done.3, ...), custom_call_target="tpu_custom_call" | custom-call | tf_op jit(solution)/shard_map/finish/pallas_call | solution.py:415
Async XLA Ops:
  0.6 11.2 %collective-permute-start.4 = (bf16[1,512,3584]{2,1,0:T(8,128)(2,1)}, bf16[1,512,3584]{2,1,0:T(8,128)(2,1)S(1)}, u32[]{:S(2)}, u32[]{:S(2)}) collective-permute-start(bf16[1,512,3584]{2,1,0:T(8,128)(2,1)} %refs_8_.1), channel_id=1, source_target_pairs={{0,1},{1,0},{2,3},{3,2},{4,5},{5,4},{6,7},{7,6},{8,9},{9,8},{10,11... | collective-permute-start | bytes 11010056 | tf_op jit(solution)/shard_map/ppermute | solution.py:340
  4.7 10.1 %collective-permute-start = (bf16[16,3456]{1,0:T(8,128)(2,1)}, bf16[16,3456]{1,0:T(8,128)(2,1)S(1)}, u32[]{:S(2)}, u32[]{:S(2)}) collective-permute-start(bf16[16,3456]{1,0:T(8,128)(2,1)} %get-tuple-element.25), channel_id=1, source_target_pairs={{0,8},{2,10},{4,12},{6,14},{8,0},{10,2},{12,4},{14,6},{1,9},{3,11}... | collective-permute-start | bytes 331784 | tf_op jit(solution)/shard_map/ppermute | solution.py:337
  8.4 10.7 %collective-permute-start.1 = (bf16[16,3456]{1,0:T(8,128)(2,1)}, bf16[16,3456]{1,0:T(8,128)(2,1)S(1)}, u32[]{:S(2)}, u32[]{:S(2)}) collective-permute-start(bf16[16,3456]{1,0:T(8,128)(2,1)} %get-tuple-element.26), channel_id=1, source_target_pairs={{0,6},{2,4},{4,2},{6,0},{8,14},{10,12},{12,10},{14,8},{1,7},{3,5},... | collective-permute-start | bytes 331784 | tf_op jit(solution)/shard_map/ppermute | solution.py:337
  10.9 16.0 %collective-permute-start.2 = (bf16[16,3456]{1,0:T(8,128)(2,1)}, bf16[16,3456]{1,0:T(8,128)(2,1)S(1)}, u32[]{:S(2)}, u32[]{:S(2)}) collective-permute-start(bf16[16,3456]{1,0:T(8,128)(2,1)} %get-tuple-element.27), channel_id=1, source_target_pairs={{0,4},{2,6},{4,0},{6,2},{8,12},{10,14},{12,8},{14,10},{1,5},{3,7},... | collective-permute-start | bytes 331784 | tf_op jit(solution)/shard_map/ppermute | solution.py:337
  11.3 15.6 %collective-permute-start.3 = (bf16[16,3456]{1,0:T(8,128)(2,1)}, bf16[16,3456]{1,0:T(8,128)(2,1)S(1)}, u32[]{:S(2)}, u32[]{:S(2)}) collective-permute-start(bf16[16,3456]{1,0:T(8,128)(2,1)} %get-tuple-element.28), channel_id=1, source_target_pairs={{0,2},{2,0},{4,6},{6,4},{8,10},{10,8},{12,14},{14,12},{1,3},{3,1},... | collective-permute-start | bytes 331784 | tf_op jit(solution)/shard_map/ppermute | solution.py:337
  11.9 15.1 %collective-permute-start.5 = (bf16[16,3456]{1,0:T(8,128)(2,1)}, bf16[16,3456]{1,0:T(8,128)(2,1)S(1)}, u32[]{:S(2)}, u32[]{:S(2)}) collective-permute-start(bf16[16,3456]{1,0:T(8,128)(2,1)} %get-tuple-element.30), channel_id=1, source_target_pairs={{0,10},{2,8},{4,14},{6,12},{8,2},{10,0},{12,6},{14,4},{1,11},{3,9}... | collective-permute-start | bytes 331784 | tf_op jit(solution)/shard_map/ppermute | solution.py:337
  14.8 12.2 %collective-permute-start.6 = (bf16[16,3456]{1,0:T(8,128)(2,1)}, bf16[16,3456]{1,0:T(8,128)(2,1)S(1)}, u32[]{:S(2)}, u32[]{:S(2)}) collective-permute-start(bf16[16,3456]{1,0:T(8,128)(2,1)} %get-tuple-element.32), channel_id=1, source_target_pairs={{0,12},{2,14},{4,8},{6,10},{8,4},{10,6},{12,0},{14,2},{1,13},{3,15... | collective-permute-start | bytes 331784 | tf_op jit(solution)/shard_map/ppermute | solution.py:337
  19.1 7.9 %collective-permute-start.7 = (bf16[16,3456]{1,0:T(8,128)(2,1)}, bf16[16,3456]{1,0:T(8,128)(2,1)S(1)}, u32[]{:S(2)}, u32[]{:S(2)}) collective-permute-start(bf16[16,3456]{1,0:T(8,128)(2,1)} %get-tuple-element.34), channel_id=1, source_target_pairs={{0,14},{2,12},{4,10},{6,8},{8,6},{10,4},{12,2},{14,0},{1,15},{3,13... | collective-permute-start | bytes 331784 | tf_op jit(solution)/shard_map/ppermute | solution.py:337
  22.0 2.0 %copy-start = (bf16[1,512,3584]{2,1,0:T(8,128)(2,1)S(1)}, bf16[1,512,3584]{2,1,0:T(8,128)(2,1)}, u32[]{:S(2)}) copy-start(bf16[1,512,3584]{2,1,0:T(8,128)(2,1)} %refs_8_.1) | copy-start | bytes 11010052
  24.0 0.9 %copy-start.2 = (bf16[16,3456]{1,0:T(8,128)(2,1)S(1)}, bf16[16,3456]{1,0:T(8,128)(2,1)}, u32[]{:S(2)}) copy-start(bf16[16,3456]{1,0:T(8,128)(2,1)} %get-tuple-element.35.block_ref.refs_7_) | copy-start | bytes 331780
  24.9 0.7 %copy-start.4 = (s32[128,8]{0,1:T(8,128)S(1)}, s32[128,8]{0,1:T(8,128)}, u32[]{:S(2)}) copy-start(s32[128,8]{0,1:T(8,128)} %param.7) | copy-start | bytes 12292
  25.6 0.7 %copy-start.5 = (f32[128,8]{0,1:T(8,128)S(1)}, f32[128,8]{0,1:T(8,128)}, u32[]{:S(2)}) copy-start(f32[128,8]{0,1:T(8,128)} %param.8) | copy-start | bytes 12292
  26.3 2.0 %copy-start.1 = (bf16[1,512,3584]{2,1,0:T(8,128)(2,1)S(1)}, bf16[1,512,3584]{2,1,0:T(8,128)(2,1)}, u32[]{:S(2)}) copy-start(bf16[1,512,3584]{2,1,0:T(8,128)(2,1)} %refs_8_.1) | copy-start | bytes 11010052
  28.3 17.3 %copy-start.3 = (bf16[128,768]{1,0:T(8,128)(2,1)S(1)}, bf16[128,768]{1,0:T(8,128)(2,1)}, u32[]{:S(2)}) copy-start(bf16[128,768]{1,0:T(8,128)(2,1)} %get-tuple-element.42.refs_0_) | copy-start | bytes 589828
  31.5 5.5 %collective-permute-start.8 = (bf16[128,4096]{1,0:T(8,128)(2,1)S(1)}, bf16[128,4096]{1,0:T(8,128)(2,1)S(1)}, u32[]{:S(2)}, u32[]{:S(2)}) collective-permute-start(bf16[128,4096]{1,0:T(8,128)(2,1)S(1)} %get-tuple-element.38.own_ref), channel_id=1, source_target_pairs={{0,1},{1,0},{2,3},{3,2},{4,5},{5,4},{6,7},{7,6},{8,9},{9,8},{10,11... | collective-permute-start | bytes 3145736 | tf_op jit(solution)/shard_map/ppermute | solution.py:340
  31.5 14.1 %all-to-all-start = ((bf16[8,16,768]{2,1,0:T(8,128)(2,1)}), bf16[8,16,768]{2,1,0:T(8,128)(2,1)S(1)}, u32[]{:S(2)}, u32[]{:S(2)}) async-start(bf16[8,16,768]{2,1,0:T(8,128)(2,1)} %bitcast.3), calls=%async_computation | async-start | bytes 393216 | tf_op jit(solution)/shard_map/all_to_all | solution.py:400
